TPU v7x, 32 devices: a whole 2x2x4 slice. The times are simulated.
32 devices in a mesh: window: 2 (over x), tile: 8 (over z, y), member: 2 (over core).
Axes of the slice: x: 2, y: 2, z: 4, core: 2. Of those that a mesh axis runs over, the one named last changes fastest.
Arguments:
- control: float32 [40, 192, 2048], P(('window', 'member'), 'tile'), parts along dimension 0, may hold values from -6 to 6
- velocity: float32 [40, 192, 2048], P(('window', 'member'), 'tile'), parts along dimension 0, may hold values from -6 to 6
- perturb: bfloat16 [40, 3, 192, 2048], P(('window', 'member'), None, 'tile'), parts along dimension 0, as said below
- adjoint_forcing: float32 [4, 3, 192, 2048], P(('window', 'member'), None, 'tile'), parts along dimension 0, as said below
- slot_owner: int32 [6, 8], P('window', 'tile'), parts along dimension 0, may hold values from 0 to 1
- taps_x: float32 [7], replicated, may hold values from 0.3 to 1
- taps_y: float32 [7], replicated, may hold values from 0.3 to 1
- vertical_mix: float32 [64, 64], replicated, may hold values from -0.75 to 0.75
Outputs:
- new_control: float32 [40, 192, 2048], P(('window', 'member'), 'tile'), parts along dimension 0
- new_velocity: float32 [40, 192, 2048], P(('window', 'member'), 'tile'), parts along dimension 0
There are 2 independent parts, one for each index of `window`. A program takes and returns all parts, laid end to end along the dimension named above; an argument that names none is the same for every part. Nothing has to cross between parts.
Inputs may be any that keep to these rules, and one draw needn't show every extreme that they name: `adjoint_forcing`: gradient values of order one to some tens. `perturb`: perturbation values of order one.
All inputs are finite; a program needn't handle non-finite values.
Results may differ from a plain program's by a relative error of at most 0.0003.
Values sent between devices are 32-bit elements; how exact they have to be, the bound alone decides.
No kernel may reach another device: no remote copies, remote signals or barrier semaphores. Data moves between devices by JAX's collectives and lax.ppermute only.
A program may use at most 128 MiB of HBM per device.

v0:
```python
import jax
import jax.numpy as jnp
from jax import lax
from jax.sharding import PartitionSpec as P

NZ = 64
SLOTS = 3
NY = 32


def spread(value, axis, root):
    mine = lax.axis_index(axis) == root
    return lax.psum(jnp.where(mine, value, jnp.zeros_like(value)), axis)


def with_halo(cells, sides, width):
    for axis, dim in sides:
        count = lax.axis_size(axis)
        ends = count - 1
        head = lax.slice_in_dim(cells, 0, width, axis=dim)
        tail = lax.slice_in_dim(cells, cells.shape[dim] - width, cells.shape[dim], axis=dim)
        cells = jnp.concatenate(
            [
                lax.ppermute(tail, axis, [(i, (i + 1) % count) for i in range(ends)]),
                cells,
                lax.ppermute(head, axis, [((i + 1) % count, i) for i in range(ends)]),
            ],
            axis=dim,
        )
    return cells


def row_filter(padded, taps_x, rows_here):
    along_x = taps_x[0] * padded[:, 0:rows_here]
    for offset in range(1, 7):
        along_x = along_x + taps_x[offset] * padded[:, offset : offset + rows_here]
    return along_x


def column_level(field, taps_y, vertical_mix):
    members_here, rows_here, cells_here = field.shape
    shaped = field.reshape(members_here, rows_here, NY, NZ)
    padded_y = jnp.pad(shaped, ((0, 0), (0, 0), (3, 3), (0, 0)))
    along_y = jnp.zeros_like(shaped)
    for offset in range(7):
        along_y = along_y + taps_y[offset] * padded_y[:, :, offset : offset + NY]
    mixed = jnp.einsum("mxyw,wz->mxyz", along_y, vertical_mix, precision=lax.Precision.HIGHEST)
    return mixed.reshape(members_here, rows_here, cells_here)


def body(control, velocity, perturb, adjoint_forcing, slot_owner, taps_x, taps_y, vertical_mix):
    members_here = control.shape[0]
    rows_here = control.shape[1]
    cells_here = control.shape[2]
    slot_fields = []
    for slot in range(SLOTS):
        slot_fields.append(spread(adjoint_forcing[0, slot], "member", slot_owner[slot, 0]))
    forcing = jnp.stack(slot_fields)
    product = jnp.zeros((members_here, rows_here, cells_here), jnp.float32)
    for slot in range(SLOTS):
        product = product + perturb[:, slot].astype(jnp.float32) * forcing[slot][None]
    leveled = column_level(product, taps_y, vertical_mix)
    padded = with_halo(leveled, (("tile", 1),), 3)
    mixed = row_filter(padded, taps_x, rows_here)
    gradient = control + mixed
    total_square = lax.psum(jnp.sum(gradient * gradient), ("tile", "member"))
    entries = (
        members_here * lax.axis_size("member") * rows_here * lax.axis_size("tile") * cells_here
    )
    scale = lax.rsqrt(total_square / entries + 1e-06)
    new_velocity = 0.9 * velocity + scale * gradient
    new_control = control - 0.5 * new_velocity
    return (new_control, new_velocity)


def solution(mesh):
    placed = (
        P(("window", "member"), "tile", None),
        P(("window", "member"), "tile", None),
        P(("window", "member"), None, "tile", None),
        P(("window", "member"), None, "tile", None),
        P("window", "tile"),
        P(),
        P(),
        P(),
    )
    return jax.shard_map(
        body,
        mesh=mesh,
        in_specs=placed,
        out_specs=(P(("window", "member"), "tile", None), P(("window", "member"), "tile", None)),
        check_vma=False,
    )
```

profile of v0, /device:TPU:0, one launch (start us, length us, event | category | flops | bytes accessed | tf_op | source)
XLA Modules:
  0.0 131.6 jit_solution(5773188311054502174)
XLA Ops:
  7.2 0.0 copy-start
  7.2 0.0 all-reduce.4.cloned.1.call-start
  7.2 1.4 %fusion.45 = (s32[1,1]{0,1:T(1,128)}, s32[1,1]{0,1:T(1,128)}, s32[1,1]{0,1:T(1,128)}) fusion(s32[3,1]{0,1:T(1,128)} %param.12), kind=kLoop, calls=%fused_computation.64 | loop fusion | bytes 24 | tf_op jit(solution)/shard_map/slice | solution.py:57
  10.6 1.2 slice_select_fusion.2
  11.7 1.0 mul.148
  12.7 0.9 mul.145
  13.6 0.9 mul.142
  14.5 0.0 all-reduce.4.cloned.1.call-update
  14.5 4.5 %slice_convert_fusion.2 = (f32[10,1,24,2048]{3,2,1,0:T(8,128)S(1)}, f32[10,1,24,2048]{3,2,1,0:T(8,128)}, f32[10,1,24,2048]{3,2,1,0:T(8,128)}) fusion(bf16[10,3,24,2048]{3,2,1,0:T(8,128)(2,1)} %param.10), kind=kLoop, calls=%fused_computation.53 | loop fusion | flops 1474560 | bytes 8847360 | tf_op jit(solution)/shard_map/convert_element_type | solution.py:61
  19.1 4.5 %reshape.41 = f32[10,24,32,64]{3,2,1,0:T(8,128)} reshape(f32[10,1,24,2048]{3,2,1,0:T(8,128)} %get-tuple-element.10) | data formatting | bytes 3932160 | tf_op jit(solution)/shard_map/convert_element_type | solution.py:61
  23.6 4.5 %reshape.40 = f32[10,24,32,64]{3,2,1,0:T(8,128)} reshape(f32[10,1,24,2048]{3,2,1,0:T(8,128)} %get-tuple-element.11) | data formatting | bytes 3932160 | tf_op jit(solution)/shard_map/convert_element_type | solution.py:61
  28.1 0.0 copy-start.2
  28.1 0.0 copy-start.3
  28.1 2.9 %reshape.39 = f32[10,24,32,64]{3,2,1,0:T(8,128)} reshape(f32[10,1,24,2048]{3,2,1,0:T(8,128)S(1)} %get-tuple-element.9) | data formatting | bytes 3932160 | tf_op jit(solution)/shard_map/convert_element_type | solution.py:61
  31.0 0.0 copy-done.2
  31.0 0.7 fusion.44
  31.7 0.0 copy-done.3
  31.7 0.7 fusion.43
  32.3 5.0 %all-reduce.4.cloned.1.call-done = (f32[24,32,64]{2,1,0:T(8,128)}, f32[24,32,64]{2,1,0:T(8,128)}, f32[24,32,64]{2,1,0:T(8,128)}) async-done(((f32[24,32,64]{2,1,0:T(8,128)}, f32[24,32,64]{2,1,0:T(8,128)}, f32[24,32,64]{2,1,0:T(8,128)}), (f32[24,32,64]{2,1,0:T(8,128)}, f32[24,32,64]{2,1,0:T(8,128)}, f32[24,32,64]{2,1,0:T(8,128)})) %all-reduce.4.cloned.1.call-update) | async-done | bytes 589840 | tf_op jit(solution)/shard_map/psum | solution.py:13
  37.3 6.3 %multiply_add_fusion = f32[10,24,32,64]{3,2,1,0:T(8,128)S(1)} fusion(f32[10,24,32,64]{3,2,1,0:T(8,128)} %reshape.41, f32[10,24,32,64]{3,2,1,0:T(8,128)} %reshape.40, f32[10,24,32,64]{3,2,1,0:T(8,128)} %reshape.39, f32[24,32,64]{2,1,0:T(8,128)} %get-tuple-element.2, f32[24,32,64]{2,1,0:T(8,128)} %get-tuple-element.3, f32[24,32,64]{2,1,0:T(8,128)} %get-tuple-element.4), kind=kLoop, calls=%fused_computation.20 | loop fusion | flops 2457600 | bytes 8454144 | tf_op jit(solution)/shard_map/add | solution.py:61
  43.6 0.0 copy-done
  43.6 12.7 %fusion.7 = f32[10,24,32,64]{3,2,1,0:T(8,128)} fusion(f32[10,24,32,64]{3,2,1,0:T(8,128)S(1)} %multiply_add_fusion, f32[]{:T(128)} %bitcast.10, f32[]{:T(128)} %bitcast.9, f32[]{:T(128)} %bitcast.8, f32[]{:T(128)} %bitcast.7, f32[]{:T(128)} %bitcast.6, f32[]{:T(128)} %bitcast.5, f32[]{:T(128)} %bitcast.1, f32[64,64]{1,0:T(8,128)S(1)} %copy-done), kind=kOutput, calls=%fused_computation.13 | convolution fusion | flops 383877120 | bytes 3948572 | tf_op jit(solution)/shard_map/mxyw,wz->mxyz/dot_general | solution.py:47
  56.3 3.4 %reshape.35 = f32[10,24,2048]{2,1,0:T(8,128)S(1)} reshape(f32[10,24,32,64]{3,2,1,0:T(8,128)} %fusion.7) | data formatting | bytes 3932160 | tf_op jit(solution)/shard_map/reshape | solution.py:48
  59.7 0.1 fusion.42
  59.8 1.3 collective-permute-start.1
  61.1 0.0 copy-start.1
  61.2 4.7 %collective-permute-start = (f32[10,3,2048]{2,1,0:T(4,128)S(1)}, f32[10,3,2048]{2,1,0:T(4,128)S(1)}, u32[]{:S(2)}, u32[]{:S(2)}) collective-permute-start(f32[10,3,2048]{2,1,0:T(4,128)S(1)} %get-tuple-element.12), channel_id=1, source_target_pairs={{0,2},{2,4},{4,6},{6,8},{8,10},{10,12},{12,14},{1,3},{3,5},{5,7},{... | collective-permute-start | bytes 737288 | tf_op jit(solution)/shard_map/ppermute | solution.py:24
  65.9 0.1 constant_dynamic-update-slice_fusion.1
  66.0 5.7 %collective-permute-done.1 = f32[10,3,2048]{2,1,0:T(4,128)S(1)} collective-permute-done((f32[10,3,2048]{2,1,0:T(4,128)S(1)}, f32[10,3,2048]{2,1,0:T(4,128)S(1)}, u32[]{:S(2)}, u32[]{:S(2)}) %collective-permute-start.1) | collective-permute-done | bytes 245792 | tf_op jit(solution)/shard_map/ppermute | solution.py:26
  71.7 0.1 constant_dynamic-update-slice_fusion
  71.8 7.1 %collective-permute-done = f32[10,3,2048]{2,1,0:T(4,128)S(1)} collective-permute-done((f32[10,3,2048]{2,1,0:T(4,128)S(1)}, f32[10,3,2048]{2,1,0:T(4,128)S(1)}, u32[]{:S(2)}, u32[]{:S(2)}) %collective-permute-start) | collective-permute-done | bytes 245792 | tf_op jit(solution)/shard_map/ppermute | solution.py:24
  78.9 0.0 copy-done.1
  78.9 7.9 %multiply_reduce_fusion = (f32[]{:T(128)}, f32[10,24,2048]{2,1,0:T(8,128)}) fusion(f32[10,24,2048]{2,1,0:T(8,128)S(1)} %copy-done.1, f32[10,27,2048]{2,1,0:T(8,128)S(1)} %constant_dynamic-update-slice_fusion, f32[]{:T(128)} %bitcast.18, f32[]{:T(128)} %bitcast.17, f32[]{:T(128)} %bitcast.16, f32[10,24,2048]{2,1,0:T(8,128)S(1)} %reshape.35, f32[]{:T(128)} %bitcast.15, ...), kind=kLoop, calls=%fused_computation.43 | loop fusion | flops 9338879 | bytes 12042272 | tf_op jit(solution)/shard_map/reduce_sum | solution.py:66
  86.8 31.7 %psum.31 = f32[]{:T(128)} all-reduce(f32[]{:T(128)} %get-tuple-element.7), channel_id=1, replica_groups=mesh['window'=2,'tile'=8,'member'=2] {'tile','member'}, use_global_device_ids=true, to_apply=%region_4.5 | all-reduce | flops 1 | bytes 8 | tf_op jit(solution)/shard_map/psum | solution.py:66
  119.2 5.6 %multiply_subtract_fusion = (f32[10,24,2048]{2,1,0:T(8,128)}, f32[10,24,2048]{2,1,0:T(8,128)}) fusion(f32[10,24,2048]{2,1,0:T(8,128)} %param.8, f32[10,24,2048]{2,1,0:T(8,128)} %get-tuple-element.8, f32[]{:T(128)S(6)} %rsqrt.3, f32[10,24,2048]{2,1,0:T(8,128)} %param.9), kind=kLoop, calls=%fused_computation.41 | loop fusion | flops 2457600 | bytes 9830404 | tf_op jit(solution)/shard_map/sub | solution.py:72
Async XLA Ops:
  7.2 36.4 %copy-start = (f32[64,64]{1,0:T(8,128)S(1)}, f32[64,64]{1,0:T(8,128)}, u32[]{:S(2)}) copy-start(f32[64,64]{1,0:T(8,128)} %param.15) | copy-start | bytes 49156
  7.2 30.1 %all-reduce.4.cloned.1.call-start = ((), (), s32[]{:S(2)}) async-start(), calls=%async_computation | async-start | bytes 2359296 | tf_op jit(solution)/shard_map/psum | solution.py:13
  28.1 2.9 %copy-start.2 = (f32[7]{0:T(128)S(1)}, f32[7]{0:T(128)}, u32[]{:S(2)}) copy-start(f32[7]{0:T(128)} %param.14) | copy-start | bytes 88
  28.1 3.5 %copy-start.3 = (f32[7]{0:T(128)S(1)}, f32[7]{0:T(128)}, u32[]{:S(2)}) copy-start(f32[7]{0:T(128)} %param.13) | copy-start | bytes 88
  59.8 11.8 %collective-permute-start.1 = (f32[10,3,2048]{2,1,0:T(4,128)S(1)}, f32[10,3,2048]{2,1,0:T(4,128)S(1)}, u32[]{:S(2)}, u32[]{:S(2)}) collective-permute-start(f32[10,3,2048]{2,1,0:T(4,128)S(1)} %get-tuple-element.13), channel_id=1, source_target_pairs={{2,0},{4,2},{6,4},{8,6},{10,8},{12,10},{14,12},{3,1},{5,3},{7,5},{... | collective-permute-start | bytes 737288 | tf_op jit(solution)/shard_map/ppermute | solution.py:26
  61.1 17.7 %copy-start.1 = (f32[10,24,2048]{2,1,0:T(8,128)S(1)}, f32[10,24,2048]{2,1,0:T(8,128)}, u32[]{:S(2)}) copy-start(f32[10,24,2048]{2,1,0:T(8,128)} %param.8) | copy-start | bytes 5898244
  61.2 17.7 %collective-permute-start = (f32[10,3,2048]{2,1,0:T(4,128)S(1)}, f32[10,3,2048]{2,1,0:T(4,128)S(1)}, u32[]{:S(2)}, u32[]{:S(2)}) collective-permute-start(f32[10,3,2048]{2,1,0:T(4,128)S(1)} %get-tuple-element.12), channel_id=1, source_target_pairs={{0,2},{2,4},{4,6},{6,8},{8,10},{10,12},{12,14},{1,3},{3,5},{5,7},{... | collective-permute-start | bytes 737288 | tf_op jit(solution)/shard_map/ppermute | solution.py:24
Sparse Core Ops, SparseCore 0:
  14.7 22.6 all-reduce.3
where the time goes:
time: 132 us
  blocking collectives  31.7 us (24%)
  other arithmetic  25.4 us (19%)
  local copies, waits for them, and re-layouts  21.3 us (16%)
  waiting for transfers between devices  17.8 us (13%)
  between operations  16.7 us (13%)
  matrix products  12.7 us (10%)
  starting transfers between devices  6.03 us (5%)
    psum x1, blocking collectives, body(): total_square = lax.psum(jnp.sum(gradient * gradient), ('tile', 'member'))  31.7 us
    dot_general x1, matrix products, column_level(): jnp.einsum('mxyw,wz->mxyz', along_y, vertical_mix, precision=lax.Precisio...  12.7 us
    convert_element_type x3, local copies, waits for them, and re-layouts, body(): perturb[:, slot].astype(jnp.float32) * forcing[slot][None]  11.9 us
    reduce_sum x1, other arithmetic, body(): total_square = lax.psum(jnp.sum(gradient * gradient), ('tile', 'member'))  7.91 us
    ppermute x1, waiting for transfers between devices, with_halo(): lax.ppermute(tail, axis, [(i, (i + 1) % count) for i in range(ends)])  7.06 us
    add x1, other arithmetic, body(): product + perturb[:, slot].astype(jnp.float32) * forcing[slot][None]  6.28 us
    ppermute x1, waiting for transfers between devices, with_halo(): lax.ppermute(head, axis, [((i + 1) % count, i) for i in range(ends)])  5.69 us
    sub x1, other arithmetic, body(): new_control = control - 0.5 * new_velocity  5.59 us
  transfers between devices with their start and end apart: 3, of which 3 were waited for; matrix products, arithmetic and copies ran while one was open for 14% of the time, Pallas kernels for 0%

commit v1 on v0

v1 whole, which is shorter than its diff:
```python
import functools

import jax
import jax.numpy as jnp
from jax import lax
from jax.experimental import pallas as pl
from jax.experimental.pallas import tpu as pltpu
from jax.sharding import PartitionSpec as P

NZ = 64
SLOTS = 3
BLOCK = 256
BAND = 3 * BLOCK
F32 = jnp.float32
BF16 = jnp.bfloat16

VMEM = pl.BlockSpec(memory_space=pltpu.VMEM)
SMEM = pl.BlockSpec(memory_space=pltpu.SMEM)
ANY = pl.BlockSpec(memory_space=pl.ANY)


def params(mib):
    return pltpu.CompilerParams(vmem_limit_bytes=mib * 1024 * 1024)


def cost(flops, nbytes):
    return pl.CostEstimate(flops=flops, bytes_accessed=nbytes, transcendentals=0)


def pack(ref, member, rows):
    cells = rows.shape[1]
    if member < 8:
        ref[3 * member : 3 * member + 3, 0:cells] = rows
        return
    part = cells // 4
    for quarter in range(4):
        top = 6 * quarter + 3 * (member - 8)
        ref[top : top + 3, cells : cells + part] = rows[:, part * quarter : part * (quarter + 1)]


def unpack(ref, member, cells):
    if member < 8:
        return ref[3 * member : 3 * member + 3, 0:cells]
    part = cells // 4
    pieces = []
    for quarter in range(4):
        top = 6 * quarter + 3 * (member - 8)
        pieces.append(ref[top : top + 3, cells : cells + part])
    return jnp.concatenate(pieces, axis=1)


def split(value):
    high = value.astype(BF16)
    return high, (value - high.astype(F32)).astype(BF16)


def dot3(left, high, low):
    left_high, left_low = split(left)
    total = jnp.dot(left_high, low, preferred_element_type=F32)
    total += jnp.dot(left_low, high, preferred_element_type=F32)
    return total + jnp.dot(left_high, high, preferred_element_type=F32)


def build_band(mix, taps_ref, tap_of, high_ref, low_ref):
    wide = jnp.concatenate([mix] * (BLOCK // NZ), axis=1)
    group = lax.broadcasted_iota(jnp.int32, (1, BLOCK), 1) // NZ
    for a in range(BAND // NZ):
        factor = jnp.zeros((1, BLOCK), F32)
        for b in range(BLOCK // NZ):
            k = tap_of(a, b)
            if 0 <= k <= 6:
                factor = jnp.where(group == b, taps_ref[k], factor)
        high, low = split(wide * factor)
        high_ref[NZ * a : NZ * (a + 1), :] = high
        low_ref[NZ * a : NZ * (a + 1), :] = low


def border_kernel(owner_ref, perturb_ref, mine_ref, other_ref, up_ref, down_ref):
    members, _, rows, cells = perturb_ref.shape
    me = lax.axis_index("member")
    fields = []
    for slot in range(SLOTS):
        valid = owner_ref[slot, 0] == me
        pair = []
        for start in (0, rows - 8):
            here = mine_ref[0, slot, start : start + 8, :]
            there = other_ref[0, slot, start : start + 8, :]
            pair.append(jnp.where(valid, here, there))
        fields.append(pair)
    for member in range(members):
        for side, start in enumerate((0, rows - 8)):
            total = jnp.zeros((8, cells), F32)
            for slot in range(SLOTS):
                total += perturb_ref[member, slot, start : start + 8, :].astype(F32) * fields[slot][side]
            if side == 0:
                pack(down_ref, member, total[0:3])
            else:
                pack(up_ref, member, total[5:8])


def bulk_kernel(
    owner_ref, taps_x_ref, taps_y_ref, mix_ref, perturb_ref, mine_ref, other_ref, control_ref,
    local_ref, cross_up_ref, cross_down_ref, square_ref,
    field, filtered, turned, high, low, high_t, low_t,
):
    members, _, rows, cells = perturb_ref.shape
    tall = rows + 16
    me = lax.axis_index("member")
    tile = lax.axis_index("tile")
    tiles = lax.axis_size("tile")
    mix = mix_ref[...]
    build_band(mix, taps_y_ref, lambda a, b: a - b - 1, high, low)
    build_band(mix.T, taps_y_ref, lambda a, b: b - a + 7, high_t, low_t)
    for slot in range(SLOTS):
        field[slot] = jnp.where(owner_ref[slot, 0] == me, mine_ref[0, slot], other_ref[0, slot])
    filtered[:, :, 0:BLOCK] = jnp.zeros((members, tall, BLOCK), F32)
    filtered[:, :, BLOCK + cells :] = jnp.zeros((members, tall, BLOCK), F32)
    turned[:, 0:BLOCK] = jnp.zeros((members * 16, BLOCK), F32)
    turned[:, BLOCK + cells :] = jnp.zeros((members * 16, BLOCK), F32)
    part = 512

    def rows_step(member, carry):
        for start in range(0, cells, part):
            lanes = slice(start, start + part)
            product = jnp.zeros((rows, part), F32)
            for slot in range(SLOTS):
                product += perturb_ref[member, slot, :, lanes].astype(F32) * field[slot, :, lanes]
            edge = jnp.zeros((16, part), F32)
            padded = jnp.concatenate([edge, product, edge], axis=0)
            total = taps_x_ref[0] * padded[5 : 5 + tall]
            for k in range(1, 7):
                total += taps_x_ref[k] * padded[5 + k : 5 + k + tall]
            filtered[member, :, BLOCK + start : BLOCK + start + part] = total
        return carry

    lax.fori_loop(0, members, rows_step, 0)
    weight_top = jnp.where(tile > 0, 1.0, 0.0).astype(F32)
    weight_bottom = jnp.where(tile < tiles - 1, 1.0, 0.0).astype(F32)

    def block_step(j, carry):
        lanes = pl.ds(pl.multiple_of(j * BLOCK, BLOCK), BAND)
        out = pl.ds(pl.multiple_of(j * BLOCK, BLOCK), BLOCK)
        left = filtered[:, :, lanes].reshape(members * tall, BAND)
        result = dot3(left, high[...], low[...]).reshape(members, tall, BLOCK)
        local = control_ref[:, :, out] + result[:, 8 : 8 + rows]
        local_ref[:, :, out] = local
        total = jnp.sum((local * local).reshape(members * rows // 8, 8, BLOCK), axis=0)
        above, below = result[:, 0:8], result[:, 8 + rows :]
        total += weight_top * jnp.sum(above * above, axis=0)
        total += weight_bottom * jnp.sum(below * below, axis=0)
        return carry + total[:, 0:128] + total[:, 128:256]

    square_ref[...] = lax.fori_loop(0, cells // BLOCK, block_step, jnp.zeros((8, 128), F32))

    def turn_step(member, carry):
        for start in range(0, cells, part):
            lanes = slice(start, start + part)
            zero = jnp.zeros((8, part), F32)
            top = jnp.concatenate([zero, local_ref[member, 0:8, lanes]], axis=0)
            bottom = jnp.concatenate([local_ref[member, rows - 8 : rows, lanes], zero], axis=0)
            first = taps_x_ref[0] * top[8:16] + taps_x_ref[1] * top[7:15] + taps_x_ref[2] * top[6:14]
            last = taps_x_ref[6] * bottom[0:8] + taps_x_ref[5] * bottom[1:9] + taps_x_ref[4] * bottom[2:10]
            both = jnp.concatenate([first, last], axis=0)
            turned[pl.ds(pl.multiple_of(member * 16, 16), 16), BLOCK + start : BLOCK + start + part] = both
        return carry

    lax.fori_loop(0, members, turn_step, 0)
    adjoint = filtered

    def turn_block(j, carry):
        lanes = pl.ds(pl.multiple_of(j * BLOCK, BLOCK), BAND)
        out = pl.ds(pl.multiple_of(j * BLOCK, BLOCK), BLOCK)
        result = dot3(turned[:, lanes], high_t[...], low_t[...])
        adjoint[:, 0:16, out] = result.reshape(members, 16, BLOCK)
        return carry

    lax.fori_loop(0, cells // BLOCK, turn_block, 0)
    for member in range(members):
        pack(cross_up_ref, member, adjoint[member, 0:3, 0:cells])
        pack(cross_down_ref, member, adjoint[member, 13:16, 0:cells])


def cross_kernel(square_ref, cross_up_ref, cross_down_ref, from_left_ref, from_right_ref, total_ref):
    rows, width = cross_up_ref.shape
    total = jnp.zeros((8, 128), F32)
    part = 512
    for row in range(0, rows, 8):
        for start in range(0, width, part):
            lanes = slice(start, start + part)
            value = cross_up_ref[row : row + 8, lanes] * from_left_ref[row : row + 8, lanes]
            value += cross_down_ref[row : row + 8, lanes] * from_right_ref[row : row + 8, lanes]
            for lane in range(0, part, 128):
                total += value[:, lane : lane + 128]
    total_ref[...] = square_ref[...] + 2.0 * total


def correct_kernel(
    taps_x_ref, taps_y_ref, mix_ref, from_left_ref, from_right_ref, correction_ref, filtered, high, low
):
    members, _, cells = correction_ref.shape
    build_band(mix_ref[...], taps_y_ref, lambda a, b: a - b - 1, high, low)
    filtered[:, :, 0:BLOCK] = jnp.zeros((members, 16, BLOCK), F32)
    filtered[:, :, BLOCK + cells :] = jnp.zeros((members, 16, BLOCK), F32)
    for member in range(members):
        left = unpack(from_left_ref, member, cells)
        right = unpack(from_right_ref, member, cells)
        first = jnp.concatenate([left, jnp.zeros((13, cells), F32)], axis=0)
        last = jnp.concatenate([jnp.zeros((13, cells), F32), right], axis=0)
        top = taps_x_ref[0] * first[0:8] + taps_x_ref[1] * first[1:9] + taps_x_ref[2] * first[2:10]
        bottom = taps_x_ref[6] * last[8:16] + taps_x_ref[5] * last[7:15] + taps_x_ref[4] * last[6:14]
        filtered[member, 0:8, BLOCK : BLOCK + cells] = top
        filtered[member, 8:16, BLOCK : BLOCK + cells] = bottom

    def block_step(j, carry):
        lanes = pl.ds(pl.multiple_of(j * BLOCK, BLOCK), BAND)
        out = pl.ds(pl.multiple_of(j * BLOCK, BLOCK), BLOCK)
        left = filtered[:, :, lanes].reshape(members * 16, BAND)
        correction_ref[:, :, out] = dot3(left, high[...], low[...]).reshape(members, 16, BLOCK)
        return carry

    lax.fori_loop(0, cells // BLOCK, block_step, 0)


def update_kernel(
    entries, near_ref, far_ref, control_ref, velocity_ref, local_ref, correction_ref,
    new_control_hbm, new_velocity_hbm, new_control, new_velocity, sems,
):
    members, rows, cells = control_ref.shape
    mean = jnp.sum(near_ref[...] + far_ref[...], keepdims=True) / entries
    scale = lax.rsqrt(mean + 1e-06)
    copies = []
    for member in range(members):
        for start in range(0, rows, 8):
            tile = slice(start, start + 8)
            gradient = local_ref[member, tile]
            if start == 0:
                gradient += correction_ref[member, 0:8]
            if start == rows - 8:
                gradient += correction_ref[member, 8:16]
            moved = 0.9 * velocity_ref[member, tile] + scale * gradient
            new_velocity[member, tile] = moved
            new_control[member, tile] = control_ref[member, tile] - 0.5 * moved
        for which, (src, dst) in enumerate(((new_control, new_control_hbm), (new_velocity, new_velocity_hbm))):
            copy = pltpu.make_async_copy(src.at[member], dst.at[member], sems.at[which, member])
            copy.start()
            copies.append(copy)
    for copy in copies:
        copy.wait()


def body(control, velocity, perturb, adjoint_forcing, slot_owner, taps_x, taps_y, vertical_mix):
    members, rows, cells = control.shape
    tiles = lax.axis_size("tile")
    groups = lax.axis_size("member")
    swap = [(0, 1), (1, 0)]
    other = lax.ppermute(adjoint_forcing, "member", swap)
    packed = jax.ShapeDtypeStruct((24, cells + cells // 4), F32)
    up, down = pl.pallas_call(
        border_kernel,
        name="border_product",
        out_shape=(packed, packed),
        in_specs=[SMEM, VMEM, VMEM, VMEM],
        out_specs=(VMEM, VMEM),
        compiler_params=params(16),
        cost_estimate=cost(4_000_000, 4_000_000),
    )(slot_owner, perturb, adjoint_forcing, other)
    from_left = lax.ppermute(up, "tile", [(i, i + 1) for i in range(tiles - 1)])
    from_right = lax.ppermute(down, "tile", [(i + 1, i) for i in range(tiles - 1)])
    wide = cells + 2 * BLOCK
    band = pltpu.VMEM((BAND, BLOCK), BF16)
    local, cross_up, cross_down, square = pl.pallas_call(
        bulk_kernel,
        name="bulk",
        out_shape=(
            jax.ShapeDtypeStruct(control.shape, F32), packed, packed, jax.ShapeDtypeStruct((8, 128), F32),
        ),
        in_specs=[SMEM, SMEM, SMEM, VMEM, VMEM, VMEM, VMEM, VMEM],
        out_specs=(VMEM, VMEM, VMEM, VMEM),
        scratch_shapes=[
            pltpu.VMEM((SLOTS, rows, cells), F32),
            pltpu.VMEM((members, rows + 16, wide), F32),
            pltpu.VMEM((members * 16, wide), F32),
            band, band, band, band,
        ],
        compiler_params=params(32),
        cost_estimate=cost(9_000_000_000, 12_000_000),
    )(slot_owner, taps_x, taps_y, vertical_mix, perturb, adjoint_forcing, other, control)
    near = pl.pallas_call(
        cross_kernel,
        name="cross_term",
        out_shape=jax.ShapeDtypeStruct((8, 128), F32),
        in_specs=[VMEM] * 5,
        out_specs=VMEM,
        compiler_params=params(8),
        cost_estimate=cost(200_000, 1_000_000),
    )(square, cross_up, cross_down, from_left, from_right)
    correction = pl.pallas_call(
        correct_kernel,
        name="border_correction",
        out_shape=jax.ShapeDtypeStruct((members, 16, cells), F32),
        in_specs=[SMEM, SMEM, VMEM, VMEM, VMEM],
        out_specs=VMEM,
        scratch_shapes=[pltpu.VMEM((members, 16, wide), F32), band, band],
        compiler_params=params(16),
        cost_estimate=cost(2_000_000_000, 2_000_000),
    )(taps_x, taps_y, vertical_mix, from_left, from_right)
    steps = [("member", swap)]
    width = 1
    while width < tiles:
        steps.append(("tile", [(i, i ^ width) for i in range(tiles)]))
        width *= 2
    for axis, pairs in steps[:-1]:
        near = near + lax.ppermute(near, axis, pairs)
    far = lax.ppermute(near, *steps[-1])
    entries = members * groups * rows * tiles * cells
    whole = jax.ShapeDtypeStruct(control.shape, F32)
    return tuple(
        pl.pallas_call(
            functools.partial(update_kernel, float(entries)),
            name="update",
            out_shape=(whole, whole),
            in_specs=[VMEM] * 6,
            out_specs=(ANY, ANY),
            scratch_shapes=[
                pltpu.VMEM(control.shape, F32),
                pltpu.VMEM(control.shape, F32),
                pltpu.SemaphoreType.DMA((2, members)),
            ],
            compiler_params=params(16),
            cost_estimate=cost(3_000_000, 12_000_000),
        )(near, far, control, velocity, local, correction)
    )


def solution(mesh):
    placed = (
        P(("window", "member"), "tile", None),
        P(("window", "member"), "tile", None),
        P(("window", "member"), None, "tile", None),
        P(("window", "member"), None, "tile", None),
        P("window", "tile"),
        P(),
        P(),
        P(),
    )
    return jax.shard_map(
        body,
        mesh=mesh,
        in_specs=placed,
        out_specs=(P(("window", "member"), "tile", None), P(("window", "member"), "tile", None)),
        check_vma=False,
    )
```

time: 132 us -> 48 us (0.36)
  blocking collectives: 31.7 us -> 0 us
  other arithmetic: 25.4 us -> 0.01 us
  Pallas kernels: 0 us -> 20.9 us
  local copies, waits for them, and re-layouts: 21.3 us -> 5.2 us
  between operations: 16.7 us -> 0.77 us
  matrix products: 12.7 us -> 0 us
  waiting for transfers between devices: 17.8 us -> 5.43 us
  starting transfers between devices: 6.03 us -> 15.5 us
    psum x1 -> x0, blocking collectives: 31.7 us -> none  [body(): total_square = lax.psum(jnp.sum(gradient * gradient), ('tile', 'member'))]
    pallas_call x0 -> x5, Pallas kernels: none -> 20.9 us  [the longest x1 13.3 us: body(): pl.pallas_call(bulk_kernel, name='bulk', out_shape=(jax.ShapeDtypeStruct(...]
    dot_general x1 -> x0, matrix products: 12.7 us -> none  [column_level(): jnp.einsum('mxyw,wz->mxyz', along_y, vertical_mix, precision=lax.Precisio...]
    convert_element_type x3 -> x0, local copies, waits for them, and re-layouts: 11.9 us -> none  [body(): perturb[:, slot].astype(jnp.float32) * forcing[slot][None]]
    ppermute x2 -> x7, starting transfers between devices: 5.99 us -> 15.5 us  [the longest x3 5.67 us: body(): near = near + lax.ppermute(near, axis, pairs)]
    reduce_sum x1 -> x0, other arithmetic: 7.91 us -> none  [body(): total_square = lax.psum(jnp.sum(gradient * gradient), ('tile', 'member'))]
    ppermute x2 -> x7, waiting for transfers between devices: 12.7 us -> 5.43 us  [the longest x3 4.32 us: body(): near = near + lax.ppermute(near, axis, pairs)]
    add x1 -> x3, other arithmetic: 6.28 us -> 0.01 us  [body(): near = near + lax.ppermute(near, axis, pairs)]
  transfers between devices with their start and end apart: 3 -> 7, of which waited for: 3 -> 4; matrix products, arithmetic and copies ran while one was open for 14% -> 2% of each run, Pallas kernels for 0% -> 37%
where the time goes in v1:
time: 48 us; the launch traced here: 47.8 us
  Pallas kernels  20.9 us (44%)
  starting transfers between devices  15.5 us (32%)
  waiting for transfers between devices  5.43 us (11%)
  local copies, waits for them, and re-layouts  5.2 us (11%)
  between operations  0.77 us (2%)
    pallas_call x1, Pallas kernels, body(): pl.pallas_call(bulk_kernel, name='bulk', out_shape=(jax.ShapeDtypeStruct(...  13.3 us
    ppermute x3, starting transfers between devices, body(): near = near + lax.ppermute(near, axis, pairs)  5.67 us
    unnamed x19, local copies, waits for them, and re-layouts  5.2 us
    ppermute x1, starting transfers between devices, body(): from_left = lax.ppermute(up, 'tile', [(i, i + 1) for i in range(tiles - 1)])  4.94 us
    ppermute x3, waiting for transfers between devices, body(): near = near + lax.ppermute(near, axis, pairs)  4.32 us
    pallas_call x1, Pallas kernels, body(): pl.pallas_call(correct_kernel, name='border_correction', out_shape=jax.Sh...  4.29 us
    ppermute x1, starting transfers between devices, body(): far = lax.ppermute(near, *steps[-1])  3.04 us
    pallas_call x1, Pallas kernels, body(): pl.pallas_call(functools.partial(update_kernel, float(entries)), name='up...  2.24 us
  transfers between devices with their start and end apart: 7, of which 4 were waited for; matrix products, arithmetic and copies ran while one was open for 2% of the time, Pallas kernels for 37%

profile of v1, /device:TPU:0, one launch (start us, length us, event | category | flops | bytes accessed | tf_op | source)
XLA Modules:
  0.0 47.8 jit_solution(8260913030596731802)
XLA Ops:
  0.6 0.5 %collective-permute-start = (f32[1,3,24,2048]{3,2,1,0:T(8,128)}, f32[1,3,24,2048]{3,2,1,0:T(8,128)S(1)}, u32[]{:S(2)}, u32[]{:S(2)}) collective-permute-start(f32[1,3,24,2048]{3,2,1,0:T(8,128)} %mine_ref.3), channel_id=1, source_target_pairs={{0,1},{1,0},{2,3},{3,2},{4,5},{5,4},{6,7},{7,6},{8,9},{9,8},{10,11... | collective-permute-start | bytes 1769480 | tf_op jit(solution)/shard_map/ppermute | solution.py:256
  1.1 0.7 %copy.10.owner_ref = s32[3,1]{1,0:T(4,128)S(1)} copy(s32[3,1]{0,1:T(1,128)} %param.12) | data formatting | bytes 24 | tf_op args[4]
  1.9 1.1 %collective-permute-done.other_ref = f32[1,3,24,2048]{3,2,1,0:T(8,128)S(1)} collective-permute-done((f32[1,3,24,2048]{3,2,1,0:T(8,128)}, f32[1,3,24,2048]{3,2,1,0:T(8,128)S(1)}, u32[]{:S(2)}, u32[]{:S(2)}) %collective-permute-start) | collective-permute-done | bytes 589856 | tf_op jit(solution)/shard_map/ppermute | solution.py:256
  3.0 0.0 copy-start
  3.0 1.8 %copy-done = bf16[10,3,24,2048]{3,2,1,0:T(8,128)(2,1)S(1)} copy-done((bf16[10,3,24,2048]{3,2,1,0:T(8,128)(2,1)S(1)}, bf16[10,3,24,2048]{3,2,1,0:T(8,128)(2,1)}, u32[]{:S(2)}) %copy-start) | copy-done | bytes 2949144
  4.8 0.0 copy-start.4
  4.8 1.1 %copy-done.4 = f32[1,3,24,2048]{3,2,1,0:T(8,128)S(1)} copy-done((f32[1,3,24,2048]{3,2,1,0:T(8,128)S(1)}, f32[1,3,24,2048]{3,2,1,0:T(8,128)}, u32[]{:S(2)}) %copy-start.4) | copy-done | bytes 589848
  5.9 0.0 copy-start.1
  5.9 0.0 copy-start.5
  5.9 0.0 copy-start.6
  5.9 0.0 copy-start.7
  5.9 0.0 copy-start.8
  5.9 1.0 %border_product.1 = (f32[24,2560]{1,0:T(8,128)S(1)}, f32[24,2560]{1,0:T(8,128)S(1)}) custom-call(s32[3,1]{1,0:T(4,128)S(1)} %copy.10.owner_ref, bf16[10,3,24,2048]{3,2,1,0:T(8,128)(2,1)S(1)} %copy-done, f32[1,3,24,2048]{3,2,1,0:T(8,128)S(1)} %copy-done.4, f32[1,3,24,2048]{3,2,1,0:T(8,128)S(1)} %collective-permute-done.other_ref), custom_call_target="tpu_custom_call" | custom-call | flops 4000000 | bytes 4000000 | tf_op jit(solution)/shard_map/border_product/pallas_call | solution.py:258
  6.9 4.9 %collective-permute-start.1 = (f32[24,2560]{1,0:T(8,128)S(1)}, f32[24,2560]{1,0:T(8,128)S(1)}, u32[]{:S(2)}, u32[]{:S(2)}) collective-permute-start(f32[24,2560]{1,0:T(8,128)S(1)} %get-tuple-element.11), channel_id=1, source_target_pairs={{0,2},{2,4},{4,6},{6,8},{8,10},{10,12},{12,14},{1,3},{3,5},{5,7},{... | collective-permute-start | bytes 737288 | tf_op jit(solution)/shard_map/ppermute | solution.py:267
  11.9 1.3 %collective-permute-start.2 = (f32[24,2560]{1,0:T(8,128)S(1)}, f32[24,2560]{1,0:T(8,128)S(1)}, u32[]{:S(2)}, u32[]{:S(2)}) collective-permute-start(f32[24,2560]{1,0:T(8,128)S(1)} %get-tuple-element.12), channel_id=1, source_target_pairs={{2,0},{4,2},{6,4},{8,6},{10,8},{12,10},{14,12},{3,1},{5,3},{7,5},{... | collective-permute-start | bytes 737288 | tf_op jit(solution)/shard_map/ppermute | solution.py:268
  13.2 0.0 copy-done.1
  13.2 0.0 copy-done.5
  13.2 0.0 copy-done.6
  13.2 0.0 copy-done.7
  13.2 0.0 copy-done.8
  13.2 0.0 copy-start.2
  13.2 1.5 %copy-done.2 = f32[10,24,2048]{2,1,0:T(8,128)S(1)} copy-done((f32[10,24,2048]{2,1,0:T(8,128)S(1)}, f32[10,24,2048]{2,1,0:T(8,128)}, u32[]{:S(2)}) %copy-start.2) | copy-done | bytes 1966104
  14.8 13.3 %bulk.1 = (f32[10,24,2048]{2,1,0:T(8,128)S(1)}, f32[24,2560]{1,0:T(8,128)S(1)}, f32[24,2560]{1,0:T(8,128)S(1)}, f32[8,128]{1,0:T(8,128)S(1)}) custom-call(s32[3,1]{1,0:T(4,128)S(1)} %copy.10.owner_ref, f32[7]{0:T(128)S(1)} %copy-done.7, f32[7]{0:T(128)S(1)} %copy-done.8, f32[64,64]{1,0:T(8,128)S(1)} %copy-done.6, bf16[10,3,24,2048]{3,2,1,0:T(8,128)(2,1)S(1)} %copy-done.1, ...), custom_call_target="tpu_custom_call" | custom-call | flops 8999999488 | bytes 12000000 | tf_op jit(solution)/shard_map/bulk/pallas_call | solution.py:271
  28.0 0.0 collective-permute-done.1.from_left_ref
  28.1 0.0 collective-permute-done.2.from_right_ref
  28.1 0.1 cross_term.1
  28.1 0.1 collective-permute-start.3
  28.2 1.2 %collective-permute-done.3 = f32[8,128]{1,0:T(8,128)S(1)} collective-permute-done((f32[8,128]{1,0:T(8,128)S(1)}, f32[8,128]{1,0:T(8,128)S(1)}, u32[]{:S(2)}, u32[]{:S(2)}) %collective-permute-start.3) | collective-permute-done | bytes 4128 | tf_op jit(solution)/shard_map/ppermute | solution.py:313
  29.4 2.6 %collective-permute-start.4 = (f32[8,128]{1,0:T(8,128)S(1)}, f32[8,128]{1,0:T(8,128)S(1)}, u32[]{:S(2)}, u32[]{:S(2)}) collective-permute-start(f32[8,128]{1,0:T(8,128)S(1)} %add.9), channel_id=1, source_target_pairs={{0,2},{2,0},{4,6},{6,4},{8,10},{10,8},{12,14},{14,12},{1,3},{3,1},... | collective-permute-start | bytes 12296 | tf_op jit(solution)/shard_map/ppermute | solution.py:313
  32.0 1.6 %collective-permute-done.4 = f32[8,128]{1,0:T(8,128)S(1)} collective-permute-done((f32[8,128]{1,0:T(8,128)S(1)}, f32[8,128]{1,0:T(8,128)S(1)}, u32[]{:S(2)}, u32[]{:S(2)}) %collective-permute-start.4) | collective-permute-done | bytes 4128 | tf_op jit(solution)/shard_map/ppermute | solution.py:313
  33.6 3.0 %collective-permute-start.5 = (f32[8,128]{1,0:T(8,128)S(1)}, f32[8,128]{1,0:T(8,128)S(1)}, u32[]{:S(2)}, u32[]{:S(2)}) collective-permute-start(f32[8,128]{1,0:T(8,128)S(1)} %add.10), channel_id=1, source_target_pairs={{0,4},{2,6},{4,0},{6,2},{8,12},{10,14},{12,8},{14,10},{1,5},{3,7},... | collective-permute-start | bytes 12296 | tf_op jit(solution)/shard_map/ppermute | solution.py:313
  36.6 1.6 %collective-permute-done.5 = f32[8,128]{1,0:T(8,128)S(1)} collective-permute-done((f32[8,128]{1,0:T(8,128)S(1)}, f32[8,128]{1,0:T(8,128)S(1)}, u32[]{:S(2)}, u32[]{:S(2)}) %collective-permute-start.5) | collective-permute-done | bytes 4128 | tf_op jit(solution)/shard_map/ppermute | solution.py:313
  38.2 0.0 copy-start.3
  38.2 3.0 %collective-permute-start.6 = (f32[8,128]{1,0:T(8,128)S(1)}, f32[8,128]{1,0:T(8,128)S(1)}, u32[]{:S(2)}, u32[]{:S(2)}) collective-permute-start(f32[8,128]{1,0:T(8,128)S(1)} %add.11.near_ref), channel_id=1, source_target_pairs={{0,8},{2,10},{4,12},{6,14},{8,0},{10,2},{12,4},{14,6},{1,9},{3,11}... | collective-permute-start | bytes 12296 | tf_op jit(solution)/shard_map/ppermute | solution.py:314
  41.2 4.3 %border_correction.1.correction_ref = f32[10,16,2048]{2,1,0:T(8,128)S(1)} custom-call(f32[7]{0:T(128)S(1)} %copy-done.7, f32[7]{0:T(128)S(1)} %copy-done.8, f32[64,64]{1,0:T(8,128)S(1)} %copy-done.6, f32[24,2560]{1,0:T(8,128)S(1)} %collective-permute-done.1.from_left_ref, f32[24,2560]{1,0:T(8,128)S(1)} %collective-permute-done.2.from_right_ref), custom_call_target="tpu_custom_call" | custom-call | flops 2000000000 | bytes 2000000 | tf_op jit(solution)/shard_map/border_correction/pallas_call | solution.py:297
  45.5 0.0 collective-permute-done.6.far_ref
  45.5 0.0 copy-done.3
  45.5 2.2 %update.1 = (f32[10,24,2048]{2,1,0:T(8,128)}, f32[10,24,2048]{2,1,0:T(8,128)}) custom-call(f32[8,128]{1,0:T(8,128)S(1)} %add.11.near_ref, f32[8,128]{1,0:T(8,128)S(1)} %collective-permute-done.6.far_ref, f32[10,24,2048]{2,1,0:T(8,128)S(1)} %copy-done.2, f32[10,24,2048]{2,1,0:T(8,128)S(1)} %copy-done.3, f32[10,24,2048]{2,1,0:T(8,128)S(1)} %get-tuple-element.13.local_ref, ...), custom_call_target="tpu_custom_call" | custom-call | flops 3000000 | bytes 12000000 | tf_op jit(solution)/shard_map/update/pallas_call | solution.py:318
  (3 shorter events, 0.0 us)
Async XLA Ops:
  0.6 2.4 %collective-permute-start = (f32[1,3,24,2048]{3,2,1,0:T(8,128)}, f32[1,3,24,2048]{3,2,1,0:T(8,128)S(1)}, u32[]{:S(2)}, u32[]{:S(2)}) collective-permute-start(f32[1,3,24,2048]{3,2,1,0:T(8,128)} %mine_ref.3), channel_id=1, source_target_pairs={{0,1},{1,0},{2,3},{3,2},{4,5},{5,4},{6,7},{7,6},{8,9},{9,8},{10,11... | collective-permute-start | bytes 1769480 | tf_op jit(solution)/shard_map/ppermute | solution.py:256
  3.0 1.8 %copy-start = (bf16[10,3,24,2048]{3,2,1,0:T(8,128)(2,1)S(1)}, bf16[10,3,24,2048]{3,2,1,0:T(8,128)(2,1)}, u32[]{:S(2)}) copy-start(bf16[10,3,24,2048]{3,2,1,0:T(8,128)(2,1)} %perturb_ref.3) | copy-start | bytes 8847364
  4.8 1.1 %copy-start.4 = (f32[1,3,24,2048]{3,2,1,0:T(8,128)S(1)}, f32[1,3,24,2048]{3,2,1,0:T(8,128)}, u32[]{:S(2)}) copy-start(f32[1,3,24,2048]{3,2,1,0:T(8,128)} %mine_ref.3) | copy-start | bytes 1769476
  5.9 7.3 %copy-start.1 = (bf16[10,3,24,2048]{3,2,1,0:T(8,128)(2,1)S(1)}, bf16[10,3,24,2048]{3,2,1,0:T(8,128)(2,1)}, u32[]{:S(2)}) copy-start(bf16[10,3,24,2048]{3,2,1,0:T(8,128)(2,1)} %perturb_ref.3) | copy-start | bytes 8847364
  5.9 7.3 %copy-start.5 = (f32[1,3,24,2048]{3,2,1,0:T(8,128)S(1)}, f32[1,3,24,2048]{3,2,1,0:T(8,128)}, u32[]{:S(2)}) copy-start(f32[1,3,24,2048]{3,2,1,0:T(8,128)} %mine_ref.3) | copy-start | bytes 1769476
  5.9 7.3 %copy-start.6 = (f32[64,64]{1,0:T(8,128)S(1)}, f32[64,64]{1,0:T(8,128)}, u32[]{:S(2)}) copy-start(f32[64,64]{1,0:T(8,128)} %mix_ref.3) | copy-start | bytes 49156
  5.9 7.3 %copy-start.7 = (f32[7]{0:T(128)S(1)}, f32[7]{0:T(128)}, u32[]{:S(2)}) copy-start(f32[7]{0:T(128)} %taps_x_ref.3) | copy-start | bytes 88
  5.9 7.3 %copy-start.8 = (f32[7]{0:T(128)S(1)}, f32[7]{0:T(128)}, u32[]{:S(2)}) copy-start(f32[7]{0:T(128)} %taps_y_ref.3) | copy-start | bytes 88
  6.9 21.1 %collective-permute-start.1 = (f32[24,2560]{1,0:T(8,128)S(1)}, f32[24,2560]{1,0:T(8,128)S(1)}, u32[]{:S(2)}, u32[]{:S(2)}) collective-permute-start(f32[24,2560]{1,0:T(8,128)S(1)} %get-tuple-element.11), channel_id=1, source_target_pairs={{0,2},{2,4},{4,6},{6,8},{8,10},{10,12},{12,14},{1,3},{3,5},{5,7},{... | collective-permute-start | bytes 737288 | tf_op jit(solution)/shard_map/ppermute | solution.py:267
  11.9 16.2 %collective-permute-start.2 = (f32[24,2560]{1,0:T(8,128)S(1)}, f32[24,2560]{1,0:T(8,128)S(1)}, u32[]{:S(2)}, u32[]{:S(2)}) collective-permute-start(f32[24,2560]{1,0:T(8,128)S(1)} %get-tuple-element.12), channel_id=1, source_target_pairs={{2,0},{4,2},{6,4},{8,6},{10,8},{12,10},{14,12},{3,1},{5,3},{7,5},{... | collective-permute-start | bytes 737288 | tf_op jit(solution)/shard_map/ppermute | solution.py:268
  13.2 1.5 %copy-start.2 = (f32[10,24,2048]{2,1,0:T(8,128)S(1)}, f32[10,24,2048]{2,1,0:T(8,128)}, u32[]{:S(2)}) copy-start(f32[10,24,2048]{2,1,0:T(8,128)} %control_ref.3) | copy-start | bytes 5898244
  28.1 1.2 %collective-permute-start.3 = (f32[8,128]{1,0:T(8,128)S(1)}, f32[8,128]{1,0:T(8,128)S(1)}, u32[]{:S(2)}, u32[]{:S(2)}) collective-permute-start(f32[8,128]{1,0:T(8,128)S(1)} %cross_term.1), channel_id=1, source_target_pairs={{0,1},{1,0},{2,3},{3,2},{4,5},{5,4},{6,7},{7,6},{8,9},{9,8},{10,11... | collective-permute-start | bytes 12296 | tf_op jit(solution)/shard_map/ppermute | solution.py:313
  29.4 4.2 %collective-permute-start.4 = (f32[8,128]{1,0:T(8,128)S(1)}, f32[8,128]{1,0:T(8,128)S(1)}, u32[]{:S(2)}, u32[]{:S(2)}) collective-permute-start(f32[8,128]{1,0:T(8,128)S(1)} %add.9), channel_id=1, source_target_pairs={{0,2},{2,0},{4,6},{6,4},{8,10},{10,8},{12,14},{14,12},{1,3},{3,1},... | collective-permute-start | bytes 12296 | tf_op jit(solution)/shard_map/ppermute | solution.py:313
  33.6 4.6 %collective-permute-start.5 = (f32[8,128]{1,0:T(8,128)S(1)}, f32[8,128]{1,0:T(8,128)S(1)}, u32[]{:S(2)}, u32[]{:S(2)}) collective-permute-start(f32[8,128]{1,0:T(8,128)S(1)} %add.10), channel_id=1, source_target_pairs={{0,4},{2,6},{4,0},{6,2},{8,12},{10,14},{12,8},{14,10},{1,5},{3,7},... | collective-permute-start | bytes 12296 | tf_op jit(solution)/shard_map/ppermute | solution.py:313
  38.2 7.3 %copy-start.3 = (f32[10,24,2048]{2,1,0:T(8,128)S(1)}, f32[10,24,2048]{2,1,0:T(8,128)}, u32[]{:S(2)}) copy-start(f32[10,24,2048]{2,1,0:T(8,128)} %velocity_ref.1) | copy-start | bytes 5898244
  38.2 7.3 %collective-permute-start.6 = (f32[8,128]{1,0:T(8,128)S(1)}, f32[8,128]{1,0:T(8,128)S(1)}, u32[]{:S(2)}, u32[]{:S(2)}) collective-permute-start(f32[8,128]{1,0:T(8,128)S(1)} %add.11.near_ref), channel_id=1, source_target_pairs={{0,8},{2,10},{4,12},{6,14},{8,0},{10,2},{12,4},{14,6},{1,9},{3,11}... | collective-permute-start | bytes 12296 | tf_op jit(solution)/shard_map/ppermute | solution.py:314

commit v2 on v1

v2 whole, which is shorter than its diff:
```python
import functools

import jax
import jax.numpy as jnp
from jax import lax
from jax.experimental import pallas as pl
from jax.experimental.pallas import tpu as pltpu
from jax.sharding import PartitionSpec as P

NZ = 64
SLOTS = 3
LANES = 128
EDGE = 3
F32 = jnp.float32
BF16 = jnp.bfloat16

VMEM = pl.BlockSpec(memory_space=pltpu.VMEM)
SMEM = pl.BlockSpec(memory_space=pltpu.SMEM)
HBM = pl.BlockSpec(memory_space=pltpu.HBM)


def params(mib):
    return pltpu.CompilerParams(vmem_limit_bytes=mib * 1024 * 1024)


def cost(flops, nbytes):
    return pl.CostEstimate(flops=flops, bytes_accessed=nbytes, transcendentals=0)


def in_hbm(array):
    return pltpu.with_memory_space_constraint(array, pltpu.HBM)


def split(value):
    high = value.astype(BF16)
    return high, (value - high.astype(F32)).astype(BF16)


def build_mix(mix, out_ref):
    zero = jnp.zeros((NZ, NZ), F32)
    pair = jnp.concatenate(
        [jnp.concatenate([mix, zero], axis=1), jnp.concatenate([zero, mix], axis=1)], axis=0
    )
    high, low = split(pair)
    out_ref[0:LANES, 0:LANES] = high
    out_ref[LANES:, 0:LANES] = high
    out_ref[0:LANES, LANES:] = low
    out_ref[LANES:, LANES:] = jnp.zeros((LANES, LANES), BF16)


def columns(tiles, taps):
    count = len(tiles)
    lower = lax.broadcasted_iota(jnp.int32, tiles[0].shape, 1) < NZ
    zero = jnp.zeros_like(tiles[0])
    turned = [pltpu.roll(tile, NZ, 1) for tile in tiles]
    between = {}
    for t in range(-1, count):
        first = turned[t] if t >= 0 else zero
        second = turned[t + 1] if t + 1 < count else zero
        between[t] = jnp.where(lower, first, second)
    outs = []
    for t in range(count):
        total = taps[3] * tiles[t]
        for k, at in ((1, t - 1), (5, t + 1)):
            if 0 <= at < count:
                total += taps[k] * tiles[at]
        for k, at in ((0, t - 2), (2, t - 1), (4, t), (6, t + 1)):
            if at in between:
                total += taps[k] * between[at]
        outs.append(total)
    return outs


def store_split(ref, stride, row, upper, lower):
    for t, (first, second) in enumerate(zip(upper, lower)):
        high, low = split(jnp.concatenate([first, second], axis=0))
        ref[stride * t + row : stride * t + row + 16, 0:LANES] = high
        ref[stride * t + row : stride * t + row + 16, LANES:] = low


def mixed(ref, start, size, matrix):
    both = jnp.dot(ref[start : start + size, :], matrix, preferred_element_type=F32)
    return both[:, 0:LANES] + both[:, LANES:]


def lanes_of(t):
    return slice(LANES * t, LANES * (t + 1))


def stage_kernel(perturb_hbm, mine_hbm, perturb_ref, mine_ref, sems):
    members = perturb_ref.shape[0]
    copies = [pltpu.make_async_copy(mine_hbm, mine_ref, sems.at[members])]
    for member in range(members):
        copies.append(pltpu.make_async_copy(perturb_hbm.at[member], perturb_ref.at[member], sems.at[member]))
    for copy in copies:
        copy.start()
    for copy in copies:
        copy.wait()


def border_kernel(owner_ref, perturb_ref, mine_ref, other_ref, up_ref, down_ref):
    members, _, rows, cells = perturb_ref.shape
    me = lax.axis_index("member")
    valid = [owner_ref[slot] == me for slot in range(SLOTS)]
    for t in range(cells // LANES):
        for start, ref, first in ((0, down_ref, 0), (rows - 8, up_ref, 8 - EDGE)):
            fields = [
                jnp.where(
                    valid[slot],
                    mine_ref[0, slot, start : start + 8, lanes_of(t)],
                    other_ref[0, slot, start : start + 8, lanes_of(t)],
                )
                for slot in range(SLOTS)
            ]
            for member in range(members):
                total = perturb_ref[member, 0, start : start + 8, lanes_of(t)].astype(F32) * fields[0]
                for slot in range(1, SLOTS):
                    total += perturb_ref[member, slot, start : start + 8, lanes_of(t)].astype(F32) * fields[slot]
                at = EDGE * (members * t + member)
                ref[at : at + EDGE, :] = total[first : first + EDGE]


def bulk_kernel(
    owner_ref, taps_x_ref, taps_y_ref, mix_ref, perturb_ref, mine_ref, other_ref, control_hbm, velocity_hbm,
    local_ref, cross_up_ref, cross_down_ref, square_ref, control_ref, velocity_ref,
    field, rows_of, left, turned, matrix, matrix_t, sems,
):
    members, _, rows, cells = perturb_ref.shape
    count = cells // LANES
    tall = rows + 16
    control_copy = pltpu.make_async_copy(control_hbm, control_ref, sems.at[0])
    velocity_copy = pltpu.make_async_copy(velocity_hbm, velocity_ref, sems.at[1])
    control_copy.start()
    velocity_copy.start()
    me = lax.axis_index("member")
    tile = lax.axis_index("tile")
    tiles = lax.axis_size("tile")
    taps_x = [taps_x_ref[k] for k in range(7)]
    taps_y = [taps_y_ref[k] for k in range(7)]
    build_mix(mix_ref[...], matrix)
    build_mix(mix_ref[...].T, matrix_t)
    for slot in range(SLOTS):
        field[slot] = jnp.where(owner_ref[slot] == me, mine_ref[0, slot], other_ref[0, slot])
    for half in range(2):
        rows_of[half, :, 0:8, :] = jnp.zeros((count, 8, LANES), F32)
        rows_of[half, :, tall - 8 : tall, :] = jnp.zeros((count, 8, LANES), F32)
    weight_top = jnp.where(tile > 0, 1.0, 0.0).astype(F32)
    weight_bottom = jnp.where(tile < tiles - 1, 1.0, 0.0).astype(F32)

    def pair_step(pair, carry):
        for half in range(2):
            member = 2 * pair + half
            for t in range(count):
                product = perturb_ref[member, 0, :, lanes_of(t)].astype(F32) * field[0, :, lanes_of(t)]
                for slot in range(1, SLOTS):
                    product += perturb_ref[member, slot, :, lanes_of(t)].astype(F32) * field[slot, :, lanes_of(t)]
                rows_of[half, t, 8 : 8 + rows, :] = product
        blocks = []
        for half in range(2):
            for row in range(0, tall, 8):
                used = range(7)
                if row == 0:
                    used = range(4, 7)
                if row == tall - 8:
                    used = range(0, 3)
                block = []
                for t in range(count):
                    total = None
                    for k in used:
                        term = taps_x[k] * rows_of[half, t, row + k - 3 : row + k + 5, :]
                        total = term if total is None else total + term
                    block.append(total)
                blocks.append(columns(block, taps_y))
                if len(blocks) == 2:
                    at = half * tall + row - 8
                    store_split(left, 2 * tall, at, *blocks)
                    blocks = []
        pl.when(pair == 0)(control_copy.wait)
        group = 4
        for first in range(0, count, group):
            size = 2 * tall
            out = mixed(left, size * first, size * group, matrix[...])
            for t in range(first, first + group):
                for half in range(2):
                    member = 2 * pair + half
                    base = size * (t - first) + tall * half
                    here = control_ref[member, :, lanes_of(t)] + out[base + 8 : base + 8 + rows]
                    local_ref[member, :, lanes_of(t)] = here
                    squared = here * here
                    for row in range(0, rows, 8):
                        carry += squared[row : row + 8]
                    above, below = out[base : base + 8], out[base + tall - 8 : base + tall]
                    carry += weight_top * (above * above) + weight_bottom * (below * below)
        return carry

    square_ref[...] = lax.fori_loop(0, members // 2, pair_step, jnp.zeros((8, LANES), F32))
    velocity_copy.wait()
    back = taps_y[::-1]

    def turn_step(pair, carry):
        for half in range(2):
            member = 2 * pair + half
            for t in range(count):
                rows_of[half, t, 8:16, :] = local_ref[member, 0:8, lanes_of(t)]
                rows_of[half, t, rows : rows + 8, :] = local_ref[member, rows - 8 : rows, lanes_of(t)]
        for half in range(2):
            first, last = [], []
            for t in range(count):
                total = taps_x[0] * rows_of[half, t, 8:16, :]
                other = taps_x[6] * rows_of[half, t, rows : rows + 8, :]
                for d in range(1, EDGE):
                    total += taps_x[d] * rows_of[half, t, 8 - d : 16 - d, :]
                    other += taps_x[6 - d] * rows_of[half, t, rows + d : rows + 8 + d, :]
                first.append(total)
                last.append(other)
            store_split(left, 32, 16 * half, columns(first, back), columns(last, back))
        out = mixed(left, 0, 32 * count, matrix_t[...])
        for t in range(count):
            for half in range(2):
                turned[2 * pair + half, t] = out[32 * t + 16 * half : 32 * t + 16 * half + 16]
        return carry

    lax.fori_loop(0, members // 2, turn_step, 0)
    for member in range(members):
        for t in range(count):
            at = EDGE * (members * t + member)
            cross_up_ref[at : at + EDGE, :] = turned[member, t, 0:EDGE, :]
            cross_down_ref[at : at + EDGE, :] = turned[member, t, 16 - EDGE : 16, :]


def cross_kernel(square_ref, cross_up_ref, cross_down_ref, from_left_ref, from_right_ref, total_ref):
    total = [jnp.zeros((8, LANES), F32) for _ in range(4)]
    for step, row in enumerate(range(0, cross_up_ref.shape[0], 8)):
        at = slice(row, row + 8)
        which = 2 * (step % 2)
        total[which] += cross_up_ref[at] * from_left_ref[at]
        total[which + 1] += cross_down_ref[at] * from_right_ref[at]
    total_ref[...] = square_ref[...] + 2.0 * ((total[0] + total[1]) + (total[2] + total[3]))


def correct_kernel(
    taps_x_ref, taps_y_ref, mix_ref, from_left_ref, from_right_ref, correction_ref, rows_of, left, matrix
):
    members, _, cells = correction_ref.shape
    count = cells // LANES
    taps_x = [taps_x_ref[k] for k in range(7)]
    taps_y = [taps_y_ref[k] for k in range(7)]
    build_mix(mix_ref[...], matrix)
    zero = jnp.zeros((8, LANES), F32)
    for member in range(members):
        for t in range(count):
            at = EDGE * (members * t + member)
            for row in range(0, 32, 8):
                rows_of[member, t, row : row + 8, :] = zero
            rows_of[member, t, 0:EDGE, :] = from_left_ref[at : at + EDGE, :]
            rows_of[member, t, 32 - EDGE : 32, :] = from_right_ref[at : at + EDGE, :]

    def pair_step(pair, carry):
        for half in range(2):
            member = 2 * pair + half
            first, last = [], []
            for t in range(count):
                total = taps_x[0] * rows_of[member, t, 0:8, :]
                other = taps_x[6] * rows_of[member, t, 24:32, :]
                for d in range(1, EDGE):
                    total += taps_x[d] * rows_of[member, t, d : 8 + d, :]
                    other += taps_x[6 - d] * rows_of[member, t, 24 - d : 32 - d, :]
                first.append(total)
                last.append(other)
            store_split(left, 32, 16 * half, columns(first, taps_y), columns(last, taps_y))
        out = mixed(left, 0, 32 * count, matrix[...])
        for t in range(count):
            for half in range(2):
                correction_ref[2 * pair + half, :, lanes_of(t)] = out[32 * t + 16 * half : 32 * t + 16 * half + 16]
        return carry

    lax.fori_loop(0, members // 2, pair_step, 0)


def update_kernel(
    entries, near_ref, far_ref, control_ref, velocity_ref, local_ref, correction_ref,
    new_control_hbm, new_velocity_hbm, new_control, new_velocity, sems,
):
    members, rows, cells = control_ref.shape
    mean = jnp.sum(near_ref[...] + far_ref[...], keepdims=True) / entries
    scale = lax.rsqrt(mean + 1e-06)
    copies = []
    for member in range(members):
        for start in range(0, rows, 8):
            tile = slice(start, start + 8)
            gradient = local_ref[member, tile]
            if start == 0:
                gradient += correction_ref[member, 0:8]
            if start == rows - 8:
                gradient += correction_ref[member, 8:16]
            moved = 0.9 * velocity_ref[member, tile] + scale * gradient
            new_velocity[member, tile] = moved
            new_control[member, tile] = control_ref[member, tile] - 0.5 * moved
        for which, (src, dst) in enumerate(((new_control, new_control_hbm), (new_velocity, new_velocity_hbm))):
            copy = pltpu.make_async_copy(src.at[member], dst.at[member], sems.at[which, member])
            copy.start()
            copies.append(copy)
    for copy in copies:
        copy.wait()


def body(control, velocity, perturb, adjoint_forcing, slot_owner, taps_x, taps_y, vertical_mix):
    members, rows, cells = control.shape
    count = cells // LANES
    tiles = lax.axis_size("tile")
    groups = lax.axis_size("member")
    owner = slot_owner.reshape(SLOTS)
    swap = [(0, 1), (1, 0)]
    other = lax.ppermute(adjoint_forcing, "member", swap)
    perturb, mine = pl.pallas_call(
        stage_kernel,
        name="stage",
        out_shape=(
            jax.ShapeDtypeStruct(perturb.shape, perturb.dtype),
            jax.ShapeDtypeStruct(adjoint_forcing.shape, F32),
        ),
        in_specs=[HBM, HBM],
        out_specs=(VMEM, VMEM),
        scratch_shapes=[pltpu.SemaphoreType.DMA((members + 1,))],
        compiler_params=params(8),
        cost_estimate=cost(0, 8_000_000),
    )(in_hbm(perturb), in_hbm(adjoint_forcing))
    packed = jax.ShapeDtypeStruct((EDGE * members * count, LANES), F32)
    up, down = pl.pallas_call(
        border_kernel,
        name="border_product",
        out_shape=(packed, packed),
        in_specs=[SMEM, VMEM, VMEM, VMEM],
        out_specs=(VMEM, VMEM),
        compiler_params=params(8),
        cost_estimate=cost(4_000_000, 4_000_000),
    )(owner, perturb, mine, other)
    from_left = lax.ppermute(up, "tile", [(i, i + 1) for i in range(tiles - 1)])
    from_right = lax.ppermute(down, "tile", [(i + 1, i) for i in range(tiles - 1)])
    matrix = pltpu.VMEM((2 * LANES, 2 * LANES), BF16)
    whole = jax.ShapeDtypeStruct(control.shape, F32)
    local, cross_up, cross_down, square, control, velocity = pl.pallas_call(
        bulk_kernel,
        name="bulk",
        out_shape=(whole, packed, packed, jax.ShapeDtypeStruct((8, LANES), F32), whole, whole),
        in_specs=[SMEM, SMEM, SMEM, VMEM, VMEM, VMEM, VMEM, HBM, HBM],
        out_specs=(VMEM,) * 6,
        scratch_shapes=[
            pltpu.VMEM((SLOTS, rows, cells), F32),
            pltpu.VMEM((2, count, rows + 16, LANES), F32),
            pltpu.VMEM((count * 2 * (rows + 16), 2 * LANES), BF16),
            pltpu.VMEM((members, count, 16, LANES), F32),
            matrix, matrix,
            pltpu.SemaphoreType.DMA((2,)),
        ],
        compiler_params=params(24),
        cost_estimate=cost(9_000_000_000, 12_000_000),
    )(owner, taps_x, taps_y, vertical_mix, perturb, mine, other, in_hbm(control), in_hbm(velocity))
    near = pl.pallas_call(
        cross_kernel,
        name="cross_term",
        out_shape=jax.ShapeDtypeStruct((8, LANES), F32),
        in_specs=[VMEM] * 5,
        out_specs=VMEM,
        compiler_params=params(8),
        cost_estimate=cost(200_000, 1_000_000),
    )(square, cross_up, cross_down, from_left, from_right)
    correction = pl.pallas_call(
        correct_kernel,
        name="border_correction",
        out_shape=jax.ShapeDtypeStruct((members, 16, cells), F32),
        in_specs=[SMEM, SMEM, VMEM, VMEM, VMEM],
        out_specs=VMEM,
        scratch_shapes=[
            pltpu.VMEM((members, count, 32, LANES), F32),
            pltpu.VMEM((count * 32, 2 * LANES), BF16),
            matrix,
        ],
        compiler_params=params(16),
        cost_estimate=cost(2_000_000_000, 2_000_000),
    )(taps_x, taps_y, vertical_mix, from_left, from_right)
    steps = [("member", swap)]
    width = 1
    while width < tiles:
        steps.append(("tile", [(i, i ^ width) for i in range(tiles)]))
        width *= 2
    for axis, pairs in steps[:-1]:
        near = near + lax.ppermute(near, axis, pairs)
    far = lax.ppermute(near, *steps[-1])
    entries = members * groups * rows * tiles * cells
    return tuple(
        pl.pallas_call(
            functools.partial(update_kernel, float(entries)),
            name="update",
            out_shape=(whole, whole),
            in_specs=[VMEM] * 6,
            out_specs=(HBM, HBM),
            scratch_shapes=[
                pltpu.VMEM(control.shape, F32),
                pltpu.VMEM(control.shape, F32),
                pltpu.SemaphoreType.DMA((2, members)),
            ],
            compiler_params=params(16),
            cost_estimate=cost(3_000_000, 12_000_000),
        )(near, far, control, velocity, local, correction)
    )


def solution(mesh):
    placed = (
        P(("window", "member"), "tile", None),
        P(("window", "member"), "tile", None),
        P(("window", "member"), None, "tile", None),
        P(("window", "member"), None, "tile", None),
        P("window", "tile"),
        P(),
        P(),
        P(),
    )
    return jax.shard_map(
        body,
        mesh=mesh,
        in_specs=placed,
        out_specs=(P(("window", "member"), "tile", None), P(("window", "member"), "tile", None)),
        check_vma=False,
    )
```

time: 48 us -> 37.7 us (0.79)
  local copies, waits for them, and re-layouts: 5.2 us -> 0.02 us
  Pallas kernels: 20.9 us -> 17.1 us
  waiting for transfers between devices: 5.43 us -> 4.74 us
  starting transfers between devices: 15.5 us -> 15 us
    unnamed x19 -> x8, local copies, waits for them, and re-layouts: 5.2 us -> 0.02 us
    pallas_call x1 -> x2, Pallas kernels: 13.3 us -> 11.3 us  [the longest x1 9.22 us: body(): pl.pallas_call(bulk_kernel, name='bulk', out_shape=(whole, packed, packed...]
    pallas_call x1, Pallas kernels: 4.29 us -> 2.56 us  [body(): pl.pallas_call(correct_kernel, name='border_correction', out_shape=jax.Sh...]
    ppermute x1, waiting for transfers between devices: 1.1 us -> 0.01 us  [body(): other = lax.ppermute(adjoint_forcing, 'member', swap)]
  transfers between devices with their start and end apart: 7 -> 7, of which waited for: 4 -> 4; matrix products, arithmetic and copies ran while one was open for 2% -> 0% of each run, Pallas kernels for 37% -> 37%
where the time goes in v2:
time: 37.7 us; the launch traced here: 37.6 us
  Pallas kernels  17.1 us (45%)
  starting transfers between devices  15 us (40%)
  waiting for transfers between devices  4.74 us (13%)
  between operations  0.77 us (2%)
    pallas_call x1, Pallas kernels, body(): pl.pallas_call(bulk_kernel, name='bulk', out_shape=(whole, packed, packed...  9.22 us
    ppermute x3, starting transfers between devices, body(): near = near + lax.ppermute(near, axis, pairs)  5.53 us
    ppermute x1, starting transfers between devices, body(): from_left = lax.ppermute(up, 'tile', [(i, i + 1) for i in range(tiles - 1)])  4.58 us
    ppermute x3, waiting for transfers between devices, body(): near = near + lax.ppermute(near, axis, pairs)  4.32 us
    ppermute x1, starting transfers between devices, body(): far = lax.ppermute(near, *steps[-1])  3.04 us
    pallas_call x1, Pallas kernels, body(): pl.pallas_call(correct_kernel, name='border_correction', out_shape=jax.Sh...  2.56 us
    pallas_call x1, Pallas kernels, body(): pl.pallas_call(functools.partial(update_kernel, float(entries)), name='up...  2.24 us
    pallas_call x1, Pallas kernels, body(): pl.pallas_call(stage_kernel, name='stage', out_shape=(jax.ShapeDtypeStruc...  2.03 us
  transfers between devices with their start and end apart: 7, of which 4 were waited for; matrix products, arithmetic and copies ran while one was open for 0% of the time, Pallas kernels for 37%

profile of v2, /device:TPU:0, one launch (start us, length us, event | category | flops | bytes accessed | tf_op | source)
XLA Modules:
  0.0 37.6 jit_solution(4649713291349960883)
XLA Ops:
  0.6 0.0 copy-start
  0.6 0.5 %collective-permute-start = (f32[1,3,24,2048]{3,2,1,0:T(8,128)}, f32[1,3,24,2048]{3,2,1,0:T(8,128)S(1)}, u32[]{:S(2)}, u32[]{:S(2)}) collective-permute-start(f32[1,3,24,2048]{3,2,1,0:T(8,128)} %mine_hbm.1), channel_id=1, source_target_pairs={{0,1},{1,0},{2,3},{3,2},{4,5},{5,4},{6,7},{7,6},{8,9},{9,8},{10,11... | collective-permute-start | bytes 1769480 | tf_op jit(solution)/shard_map/ppermute | solution.py:314
  1.2 2.0 %stage.1 = (bf16[10,3,24,2048]{3,2,1,0:T(8,128)(2,1)S(1)}, f32[1,3,24,2048]{3,2,1,0:T(8,128)S(1)}) custom-call(bf16[10,3,24,2048]{3,2,1,0:T(8,128)(2,1)} %perturb_hbm.1, f32[1,3,24,2048]{3,2,1,0:T(8,128)} %mine_hbm.1), custom_call_target="tpu_custom_call" | custom-call | bytes 8000000 | tf_op jit(solution)/shard_map/stage/pallas_call | solution.py:315
  3.2 0.0 collective-permute-done.other_ref
  3.2 0.0 copy-done
  3.2 0.0 copy-start.1
  3.2 0.0 copy-start.2
  3.2 0.0 copy-start.3
  3.3 1.0 %border_product.1 = (f32[480,128]{1,0:T(8,128)S(1)}, f32[480,128]{1,0:T(8,128)S(1)}) custom-call(s32[3]{0:T(128)S(1)} %bitcast.1, bf16[10,3,24,2048]{3,2,1,0:T(8,128)(2,1)S(1)} %get-tuple-element.12.perturb_ref, f32[1,3,24,2048]{3,2,1,0:T(8,128)S(1)} %get-tuple-element.13.mine_ref, f32[1,3,24,2048]{3,2,1,0:T(8,128)S(1)} %collective-permute-done.other_ref), custom_call_target="tpu_custom_call" | custom-call | flops 4000000 | bytes 4000000 | tf_op jit(solution)/shard_map/border_product/pallas_call | solution.py:329
  4.2 4.6 %collective-permute-start.1 = (f32[480,128]{1,0:T(8,128)S(1)}, f32[480,128]{1,0:T(8,128)S(1)}, u32[]{:S(2)}, u32[]{:S(2)}) collective-permute-start(f32[480,128]{1,0:T(8,128)S(1)} %get-tuple-element.17), channel_id=1, source_target_pairs={{0,2},{2,4},{4,6},{6,8},{8,10},{10,12},{12,14},{1,3},{3,5},{5,7},{... | collective-permute-start | bytes 737288 | tf_op jit(solution)/shard_map/ppermute | solution.py:338
  8.8 1.3 %collective-permute-start.2 = (f32[480,128]{1,0:T(8,128)S(1)}, f32[480,128]{1,0:T(8,128)S(1)}, u32[]{:S(2)}, u32[]{:S(2)}) collective-permute-start(f32[480,128]{1,0:T(8,128)S(1)} %get-tuple-element.18), channel_id=1, source_target_pairs={{2,0},{4,2},{6,4},{8,6},{10,8},{12,10},{14,12},{3,1},{5,3},{7,5},{... | collective-permute-start | bytes 737288 | tf_op jit(solution)/shard_map/ppermute | solution.py:339
  10.1 0.0 copy-done.1
  10.1 0.0 copy-done.2
  10.1 0.0 copy-done.3
  10.1 9.2 %bulk.1 = (f32[10,24,2048]{2,1,0:T(8,128)S(1)}, f32[480,128]{1,0:T(8,128)S(1)}, f32[480,128]{1,0:T(8,128)S(1)}, f32[8,128]{1,0:T(8,128)S(1)}, f32[10,24,2048]{2,1,0:T(8,128)S(1)}, /*index=5*/f32[10,24,2048]{2,1,0:T(8,128)S(1)}) custom-call(s32[3]{0:T(128)S(1)} %bitcast.2, f32[7]{0:T(128)S(1)} %copy-done.2, f32[7]{0:T(128)S(1)} %copy-done.3, ...), custom_call_target="tpu_custom_call" | custom-call | flops 8999999488 | bytes 12000000 | tf_op jit(solution)/shard_map/bulk/pallas_call | solution.py:342
  19.4 0.4 %collective-permute-done.1.from_left_ref = f32[480,128]{1,0:T(8,128)S(1)} collective-permute-done((f32[480,128]{1,0:T(8,128)S(1)}, f32[480,128]{1,0:T(8,128)S(1)}, u32[]{:S(2)}, u32[]{:S(2)}) %collective-permute-start.1) | collective-permute-done | bytes 245792 | tf_op jit(solution)/shard_map/ppermute | solution.py:338
  19.8 0.0 collective-permute-done.2.from_right_ref
  19.8 0.1 cross_term.1
  19.8 0.1 collective-permute-start.3
  19.9 1.2 %collective-permute-done.3 = f32[8,128]{1,0:T(8,128)S(1)} collective-permute-done((f32[8,128]{1,0:T(8,128)S(1)}, f32[8,128]{1,0:T(8,128)S(1)}, u32[]{:S(2)}, u32[]{:S(2)}) %collective-permute-start.3) | collective-permute-done | bytes 4128 | tf_op jit(solution)/shard_map/ppermute | solution.py:388
  21.1 2.5 %collective-permute-start.4 = (f32[8,128]{1,0:T(8,128)S(1)}, f32[8,128]{1,0:T(8,128)S(1)}, u32[]{:S(2)}, u32[]{:S(2)}) collective-permute-start(f32[8,128]{1,0:T(8,128)S(1)} %add.9), channel_id=1, source_target_pairs={{0,2},{2,0},{4,6},{6,4},{8,10},{10,8},{12,14},{14,12},{1,3},{3,1},... | collective-permute-start | bytes 12296 | tf_op jit(solution)/shard_map/ppermute | solution.py:388
  23.6 1.6 %collective-permute-done.4 = f32[8,128]{1,0:T(8,128)S(1)} collective-permute-done((f32[8,128]{1,0:T(8,128)S(1)}, f32[8,128]{1,0:T(8,128)S(1)}, u32[]{:S(2)}, u32[]{:S(2)}) %collective-permute-start.4) | collective-permute-done | bytes 4128 | tf_op jit(solution)/shard_map/ppermute | solution.py:388
  25.1 3.0 %collective-permute-start.5 = (f32[8,128]{1,0:T(8,128)S(1)}, f32[8,128]{1,0:T(8,128)S(1)}, u32[]{:S(2)}, u32[]{:S(2)}) collective-permute-start(f32[8,128]{1,0:T(8,128)S(1)} %add.10), channel_id=1, source_target_pairs={{0,4},{2,6},{4,0},{6,2},{8,12},{10,14},{12,8},{14,10},{1,5},{3,7},... | collective-permute-start | bytes 12296 | tf_op jit(solution)/shard_map/ppermute | solution.py:388
  28.1 1.6 %collective-permute-done.5 = f32[8,128]{1,0:T(8,128)S(1)} collective-permute-done((f32[8,128]{1,0:T(8,128)S(1)}, f32[8,128]{1,0:T(8,128)S(1)}, u32[]{:S(2)}, u32[]{:S(2)}) %collective-permute-start.5) | collective-permute-done | bytes 4128 | tf_op jit(solution)/shard_map/ppermute | solution.py:388
  29.7 3.0 %collective-permute-start.6 = (f32[8,128]{1,0:T(8,128)S(1)}, f32[8,128]{1,0:T(8,128)S(1)}, u32[]{:S(2)}, u32[]{:S(2)}) collective-permute-start(f32[8,128]{1,0:T(8,128)S(1)} %add.11.near_ref), channel_id=1, source_target_pairs={{0,8},{2,10},{4,12},{6,14},{8,0},{10,2},{12,4},{14,6},{1,9},{3,11}... | collective-permute-start | bytes 12296 | tf_op jit(solution)/shard_map/ppermute | solution.py:389
  32.7 2.6 %border_correction.1.correction_ref = f32[10,16,2048]{2,1,0:T(8,128)S(1)} custom-call(f32[7]{0:T(128)S(1)} %copy-done.2, f32[7]{0:T(128)S(1)} %copy-done.3, f32[64,64]{1,0:T(8,128)S(1)} %copy-done.1, f32[480,128]{1,0:T(8,128)S(1)} %collective-permute-done.1.from_left_ref, f32[480,128]{1,0:T(8,128)S(1)} %collective-permute-done.2.from_right_ref), custom_call_target="tpu_custom_call" | custom-call | flops 2000000000 | bytes 2000000 | tf_op jit(solution)/shard_map/border_correction/pallas_call | solution.py:368
  35.3 0.0 collective-permute-done.6.far_ref
  35.3 2.2 %update.1 = (f32[10,24,2048]{2,1,0:T(8,128)}, f32[10,24,2048]{2,1,0:T(8,128)}) custom-call(f32[8,128]{1,0:T(8,128)S(1)} %add.11.near_ref, f32[8,128]{1,0:T(8,128)S(1)} %collective-permute-done.6.far_ref, f32[10,24,2048]{2,1,0:T(8,128)S(1)} %get-tuple-element.19.control_ref, f32[10,24,2048]{2,1,0:T(8,128)S(1)} %get-tuple-element.20.velocity_ref, ...), custom_call_target="tpu_custom_call" | custom-call | flops 3000000 | bytes 12000000 | tf_op jit(solution)/shard_map/update/pallas_call | solution.py:392
  (3 shorter events, 0.0 us)
Async XLA Ops:
  0.6 2.6 %copy-start = (s32[3,1]{0,1:T(1,128)S(1)}, s32[3,1]{0,1:T(1,128)}, u32[]{:S(2)}) copy-start(s32[3,1]{0,1:T(1,128)} %param.12) | copy-start | bytes 40
  0.6 2.6 %collective-permute-start = (f32[1,3,24,2048]{3,2,1,0:T(8,128)}, f32[1,3,24,2048]{3,2,1,0:T(8,128)S(1)}, u32[]{:S(2)}, u32[]{:S(2)}) collective-permute-start(f32[1,3,24,2048]{3,2,1,0:T(8,128)} %mine_hbm.1), channel_id=1, source_target_pairs={{0,1},{1,0},{2,3},{3,2},{4,5},{5,4},{6,7},{7,6},{8,9},{9,8},{10,11... | collective-permute-start | bytes 1769480 | tf_op jit(solution)/shard_map/ppermute | solution.py:314
  3.2 6.9 %copy-start.1 = (f32[64,64]{1,0:T(8,128)S(1)}, f32[64,64]{1,0:T(8,128)}, u32[]{:S(2)}) copy-start(f32[64,64]{1,0:T(8,128)} %mix_ref.3) | copy-start | bytes 49156
  3.2 6.9 %copy-start.2 = (f32[7]{0:T(128)S(1)}, f32[7]{0:T(128)}, u32[]{:S(2)}) copy-start(f32[7]{0:T(128)} %taps_x_ref.3) | copy-start | bytes 88
  3.2 6.9 %copy-start.3 = (f32[7]{0:T(128)S(1)}, f32[7]{0:T(128)}, u32[]{:S(2)}) copy-start(f32[7]{0:T(128)} %taps_y_ref.3) | copy-start | bytes 88
  4.2 15.6 %collective-permute-start.1 = (f32[480,128]{1,0:T(8,128)S(1)}, f32[480,128]{1,0:T(8,128)S(1)}, u32[]{:S(2)}, u32[]{:S(2)}) collective-permute-start(f32[480,128]{1,0:T(8,128)S(1)} %get-tuple-element.17), channel_id=1, source_target_pairs={{0,2},{2,4},{4,6},{6,8},{8,10},{10,12},{12,14},{1,3},{3,5},{5,7},{... | collective-permute-start | bytes 737288 | tf_op jit(solution)/shard_map/ppermute | solution.py:338
  8.8 11.0 %collective-permute-start.2 = (f32[480,128]{1,0:T(8,128)S(1)}, f32[480,128]{1,0:T(8,128)S(1)}, u32[]{:S(2)}, u32[]{:S(2)}) collective-permute-start(f32[480,128]{1,0:T(8,128)S(1)} %get-tuple-element.18), channel_id=1, source_target_pairs={{2,0},{4,2},{6,4},{8,6},{10,8},{12,10},{14,12},{3,1},{5,3},{7,5},{... | collective-permute-start | bytes 737288 | tf_op jit(solution)/shard_map/ppermute | solution.py:339
  19.8 1.2 %collective-permute-start.3 = (f32[8,128]{1,0:T(8,128)S(1)}, f32[8,128]{1,0:T(8,128)S(1)}, u32[]{:S(2)}, u32[]{:S(2)}) collective-permute-start(f32[8,128]{1,0:T(8,128)S(1)} %cross_term.1), channel_id=1, source_target_pairs={{0,1},{1,0},{2,3},{3,2},{4,5},{5,4},{6,7},{7,6},{8,9},{9,8},{10,11... | collective-permute-start | bytes 12296 | tf_op jit(solution)/shard_map/ppermute | solution.py:388
  21.1 4.1 %collective-permute-start.4 = (f32[8,128]{1,0:T(8,128)S(1)}, f32[8,128]{1,0:T(8,128)S(1)}, u32[]{:S(2)}, u32[]{:S(2)}) collective-permute-start(f32[8,128]{1,0:T(8,128)S(1)} %add.9), channel_id=1, source_target_pairs={{0,2},{2,0},{4,6},{6,4},{8,10},{10,8},{12,14},{14,12},{1,3},{3,1},... | collective-permute-start | bytes 12296 | tf_op jit(solution)/shard_map/ppermute | solution.py:388
  25.1 4.6 %collective-permute-start.5 = (f32[8,128]{1,0:T(8,128)S(1)}, f32[8,128]{1,0:T(8,128)S(1)}, u32[]{:S(2)}, u32[]{:S(2)}) collective-permute-start(f32[8,128]{1,0:T(8,128)S(1)} %add.10), channel_id=1, source_target_pairs={{0,4},{2,6},{4,0},{6,2},{8,12},{10,14},{12,8},{14,10},{1,5},{3,7},... | collective-permute-start | bytes 12296 | tf_op jit(solution)/shard_map/ppermute | solution.py:388
  29.7 5.6 %collective-permute-start.6 = (f32[8,128]{1,0:T(8,128)S(1)}, f32[8,128]{1,0:T(8,128)S(1)}, u32[]{:S(2)}, u32[]{:S(2)}) collective-permute-start(f32[8,128]{1,0:T(8,128)S(1)} %add.11.near_ref), channel_id=1, source_target_pairs={{0,8},{2,10},{4,12},{6,14},{8,0},{10,2},{12,4},{14,6},{1,9},{3,11}... | collective-permute-start | bytes 12296 | tf_op jit(solution)/shard_map/ppermute | solution.py:389

commit v3 on v2

--- a/solution.py
+++ b/solution.py
@@ -87,37 +87,59 @@
     return slice(LANES * t, LANES * (t + 1))
 
 
-def stage_kernel(perturb_hbm, mine_hbm, perturb_ref, mine_ref, sems):
-    members = perturb_ref.shape[0]
-    copies = [pltpu.make_async_copy(mine_hbm, mine_ref, sems.at[members])]
+def stage_kernel(perturb_hbm, mine_hbm, perturb_ref, mine_ref, border_ref, sems):
+    members, _, rows, cells = perturb_ref.shape
+    copies = []
     for member in range(members):
         copies.append(pltpu.make_async_copy(perturb_hbm.at[member], perturb_ref.at[member], sems.at[member]))
+    copies.append(pltpu.make_async_copy(mine_hbm, mine_ref, sems.at[members]))
     for copy in copies:
         copy.start()
-    for copy in copies:
-        copy.wait()
-
-
-def border_kernel(owner_ref, perturb_ref, mine_ref, other_ref, up_ref, down_ref):
-    members, _, rows, cells = perturb_ref.shape
+    for member in range(members):
+        copies[member].wait()
+        for slot in range(SLOTS):
+            for t in range(cells // LANES):
+                at = EDGE * (members * t + member)
+                for side, start, first in ((0, 0, 0), (1, rows - 8, 8 - EDGE)):
+                    value = perturb_ref[member, slot, start : start + 8, lanes_of(t)].astype(F32)
+                    border_ref[slot, side, at : at + EDGE, :] = value[first : first + EDGE]
+    copies[members].wait()
+
+
+def border_kernel(owner_ref, border_ref, mine_ref, other_ref, up_ref, down_ref):
+    _, _, rows, cells = mine_ref.shape
+    total_rows = up_ref.shape[0]
+    per_tile = total_rows // (cells // LANES)
     me = lax.axis_index("member")
     valid = [owner_ref[slot] == me for slot in range(SLOTS)]
-    for t in range(cells // LANES):
-        for start, ref, first in ((0, down_ref, 0), (rows - 8, up_ref, 8 - EDGE)):
-            fields = [
-                jnp.where(
-                    valid[slot],
-                    mine_ref[0, slot, start : start + 8, lanes_of(t)],
-                    other_ref[0, slot, start : start + 8, lanes_of(t)],
-                )
-                for slot in range(SLOTS)
-            ]
-            for member in range(members):
-                total = perturb_ref[member, 0, start : start + 8, lanes_of(t)].astype(F32) * fields[0]
-                for slot in range(1, SLOTS):
-                    total += perturb_ref[member, slot, start : start + 8, lanes_of(t)].astype(F32) * fields[slot]
-                at = EDGE * (members * t + member)
-                ref[at : at + EDGE, :] = total[first : first + EDGE]
+    sublane = lax.broadcasted_iota(jnp.int32, (8, LANES), 0)
+    phase = [lax.rem(sublane + shift, EDGE) for shift in range(EDGE)]
+    is_zero = [value == 0 for value in phase]
+    is_one = [value == 1 for value in phase]
+    for start, ref, side in ((0, down_ref, 0), (rows - EDGE, up_ref, 1)):
+        whole = {}
+        for t in range(cells // LANES):
+            for slot in range(SLOTS):
+                lines = []
+                for i in range(EDGE):
+                    here = mine_ref[0, slot, start + i : start + i + 1, lanes_of(t)]
+                    there = other_ref[0, slot, start + i : start + i + 1, lanes_of(t)]
+                    lines.append(jnp.broadcast_to(jnp.where(valid[slot], here, there), (8, LANES)))
+                for shift in range(EDGE):
+                    whole[t, slot, shift] = jnp.where(
+                        is_zero[shift], lines[0], jnp.where(is_one[shift], lines[1], lines[2])
+                    )
+            for row in range(0, total_rows, 8):
+                if (row + 7) // per_tile != t:
+                    continue
+                total = None
+                for slot in range(SLOTS):
+                    field = whole[t, slot, row % EDGE]
+                    if row // per_tile != t:
+                        field = jnp.where(sublane < per_tile * t - row, whole[t - 1, slot, row % EDGE], field)
+                    term = border_ref[slot, side, row : row + 8, :] * field
+                    total = term if total is None else total + term
+                ref[row : row + 8, :] = total
 
 
 def bulk_kernel(
@@ -239,46 +261,56 @@
 
 
 def correct_kernel(
-    taps_x_ref, taps_y_ref, mix_ref, from_left_ref, from_right_ref, correction_ref, rows_of, left, matrix
+    taps_x_ref, taps_y_ref, mix_ref, from_left_ref, from_right_ref, local_ref, gradient_ref,
+    rows_of, left, result, matrix,
 ):
-    members, _, cells = correction_ref.shape
+    members, rows, cells = local_ref.shape
     count = cells // LANES
+    here = EDGE * members
     taps_x = [taps_x_ref[k] for k in range(7)]
     taps_y = [taps_y_ref[k] for k in range(7)]
     build_mix(mix_ref[...], matrix)
     zero = jnp.zeros((8, LANES), F32)
+    for t in range(count):
+        rows_of[0, t, 24:32, :] = zero
+        rows_of[0, t, 32:40, :] = zero
+        rows_of[1, t, 0:8, :] = zero
+        rows_of[1, t, 32:40, :] = zero
+        rows_of[0, t, 0:here, :] = from_left_ref[here * t : here * (t + 1), :]
+        rows_of[1, t, 8 : 8 + here, :] = from_right_ref[here * t : here * (t + 1), :]
+    sublane = lax.broadcasted_iota(jnp.int32, (8, LANES), 0)
+    blocks = []
+    for side in range(2):
+        for row in range(0, 32, 8):
+            place = lax.rem(sublane + row, EDGE)
+            if side == 0:
+                factors = [jnp.where(place < EDGE - d, taps_x[d], 0.0) for d in range(EDGE)]
+            else:
+                factors = [jnp.where(place >= d, taps_x[6 - d], 0.0) for d in range(EDGE)]
+            block = []
+            for t in range(count):
+                total = None
+                for d in range(EDGE):
+                    at = row + d if side == 0 else 8 + row - d
+                    term = factors[d] * rows_of[side, t, at : at + 8, :]
+                    total = term if total is None else total + term
+                block.append(total)
+            blocks.append(columns(block, taps_y))
+            if len(blocks) == 2:
+                store_split(left, 64, 32 * side + row - 8, *blocks)
+                blocks = []
+    group = 4
+    for first in range(0, count, group):
+        result[64 * first : 64 * (first + group), :] = mixed(left, 64 * first, 64 * group, matrix[...])
     for member in range(members):
         for t in range(count):
-            at = EDGE * (members * t + member)
-            for row in range(0, 32, 8):
-                rows_of[member, t, row : row + 8, :] = zero
-            rows_of[member, t, 0:EDGE, :] = from_left_ref[at : at + EDGE, :]
-            rows_of[member, t, 32 - EDGE : 32, :] = from_right_ref[at : at + EDGE, :]
-
-    def pair_step(pair, carry):
-        for half in range(2):
-            member = 2 * pair + half
-            first, last = [], []
-            for t in range(count):
-                total = taps_x[0] * rows_of[member, t, 0:8, :]
-                other = taps_x[6] * rows_of[member, t, 24:32, :]
-                for d in range(1, EDGE):
-                    total += taps_x[d] * rows_of[member, t, d : 8 + d, :]
-                    other += taps_x[6 - d] * rows_of[member, t, 24 - d : 32 - d, :]
-                first.append(total)
-                last.append(other)
-            store_split(left, 32, 16 * half, columns(first, taps_y), columns(last, taps_y))
-        out = mixed(left, 0, 32 * count, matrix[...])
-        for t in range(count):
-            for half in range(2):
-                correction_ref[2 * pair + half, :, lanes_of(t)] = out[32 * t + 16 * half : 32 * t + 16 * half + 16]
-        return carry
-
-    lax.fori_loop(0, members // 2, pair_step, 0)
+            at = 64 * t + EDGE * member
+            gradient_ref[member, 0:EDGE, lanes_of(t)] += result[at : at + EDGE, :]
+            gradient_ref[member, rows - EDGE : rows, lanes_of(t)] += result[at + 32 : at + 32 + EDGE, :]
 
 
 def update_kernel(
-    entries, near_ref, far_ref, control_ref, velocity_ref, local_ref, correction_ref,
+    entries, near_ref, far_ref, control_ref, velocity_ref, gradient_ref,
     new_control_hbm, new_velocity_hbm, new_control, new_velocity, sems,
 ):
     members, rows, cells = control_ref.shape
@@ -288,12 +320,7 @@
     for member in range(members):
         for start in range(0, rows, 8):
             tile = slice(start, start + 8)
-            gradient = local_ref[member, tile]
-            if start == 0:
-                gradient += correction_ref[member, 0:8]
-            if start == rows - 8:
-                gradient += correction_ref[member, 8:16]
-            moved = 0.9 * velocity_ref[member, tile] + scale * gradient
+            moved = 0.9 * velocity_ref[member, tile] + scale * gradient_ref[member, tile]
             new_velocity[member, tile] = moved
             new_control[member, tile] = control_ref[member, tile] - 0.5 * moved
         for which, (src, dst) in enumerate(((new_control, new_control_hbm), (new_velocity, new_velocity_hbm))):
@@ -312,20 +339,22 @@
     owner = slot_owner.reshape(SLOTS)
     swap = [(0, 1), (1, 0)]
     other = lax.ppermute(adjoint_forcing, "member", swap)
-    perturb, mine = pl.pallas_call(
+    edges = EDGE * members * count
+    perturb, mine, border = pl.pallas_call(
         stage_kernel,
         name="stage",
         out_shape=(
             jax.ShapeDtypeStruct(perturb.shape, perturb.dtype),
             jax.ShapeDtypeStruct(adjoint_forcing.shape, F32),
+            jax.ShapeDtypeStruct((SLOTS, 2, edges, LANES), F32),
         ),
         in_specs=[HBM, HBM],
-        out_specs=(VMEM, VMEM),
+        out_specs=(VMEM, VMEM, VMEM),
         scratch_shapes=[pltpu.SemaphoreType.DMA((members + 1,))],
         compiler_params=params(8),
         cost_estimate=cost(0, 8_000_000),
     )(in_hbm(perturb), in_hbm(adjoint_forcing))
-    packed = jax.ShapeDtypeStruct((EDGE * members * count, LANES), F32)
+    packed = jax.ShapeDtypeStruct((edges, LANES), F32)
     up, down = pl.pallas_call(
         border_kernel,
         name="border_product",
@@ -334,7 +363,7 @@
         out_specs=(VMEM, VMEM),
         compiler_params=params(8),
         cost_estimate=cost(4_000_000, 4_000_000),
-    )(owner, perturb, mine, other)
+    )(owner, border, mine, other)
     from_left = lax.ppermute(up, "tile", [(i, i + 1) for i in range(tiles - 1)])
     from_right = lax.ppermute(down, "tile", [(i + 1, i) for i in range(tiles - 1)])
     matrix = pltpu.VMEM((2 * LANES, 2 * LANES), BF16)
@@ -365,20 +394,22 @@
         compiler_params=params(8),
         cost_estimate=cost(200_000, 1_000_000),
     )(square, cross_up, cross_down, from_left, from_right)
-    correction = pl.pallas_call(
+    gradient = pl.pallas_call(
         correct_kernel,
         name="border_correction",
-        out_shape=jax.ShapeDtypeStruct((members, 16, cells), F32),
-        in_specs=[SMEM, SMEM, VMEM, VMEM, VMEM],
+        out_shape=whole,
+        in_specs=[SMEM, SMEM, VMEM, VMEM, VMEM, VMEM],
         out_specs=VMEM,
         scratch_shapes=[
-            pltpu.VMEM((members, count, 32, LANES), F32),
-            pltpu.VMEM((count * 32, 2 * LANES), BF16),
+            pltpu.VMEM((2, count, 40, LANES), F32),
+            pltpu.VMEM((count * 64, 2 * LANES), BF16),
+            pltpu.VMEM((count * 64, LANES), F32),
             matrix,
         ],
+        input_output_aliases={5: 0},
         compiler_params=params(16),
         cost_estimate=cost(2_000_000_000, 2_000_000),
-    )(taps_x, taps_y, vertical_mix, from_left, from_right)
+    )(taps_x, taps_y, vertical_mix, from_left, from_right, local)
     steps = [("member", swap)]
     width = 1
     while width < tiles:
@@ -393,7 +424,7 @@
             functools.partial(update_kernel, float(entries)),
             name="update",
             out_shape=(whole, whole),
-            in_specs=[VMEM] * 6,
+            in_specs=[VMEM] * 5,
             out_specs=(HBM, HBM),
             scratch_shapes=[
                 pltpu.VMEM(control.shape, F32),
@@ -402,7 +433,7 @@
             ],
             compiler_params=params(16),
             cost_estimate=cost(3_000_000, 12_000_000),
-        )(near, far, control, velocity, local, correction)
+        )(near, far, control, velocity, gradient)
     )
 
 

time: 37.7 us -> 36.6 us (0.971)
  Pallas kernels: 17.1 us -> 15.6 us
  waiting for transfers between devices: 4.74 us -> 5.13 us
    pallas_call x1, Pallas kernels: 2.56 us -> 1.27 us  [body(): pl.pallas_call(correct_kernel, name='border_correction', out_shape=whole,...]
  transfers between devices with their start and end apart: 7 -> 7, of which waited for: 4 -> 5; matrix products, arithmetic and copies ran while one was open for 0% -> 0% of each run, Pallas kernels for 37% -> 34%
where the time goes in v3:
time: 36.6 us; the launch traced here: 36.4 us
  Pallas kernels  15.6 us (43%)
  starting transfers between devices  14.9 us (41%)
  waiting for transfers between devices  5.13 us (14%)
  between operations  0.76 us (2%)
    pallas_call x1, Pallas kernels, body(): pl.pallas_call(bulk_kernel, name='bulk', out_shape=(whole, packed, packed...  9.21 us
    ppermute x3, starting transfers between devices, body(): near = near + lax.ppermute(near, axis, pairs)  5.53 us
    ppermute x1, starting transfers between devices, body(): from_left = lax.ppermute(up, 'tile', [(i, i + 1) for i in range(tiles - 1)])  4.53 us
    ppermute x3, waiting for transfers between devices, body(): near = near + lax.ppermute(near, axis, pairs)  4.32 us
    ppermute x1, starting transfers between devices, body(): far = lax.ppermute(near, *steps[-1])  3.04 us
    pallas_call x1, Pallas kernels, body(): pl.pallas_call(functools.partial(update_kernel, float(entries)), name='up...  2.24 us
    pallas_call x1, Pallas kernels, body(): pl.pallas_call(stage_kernel, name='stage', out_shape=(jax.ShapeDtypeStruc...  2.05 us
    ppermute x1, starting transfers between devices, body(): lax.ppermute(down, 'tile', [(i + 1, i) for i in range(tiles - 1)])  1.29 us
  transfers between devices with their start and end apart: 7, of which 5 were waited for; matrix products, arithmetic and copies ran while one was open for 0% of the time, Pallas kernels for 34%

profile of v3, /device:TPU:0, one launch (start us, length us, event | category | flops | bytes accessed | tf_op | source)
XLA Modules:
  0.0 36.4 jit_solution(13493280682635144711)
XLA Ops:
  0.6 0.0 copy-start
  0.6 0.5 %collective-permute-start = (f32[1,3,24,2048]{3,2,1,0:T(8,128)}, f32[1,3,24,2048]{3,2,1,0:T(8,128)S(1)}, u32[]{:S(2)}, u32[]{:S(2)}) collective-permute-start(f32[1,3,24,2048]{3,2,1,0:T(8,128)} %mine_hbm.1), channel_id=1, source_target_pairs={{0,1},{1,0},{2,3},{3,2},{4,5},{5,4},{6,7},{7,6},{8,9},{9,8},{10,11... | collective-permute-start | bytes 1769480 | tf_op jit(solution)/shard_map/ppermute | solution.py:341
  1.2 2.0 %stage.1 = (bf16[10,3,24,2048]{3,2,1,0:T(8,128)(2,1)S(1)}, f32[1,3,24,2048]{3,2,1,0:T(8,128)S(1)}, f32[3,2,480,128]{3,2,1,0:T(8,128)S(1)}) custom-call(bf16[10,3,24,2048]{3,2,1,0:T(8,128)(2,1)} %perturb_hbm.1, f32[1,3,24,2048]{3,2,1,0:T(8,128)} %mine_hbm.1), custom_call_target="tpu_custom_call" | custom-call | bytes 8000000 | tf_op jit(solution)/shard_map/stage/pallas_call | solution.py:343
  3.2 0.0 copy-start.1
  3.2 0.0 copy-start.2
  3.2 0.0 copy-start.3
  3.3 0.0 collective-permute-done.other_ref
  3.3 0.0 copy-done
  3.3 0.8 %border_product.1 = (f32[480,128]{1,0:T(8,128)S(1)}, f32[480,128]{1,0:T(8,128)S(1)}) custom-call(s32[3]{0:T(128)S(1)} %bitcast.1, f32[3,2,480,128]{3,2,1,0:T(8,128)S(1)} %get-tuple-element.18.border_ref, f32[1,3,24,2048]{3,2,1,0:T(8,128)S(1)} %get-tuple-element.14.mine_ref, f32[1,3,24,2048]{3,2,1,0:T(8,128)S(1)} %collective-permute-done.other_ref), custom_call_target="tpu_custom_call" | custom-call | flops 4000000 | bytes 4000000 | tf_op jit(solution)/shard_map/border_product/pallas_call | solution.py:358
  4.1 4.5 %collective-permute-start.1 = (f32[480,128]{1,0:T(8,128)S(1)}, f32[480,128]{1,0:T(8,128)S(1)}, u32[]{:S(2)}, u32[]{:S(2)}) collective-permute-start(f32[480,128]{1,0:T(8,128)S(1)} %get-tuple-element.19), channel_id=1, source_target_pairs={{0,2},{2,4},{4,6},{6,8},{8,10},{10,12},{12,14},{1,3},{3,5},{5,7},{... | collective-permute-start | bytes 737288 | tf_op jit(solution)/shard_map/ppermute | solution.py:367
  8.6 1.3 %collective-permute-start.2 = (f32[480,128]{1,0:T(8,128)S(1)}, f32[480,128]{1,0:T(8,128)S(1)}, u32[]{:S(2)}, u32[]{:S(2)}) collective-permute-start(f32[480,128]{1,0:T(8,128)S(1)} %get-tuple-element.20), channel_id=1, source_target_pairs={{2,0},{4,2},{6,4},{8,6},{10,8},{12,10},{14,12},{3,1},{5,3},{7,5},{... | collective-permute-start | bytes 737288 | tf_op jit(solution)/shard_map/ppermute | solution.py:368
  9.9 0.0 copy-done.1
  9.9 0.0 copy-done.2
  9.9 0.0 copy-done.3
  9.9 9.2 %bulk.1 = (f32[10,24,2048]{2,1,0:T(8,128)S(1)}, f32[480,128]{1,0:T(8,128)S(1)}, f32[480,128]{1,0:T(8,128)S(1)}, f32[8,128]{1,0:T(8,128)S(1)}, f32[10,24,2048]{2,1,0:T(8,128)S(1)}, /*index=5*/f32[10,24,2048]{2,1,0:T(8,128)S(1)}) custom-call(s32[3]{0:T(128)S(1)} %bitcast.2, f32[7]{0:T(128)S(1)} %copy-done.2, f32[7]{0:T(128)S(1)} %copy-done.3, ...), custom_call_target="tpu_custom_call" | custom-call | flops 8999999488 | bytes 12000000 | tf_op jit(solution)/shard_map/bulk/pallas_call | solution.py:371
  19.1 0.5 %collective-permute-done.1.from_left_ref = f32[480,128]{1,0:T(8,128)S(1)} collective-permute-done((f32[480,128]{1,0:T(8,128)S(1)}, f32[480,128]{1,0:T(8,128)S(1)}, u32[]{:S(2)}, u32[]{:S(2)}) %collective-permute-start.1) | collective-permute-done | bytes 245792 | tf_op jit(solution)/shard_map/ppermute | solution.py:367
  19.6 0.0 collective-permute-done.2.from_right_ref
  19.6 0.1 cross_term.1
  19.7 0.1 collective-permute-start.3
  19.8 1.2 %collective-permute-done.3 = f32[8,128]{1,0:T(8,128)S(1)} collective-permute-done((f32[8,128]{1,0:T(8,128)S(1)}, f32[8,128]{1,0:T(8,128)S(1)}, u32[]{:S(2)}, u32[]{:S(2)}) %collective-permute-start.3) | collective-permute-done | bytes 4128 | tf_op jit(solution)/shard_map/ppermute | solution.py:419
  20.9 2.5 %collective-permute-start.4 = (f32[8,128]{1,0:T(8,128)S(1)}, f32[8,128]{1,0:T(8,128)S(1)}, u32[]{:S(2)}, u32[]{:S(2)}) collective-permute-start(f32[8,128]{1,0:T(8,128)S(1)} %add.9), channel_id=1, source_target_pairs={{0,2},{2,0},{4,6},{6,4},{8,10},{10,8},{12,14},{14,12},{1,3},{3,1},... | collective-permute-start | bytes 12296 | tf_op jit(solution)/shard_map/ppermute | solution.py:419
  23.4 1.6 %collective-permute-done.4 = f32[8,128]{1,0:T(8,128)S(1)} collective-permute-done((f32[8,128]{1,0:T(8,128)S(1)}, f32[8,128]{1,0:T(8,128)S(1)}, u32[]{:S(2)}, u32[]{:S(2)}) %collective-permute-start.4) | collective-permute-done | bytes 4128 | tf_op jit(solution)/shard_map/ppermute | solution.py:419
  25.0 3.0 %collective-permute-start.5 = (f32[8,128]{1,0:T(8,128)S(1)}, f32[8,128]{1,0:T(8,128)S(1)}, u32[]{:S(2)}, u32[]{:S(2)}) collective-permute-start(f32[8,128]{1,0:T(8,128)S(1)} %add.10), channel_id=1, source_target_pairs={{0,4},{2,6},{4,0},{6,2},{8,12},{10,14},{12,8},{14,10},{1,5},{3,7},... | collective-permute-start | bytes 12296 | tf_op jit(solution)/shard_map/ppermute | solution.py:419
  28.0 1.6 %collective-permute-done.5 = f32[8,128]{1,0:T(8,128)S(1)} collective-permute-done((f32[8,128]{1,0:T(8,128)S(1)}, f32[8,128]{1,0:T(8,128)S(1)}, u32[]{:S(2)}, u32[]{:S(2)}) %collective-permute-start.5) | collective-permute-done | bytes 4128 | tf_op jit(solution)/shard_map/ppermute | solution.py:419
  29.6 3.0 %collective-permute-start.6 = (f32[8,128]{1,0:T(8,128)S(1)}, f32[8,128]{1,0:T(8,128)S(1)}, u32[]{:S(2)}, u32[]{:S(2)}) collective-permute-start(f32[8,128]{1,0:T(8,128)S(1)} %add.11.near_ref), channel_id=1, source_target_pairs={{0,8},{2,10},{4,12},{6,14},{8,0},{10,2},{12,4},{14,6},{1,9},{3,11}... | collective-permute-start | bytes 12296 | tf_op jit(solution)/shard_map/ppermute | solution.py:420
  32.6 1.3 %border_correction.1.gradient_ref = f32[10,24,2048]{2,1,0:T(8,128)S(1)} custom-call(f32[7]{0:T(128)S(1)} %copy-done.2, f32[7]{0:T(128)S(1)} %copy-done.3, f32[64,64]{1,0:T(8,128)S(1)} %copy-done.1, f32[480,128]{1,0:T(8,128)S(1)} %collective-permute-done.1.from_left_ref, ...), custom_call_target="tpu_custom_call", output_to_operand_aliasing={{}: (5, {})} | custom-call | flops 2000000000 | bytes 2000000 | tf_op jit(solution)/shard_map/border_correction/pallas_call | solution.py:397
  33.9 0.3 collective-permute-done.6.far_ref
  34.2 2.2 %update.1 = (f32[10,24,2048]{2,1,0:T(8,128)}, f32[10,24,2048]{2,1,0:T(8,128)}) custom-call(f32[8,128]{1,0:T(8,128)S(1)} %add.11.near_ref, f32[8,128]{1,0:T(8,128)S(1)} %collective-permute-done.6.far_ref, f32[10,24,2048]{2,1,0:T(8,128)S(1)} %get-tuple-element.21.control_ref, f32[10,24,2048]{2,1,0:T(8,128)S(1)} %get-tuple-element.22.velocity_ref, ...), custom_call_target="tpu_custom_call" | custom-call | flops 3000000 | bytes 12000000 | tf_op jit(solution)/shard_map/update/pallas_call | solution.py:423
  (3 shorter events, 0.0 us)
Async XLA Ops:
  0.6 2.6 %copy-start = (s32[3,1]{0,1:T(1,128)S(1)}, s32[3,1]{0,1:T(1,128)}, u32[]{:S(2)}) copy-start(s32[3,1]{0,1:T(1,128)} %param.12) | copy-start | bytes 40
  0.6 2.6 %collective-permute-start = (f32[1,3,24,2048]{3,2,1,0:T(8,128)}, f32[1,3,24,2048]{3,2,1,0:T(8,128)S(1)}, u32[]{:S(2)}, u32[]{:S(2)}) collective-permute-start(f32[1,3,24,2048]{3,2,1,0:T(8,128)} %mine_hbm.1), channel_id=1, source_target_pairs={{0,1},{1,0},{2,3},{3,2},{4,5},{5,4},{6,7},{7,6},{8,9},{9,8},{10,11... | collective-permute-start | bytes 1769480 | tf_op jit(solution)/shard_map/ppermute | solution.py:341
  3.2 6.7 %copy-start.1 = (f32[64,64]{1,0:T(8,128)S(1)}, f32[64,64]{1,0:T(8,128)}, u32[]{:S(2)}) copy-start(f32[64,64]{1,0:T(8,128)} %mix_ref.3) | copy-start | bytes 49156
  3.2 6.7 %copy-start.2 = (f32[7]{0:T(128)S(1)}, f32[7]{0:T(128)}, u32[]{:S(2)}) copy-start(f32[7]{0:T(128)} %taps_x_ref.3) | copy-start | bytes 88
  3.2 6.7 %copy-start.3 = (f32[7]{0:T(128)S(1)}, f32[7]{0:T(128)}, u32[]{:S(2)}) copy-start(f32[7]{0:T(128)} %taps_y_ref.3) | copy-start | bytes 88
  4.1 15.6 %collective-permute-start.1 = (f32[480,128]{1,0:T(8,128)S(1)}, f32[480,128]{1,0:T(8,128)S(1)}, u32[]{:S(2)}, u32[]{:S(2)}) collective-permute-start(f32[480,128]{1,0:T(8,128)S(1)} %get-tuple-element.19), channel_id=1, source_target_pairs={{0,2},{2,4},{4,6},{6,8},{8,10},{10,12},{12,14},{1,3},{3,5},{5,7},{... | collective-permute-start | bytes 737288 | tf_op jit(solution)/shard_map/ppermute | solution.py:367
  8.6 11.0 %collective-permute-start.2 = (f32[480,128]{1,0:T(8,128)S(1)}, f32[480,128]{1,0:T(8,128)S(1)}, u32[]{:S(2)}, u32[]{:S(2)}) collective-permute-start(f32[480,128]{1,0:T(8,128)S(1)} %get-tuple-element.20), channel_id=1, source_target_pairs={{2,0},{4,2},{6,4},{8,6},{10,8},{12,10},{14,12},{3,1},{5,3},{7,5},{... | collective-permute-start | bytes 737288 | tf_op jit(solution)/shard_map/ppermute | solution.py:368
  19.7 1.2 %collective-permute-start.3 = (f32[8,128]{1,0:T(8,128)S(1)}, f32[8,128]{1,0:T(8,128)S(1)}, u32[]{:S(2)}, u32[]{:S(2)}) collective-permute-start(f32[8,128]{1,0:T(8,128)S(1)} %cross_term.1), channel_id=1, source_target_pairs={{0,1},{1,0},{2,3},{3,2},{4,5},{5,4},{6,7},{7,6},{8,9},{9,8},{10,11... | collective-permute-start | bytes 12296 | tf_op jit(solution)/shard_map/ppermute | solution.py:419
  20.9 4.1 %collective-permute-start.4 = (f32[8,128]{1,0:T(8,128)S(1)}, f32[8,128]{1,0:T(8,128)S(1)}, u32[]{:S(2)}, u32[]{:S(2)}) collective-permute-start(f32[8,128]{1,0:T(8,128)S(1)} %add.9), channel_id=1, source_target_pairs={{0,2},{2,0},{4,6},{6,4},{8,10},{10,8},{12,14},{14,12},{1,3},{3,1},... | collective-permute-start | bytes 12296 | tf_op jit(solution)/shard_map/ppermute | solution.py:419
  25.0 4.6 %collective-permute-start.5 = (f32[8,128]{1,0:T(8,128)S(1)}, f32[8,128]{1,0:T(8,128)S(1)}, u32[]{:S(2)}, u32[]{:S(2)}) collective-permute-start(f32[8,128]{1,0:T(8,128)S(1)} %add.10), channel_id=1, source_target_pairs={{0,4},{2,6},{4,0},{6,2},{8,12},{10,14},{12,8},{14,10},{1,5},{3,7},... | collective-permute-start | bytes 12296 | tf_op jit(solution)/shard_map/ppermute | solution.py:419
  29.6 4.6 %collective-permute-start.6 = (f32[8,128]{1,0:T(8,128)S(1)}, f32[8,128]{1,0:T(8,128)S(1)}, u32[]{:S(2)}, u32[]{:S(2)}) collective-permute-start(f32[8,128]{1,0:T(8,128)S(1)} %add.11.near_ref), channel_id=1, source_target_pairs={{0,8},{2,10},{4,12},{6,14},{8,0},{10,2},{12,4},{14,6},{1,9},{3,11}... | collective-permute-start | bytes 12296 | tf_op jit(solution)/shard_map/ppermute | solution.py:420

commit v4 on v3

--- a/solution.py
+++ b/solution.py
@@ -106,7 +106,17 @@
     copies[members].wait()
 
 
-def border_kernel(owner_ref, border_ref, mine_ref, other_ref, up_ref, down_ref):
+def by_parity(run, first, second):
+    odd = lax.rem(lax.axis_index("tile"), 2) == 1
+    pl.when(jnp.logical_not(odd))(lambda: run(first, second))
+    pl.when(odd)(lambda: run(second, first))
+
+
+def border_kernel(owner_ref, border_ref, mine_ref, other_ref, pair_ref, next_ref):
+    by_parity(functools.partial(border_rows, owner_ref, border_ref, mine_ref, other_ref), pair_ref, next_ref)
+
+
+def border_rows(owner_ref, border_ref, mine_ref, other_ref, up_ref, down_ref):
     _, _, rows, cells = mine_ref.shape
     total_rows = up_ref.shape[0]
     per_tile = total_rows // (cells // LANES)
@@ -144,7 +154,7 @@
 
 def bulk_kernel(
     owner_ref, taps_x_ref, taps_y_ref, mix_ref, perturb_ref, mine_ref, other_ref, control_hbm, velocity_hbm,
-    local_ref, cross_up_ref, cross_down_ref, square_ref, control_ref, velocity_ref,
+    local_ref, cross_pair_ref, cross_next_ref, square_ref, control_ref, velocity_ref,
     field, rows_of, left, turned, matrix, matrix_t, sems,
 ):
     members, _, rows, cells = perturb_ref.shape
@@ -243,25 +253,29 @@
         return carry
 
     lax.fori_loop(0, members // 2, turn_step, 0)
-    for member in range(members):
-        for t in range(count):
-            at = EDGE * (members * t + member)
-            cross_up_ref[at : at + EDGE, :] = turned[member, t, 0:EDGE, :]
-            cross_down_ref[at : at + EDGE, :] = turned[member, t, 16 - EDGE : 16, :]
-
-
-def cross_kernel(square_ref, cross_up_ref, cross_down_ref, from_left_ref, from_right_ref, total_ref):
+
+    def pack(cross_down_ref, cross_up_ref):
+        for member in range(members):
+            for t in range(count):
+                at = EDGE * (members * t + member)
+                cross_up_ref[at : at + EDGE, :] = turned[member, t, 0:EDGE, :]
+                cross_down_ref[at : at + EDGE, :] = turned[member, t, 16 - EDGE : 16, :]
+
+    by_parity(pack, cross_pair_ref, cross_next_ref)
+
+
+def cross_kernel(square_ref, cross_pair_ref, cross_next_ref, from_pair_ref, from_next_ref, total_ref):
     total = [jnp.zeros((8, LANES), F32) for _ in range(4)]
-    for step, row in enumerate(range(0, cross_up_ref.shape[0], 8)):
+    for step, row in enumerate(range(0, cross_pair_ref.shape[0], 8)):
         at = slice(row, row + 8)
         which = 2 * (step % 2)
-        total[which] += cross_up_ref[at] * from_left_ref[at]
-        total[which + 1] += cross_down_ref[at] * from_right_ref[at]
+        total[which] += cross_pair_ref[at] * from_pair_ref[at]
+        total[which + 1] += cross_next_ref[at] * from_next_ref[at]
     total_ref[...] = square_ref[...] + 2.0 * ((total[0] + total[1]) + (total[2] + total[3]))
 
 
 def correct_kernel(
-    taps_x_ref, taps_y_ref, mix_ref, from_left_ref, from_right_ref, local_ref, gradient_ref,
+    taps_x_ref, taps_y_ref, mix_ref, from_pair_ref, from_next_ref, local_ref, gradient_ref,
     rows_of, left, result, matrix,
 ):
     members, rows, cells = local_ref.shape
@@ -276,8 +290,13 @@
         rows_of[0, t, 32:40, :] = zero
         rows_of[1, t, 0:8, :] = zero
         rows_of[1, t, 32:40, :] = zero
-        rows_of[0, t, 0:here, :] = from_left_ref[here * t : here * (t + 1), :]
-        rows_of[1, t, 8 : 8 + here, :] = from_right_ref[here * t : here * (t + 1), :]
+
+    def unpack(from_right_ref, from_left_ref):
+        for t in range(count):
+            rows_of[0, t, 0:here, :] = from_left_ref[here * t : here * (t + 1), :]
+            rows_of[1, t, 8 : 8 + here, :] = from_right_ref[here * t : here * (t + 1), :]
+
+    by_parity(unpack, from_pair_ref, from_next_ref)
     sublane = lax.broadcasted_iota(jnp.int32, (8, LANES), 0)
     blocks = []
     for side in range(2):
@@ -355,7 +374,7 @@
         cost_estimate=cost(0, 8_000_000),
     )(in_hbm(perturb), in_hbm(adjoint_forcing))
     packed = jax.ShapeDtypeStruct((edges, LANES), F32)
-    up, down = pl.pallas_call(
+    pair, after = pl.pallas_call(
         border_kernel,
         name="border_product",
         out_shape=(packed, packed),
@@ -364,11 +383,12 @@
         compiler_params=params(8),
         cost_estimate=cost(4_000_000, 4_000_000),
     )(owner, border, mine, other)
-    from_left = lax.ppermute(up, "tile", [(i, i + 1) for i in range(tiles - 1)])
-    from_right = lax.ppermute(down, "tile", [(i + 1, i) for i in range(tiles - 1)])
+    swaps = [(i, i + 1) for i in range(tiles - 1)] + [(i + 1, i) for i in range(tiles - 1)]
+    from_next = lax.ppermute(after, "tile", [(i, j) for i, j in swaps if min(i, j) % 2 == 1])
+    from_pair = lax.ppermute(pair, "tile", [(i, j) for i, j in swaps if min(i, j) % 2 == 0])
     matrix = pltpu.VMEM((2 * LANES, 2 * LANES), BF16)
     whole = jax.ShapeDtypeStruct(control.shape, F32)
-    local, cross_up, cross_down, square, control, velocity = pl.pallas_call(
+    local, cross_pair, cross_next, square, control, velocity = pl.pallas_call(
         bulk_kernel,
         name="bulk",
         out_shape=(whole, packed, packed, jax.ShapeDtypeStruct((8, LANES), F32), whole, whole),
@@ -393,7 +413,7 @@
         out_specs=VMEM,
         compiler_params=params(8),
         cost_estimate=cost(200_000, 1_000_000),
-    )(square, cross_up, cross_down, from_left, from_right)
+    )(square, cross_pair, cross_next, from_pair, from_next)
     gradient = pl.pallas_call(
         correct_kernel,
         name="border_correction",
@@ -409,7 +429,7 @@
         input_output_aliases={5: 0},
         compiler_params=params(16),
         cost_estimate=cost(2_000_000_000, 2_000_000),
-    )(taps_x, taps_y, vertical_mix, from_left, from_right, local)
+    )(taps_x, taps_y, vertical_mix, from_pair, from_next, local)
     steps = [("member", swap)]
     width = 1
     while width < tiles:

time: 36.6 us -> 34.4 us (0.940)
  starting transfers between devices: 14.9 us -> 11.3 us
  waiting for transfers between devices: 5.13 us -> 6.5 us
    ppermute x2, starting transfers between devices: 5.83 us -> 3.34 us  [the longest x1 2.68 us: body(): lax.ppermute(pair, 'tile', [(i, j) for i, j in swaps if min(i, j) % 2 == 0])]
    ppermute x3, starting transfers between devices: 5.53 us -> 4.8 us  [body(): near = near + lax.ppermute(near, axis, pairs)]
    ppermute x2, waiting for transfers between devices: 0.5 us -> 1.15 us  [the longest x1 1.15 us: body(): lax.ppermute(pair, 'tile', [(i, j) for i, j in swaps if min(i, j) % 2 == 0])]
    ppermute x3, waiting for transfers between devices: 4.32 us -> 4.77 us  [body(): near = near + lax.ppermute(near, axis, pairs)]
    ppermute x1, starting transfers between devices: 3.04 us -> 2.59 us  [body(): far = lax.ppermute(near, *steps[-1])]
  transfers between devices with their start and end apart: 7 -> 7, of which waited for: 5 -> 5; matrix products, arithmetic and copies ran while one was open for 0% -> 0% of each run, Pallas kernels for 34% -> 37%
where the time goes in v4:
time: 34.4 us; the launch traced here: 34.2 us
  Pallas kernels  15.7 us (46%)
  starting transfers between devices  11.3 us (33%)
  waiting for transfers between devices  6.5 us (19%)
  between operations  0.76 us (2%)
    pallas_call x1, Pallas kernels, body(): pl.pallas_call(bulk_kernel, name='bulk', out_shape=(whole, packed, packed...  9.22 us
    ppermute x3, starting transfers between devices, body(): near = near + lax.ppermute(near, axis, pairs)  4.8 us
    ppermute x3, waiting for transfers between devices, body(): near = near + lax.ppermute(near, axis, pairs)  4.77 us
    ppermute x1, starting transfers between devices, body(): lax.ppermute(pair, 'tile', [(i, j) for i, j in swaps if min(i, j) % 2 == 0])  2.68 us
    ppermute x1, starting transfers between devices, body(): far = lax.ppermute(near, *steps[-1])  2.59 us
    pallas_call x1, Pallas kernels, body(): pl.pallas_call(functools.partial(update_kernel, float(entries)), name='up...  2.24 us
    pallas_call x1, Pallas kernels, body(): pl.pallas_call(stage_kernel, name='stage', out_shape=(jax.ShapeDtypeStruc...  2.05 us
    pallas_call x1, Pallas kernels, body(): pl.pallas_call(correct_kernel, name='border_correction', out_shape=whole,...  1.32 us
  transfers between devices with their start and end apart: 7, of which 5 were waited for; matrix products, arithmetic and copies ran while one was open for 0% of the time, Pallas kernels for 37%

profile of v4, /device:TPU:0, one launch (start us, length us, event | category | flops | bytes accessed | tf_op | source)
XLA Modules:
  0.0 34.2 jit_solution(10397628607705299652)
XLA Ops:
  0.6 0.0 copy-start
  0.6 0.5 %collective-permute-start = (f32[1,3,24,2048]{3,2,1,0:T(8,128)}, f32[1,3,24,2048]{3,2,1,0:T(8,128)S(1)}, u32[]{:S(2)}, u32[]{:S(2)}) collective-permute-start(f32[1,3,24,2048]{3,2,1,0:T(8,128)} %mine_hbm.1), channel_id=1, source_target_pairs={{0,1},{1,0},{2,3},{3,2},{4,5},{5,4},{6,7},{7,6},{8,9},{9,8},{10,11... | collective-permute-start | bytes 1769480 | tf_op jit(solution)/shard_map/ppermute | solution.py:360
  1.2 2.0 %stage.1 = (bf16[10,3,24,2048]{3,2,1,0:T(8,128)(2,1)S(1)}, f32[1,3,24,2048]{3,2,1,0:T(8,128)S(1)}, f32[3,2,480,128]{3,2,1,0:T(8,128)S(1)}) custom-call(bf16[10,3,24,2048]{3,2,1,0:T(8,128)(2,1)} %perturb_hbm.1, f32[1,3,24,2048]{3,2,1,0:T(8,128)} %mine_hbm.1), custom_call_target="tpu_custom_call" | custom-call | bytes 8000000 | tf_op jit(solution)/shard_map/stage/pallas_call | solution.py:362
  3.2 0.0 copy-start.1
  3.2 0.0 copy-start.2
  3.2 0.0 copy-start.3
  3.3 0.0 collective-permute-done.other_ref
  3.3 0.0 copy-done
  3.3 0.8 %border_product.1 = (f32[480,128]{1,0:T(8,128)S(1)}, f32[480,128]{1,0:T(8,128)S(1)}) custom-call(s32[3]{0:T(128)S(1)} %bitcast.1, f32[3,2,480,128]{3,2,1,0:T(8,128)S(1)} %get-tuple-element.18.border_ref, f32[1,3,24,2048]{3,2,1,0:T(8,128)S(1)} %get-tuple-element.14.mine_ref, f32[1,3,24,2048]{3,2,1,0:T(8,128)S(1)} %collective-permute-done.other_ref), custom_call_target="tpu_custom_call" | custom-call | flops 4000000 | bytes 4000000 | tf_op jit(solution)/shard_map/border_product/pallas_call | solution.py:377
  4.1 2.7 %collective-permute-start.1 = (f32[480,128]{1,0:T(8,128)S(1)}, f32[480,128]{1,0:T(8,128)S(1)}, u32[]{:S(2)}, u32[]{:S(2)}) collective-permute-start(f32[480,128]{1,0:T(8,128)S(1)} %get-tuple-element.19), channel_id=1, source_target_pairs={{0,2},{4,6},{8,10},{12,14},{2,0},{6,4},{10,8},{14,12},{1,3},{5,7},... | collective-permute-start | bytes 737288 | tf_op jit(solution)/shard_map/ppermute | solution.py:388
  6.7 0.7 %collective-permute-start.2 = (f32[480,128]{1,0:T(8,128)S(1)}, f32[480,128]{1,0:T(8,128)S(1)}, u32[]{:S(2)}, u32[]{:S(2)}) collective-permute-start(f32[480,128]{1,0:T(8,128)S(1)} %get-tuple-element.20), channel_id=1, source_target_pairs={{2,4},{6,8},{10,12},{4,2},{8,6},{12,10},{3,5},{7,9},{11,13},{5,3},... | collective-permute-start | bytes 737288 | tf_op jit(solution)/shard_map/ppermute | solution.py:387
  7.4 0.0 copy-done.1
  7.4 0.0 copy-done.2
  7.4 0.0 copy-done.3
  7.5 9.2 %bulk.1 = (f32[10,24,2048]{2,1,0:T(8,128)S(1)}, f32[480,128]{1,0:T(8,128)S(1)}, f32[480,128]{1,0:T(8,128)S(1)}, f32[8,128]{1,0:T(8,128)S(1)}, f32[10,24,2048]{2,1,0:T(8,128)S(1)}, /*index=5*/f32[10,24,2048]{2,1,0:T(8,128)S(1)}) custom-call(s32[3]{0:T(128)S(1)} %bitcast.2, f32[7]{0:T(128)S(1)} %copy-done.2, f32[7]{0:T(128)S(1)} %copy-done.3, ...), custom_call_target="tpu_custom_call" | custom-call | flops 8999999488 | bytes 12000000 | tf_op jit(solution)/shard_map/bulk/pallas_call | solution.py:391
  16.7 1.1 %collective-permute-done.1.from_pair_ref = f32[480,128]{1,0:T(8,128)S(1)} collective-permute-done((f32[480,128]{1,0:T(8,128)S(1)}, f32[480,128]{1,0:T(8,128)S(1)}, u32[]{:S(2)}, u32[]{:S(2)}) %collective-permute-start.1) | collective-permute-done | bytes 245792 | tf_op jit(solution)/shard_map/ppermute | solution.py:388
  17.8 0.0 collective-permute-done.2.from_next_ref
  17.8 0.1 cross_term.1
  17.9 0.1 collective-permute-start.3
  18.0 1.2 %collective-permute-done.3 = f32[8,128]{1,0:T(8,128)S(1)} collective-permute-done((f32[8,128]{1,0:T(8,128)S(1)}, f32[8,128]{1,0:T(8,128)S(1)}, u32[]{:S(2)}, u32[]{:S(2)}) %collective-permute-start.3) | collective-permute-done | bytes 4128 | tf_op jit(solution)/shard_map/ppermute | solution.py:439
  19.1 3.2 %collective-permute-start.4 = (f32[8,128]{1,0:T(8,128)S(1)}, f32[8,128]{1,0:T(8,128)S(1)}, u32[]{:S(2)}, u32[]{:S(2)}) collective-permute-start(f32[8,128]{1,0:T(8,128)S(1)} %add.9), channel_id=1, source_target_pairs={{0,2},{2,0},{4,6},{6,4},{8,10},{10,8},{12,14},{14,12},{1,3},{3,1},... | collective-permute-start | bytes 12296 | tf_op jit(solution)/shard_map/ppermute | solution.py:439
  22.3 1.6 %collective-permute-done.4 = f32[8,128]{1,0:T(8,128)S(1)} collective-permute-done((f32[8,128]{1,0:T(8,128)S(1)}, f32[8,128]{1,0:T(8,128)S(1)}, u32[]{:S(2)}, u32[]{:S(2)}) %collective-permute-start.4) | collective-permute-done | bytes 4128 | tf_op jit(solution)/shard_map/ppermute | solution.py:439
  23.9 1.6 %collective-permute-start.5 = (f32[8,128]{1,0:T(8,128)S(1)}, f32[8,128]{1,0:T(8,128)S(1)}, u32[]{:S(2)}, u32[]{:S(2)}) collective-permute-start(f32[8,128]{1,0:T(8,128)S(1)} %add.10), channel_id=1, source_target_pairs={{0,4},{2,6},{4,0},{6,2},{8,12},{10,14},{12,8},{14,10},{1,5},{3,7},... | collective-permute-start | bytes 12296 | tf_op jit(solution)/shard_map/ppermute | solution.py:439
  25.4 2.0 %collective-permute-done.5 = f32[8,128]{1,0:T(8,128)S(1)} collective-permute-done((f32[8,128]{1,0:T(8,128)S(1)}, f32[8,128]{1,0:T(8,128)S(1)}, u32[]{:S(2)}, u32[]{:S(2)}) %collective-permute-start.5) | collective-permute-done | bytes 4128 | tf_op jit(solution)/shard_map/ppermute | solution.py:439
  27.5 2.6 %collective-permute-start.6 = (f32[8,128]{1,0:T(8,128)S(1)}, f32[8,128]{1,0:T(8,128)S(1)}, u32[]{:S(2)}, u32[]{:S(2)}) collective-permute-start(f32[8,128]{1,0:T(8,128)S(1)} %add.11.near_ref), channel_id=1, source_target_pairs={{0,8},{2,10},{4,12},{6,14},{8,0},{10,2},{12,4},{14,6},{1,9},{3,11}... | collective-permute-start | bytes 12296 | tf_op jit(solution)/shard_map/ppermute | solution.py:440
  30.1 1.3 %border_correction.1.gradient_ref = f32[10,24,2048]{2,1,0:T(8,128)S(1)} custom-call(f32[7]{0:T(128)S(1)} %copy-done.2, f32[7]{0:T(128)S(1)} %copy-done.3, f32[64,64]{1,0:T(8,128)S(1)} %copy-done.1, f32[480,128]{1,0:T(8,128)S(1)} %collective-permute-done.1.from_pair_ref, ...), custom_call_target="tpu_custom_call", output_to_operand_aliasing={{}: (5, {})} | custom-call | flops 2000000000 | bytes 2000000 | tf_op jit(solution)/shard_map/border_correction/pallas_call | solution.py:417
  31.4 0.6 %collective-permute-done.6.far_ref = f32[8,128]{1,0:T(8,128)S(1)} collective-permute-done((f32[8,128]{1,0:T(8,128)S(1)}, f32[8,128]{1,0:T(8,128)S(1)}, u32[]{:S(2)}, u32[]{:S(2)}) %collective-permute-start.6) | collective-permute-done | bytes 4128 | tf_op jit(solution)/shard_map/ppermute | solution.py:440
  32.0 2.2 %update.1 = (f32[10,24,2048]{2,1,0:T(8,128)}, f32[10,24,2048]{2,1,0:T(8,128)}) custom-call(f32[8,128]{1,0:T(8,128)S(1)} %add.11.near_ref, f32[8,128]{1,0:T(8,128)S(1)} %collective-permute-done.6.far_ref, f32[10,24,2048]{2,1,0:T(8,128)S(1)} %get-tuple-element.21.control_ref, f32[10,24,2048]{2,1,0:T(8,128)S(1)} %get-tuple-element.22.velocity_ref, ...), custom_call_target="tpu_custom_call" | custom-call | flops 3000000 | bytes 12000000 | tf_op jit(solution)/shard_map/update/pallas_call | solution.py:443
  (3 shorter events, 0.0 us)
Async XLA Ops:
  0.6 2.6 %copy-start = (s32[3,1]{0,1:T(1,128)S(1)}, s32[3,1]{0,1:T(1,128)}, u32[]{:S(2)}) copy-start(s32[3,1]{0,1:T(1,128)} %param.12) | copy-start | bytes 40
  0.6 2.6 %collective-permute-start = (f32[1,3,24,2048]{3,2,1,0:T(8,128)}, f32[1,3,24,2048]{3,2,1,0:T(8,128)S(1)}, u32[]{:S(2)}, u32[]{:S(2)}) collective-permute-start(f32[1,3,24,2048]{3,2,1,0:T(8,128)} %mine_hbm.1), channel_id=1, source_target_pairs={{0,1},{1,0},{2,3},{3,2},{4,5},{5,4},{6,7},{7,6},{8,9},{9,8},{10,11... | collective-permute-start | bytes 1769480 | tf_op jit(solution)/shard_map/ppermute | solution.py:360
  3.2 4.2 %copy-start.1 = (f32[64,64]{1,0:T(8,128)S(1)}, f32[64,64]{1,0:T(8,128)}, u32[]{:S(2)}) copy-start(f32[64,64]{1,0:T(8,128)} %mix_ref.3) | copy-start | bytes 49156
  3.2 4.2 %copy-start.2 = (f32[7]{0:T(128)S(1)}, f32[7]{0:T(128)}, u32[]{:S(2)}) copy-start(f32[7]{0:T(128)} %taps_x_ref.3) | copy-start | bytes 88
  3.2 4.2 %copy-start.3 = (f32[7]{0:T(128)S(1)}, f32[7]{0:T(128)}, u32[]{:S(2)}) copy-start(f32[7]{0:T(128)} %taps_y_ref.3) | copy-start | bytes 88
  4.1 13.8 %collective-permute-start.1 = (f32[480,128]{1,0:T(8,128)S(1)}, f32[480,128]{1,0:T(8,128)S(1)}, u32[]{:S(2)}, u32[]{:S(2)}) collective-permute-start(f32[480,128]{1,0:T(8,128)S(1)} %get-tuple-element.19), channel_id=1, source_target_pairs={{0,2},{4,6},{8,10},{12,14},{2,0},{6,4},{10,8},{14,12},{1,3},{5,7},... | collective-permute-start | bytes 737288 | tf_op jit(solution)/shard_map/ppermute | solution.py:388
  6.7 11.1 %collective-permute-start.2 = (f32[480,128]{1,0:T(8,128)S(1)}, f32[480,128]{1,0:T(8,128)S(1)}, u32[]{:S(2)}, u32[]{:S(2)}) collective-permute-start(f32[480,128]{1,0:T(8,128)S(1)} %get-tuple-element.20), channel_id=1, source_target_pairs={{2,4},{6,8},{10,12},{4,2},{8,6},{12,10},{3,5},{7,9},{11,13},{5,3},... | collective-permute-start | bytes 737288 | tf_op jit(solution)/shard_map/ppermute | solution.py:387
  17.9 1.2 %collective-permute-start.3 = (f32[8,128]{1,0:T(8,128)S(1)}, f32[8,128]{1,0:T(8,128)S(1)}, u32[]{:S(2)}, u32[]{:S(2)}) collective-permute-start(f32[8,128]{1,0:T(8,128)S(1)} %cross_term.1), channel_id=1, source_target_pairs={{0,1},{1,0},{2,3},{3,2},{4,5},{5,4},{6,7},{7,6},{8,9},{9,8},{10,11... | collective-permute-start | bytes 12296 | tf_op jit(solution)/shard_map/ppermute | solution.py:439
  19.1 4.7 %collective-permute-start.4 = (f32[8,128]{1,0:T(8,128)S(1)}, f32[8,128]{1,0:T(8,128)S(1)}, u32[]{:S(2)}, u32[]{:S(2)}) collective-permute-start(f32[8,128]{1,0:T(8,128)S(1)} %add.9), channel_id=1, source_target_pairs={{0,2},{2,0},{4,6},{6,4},{8,10},{10,8},{12,14},{14,12},{1,3},{3,1},... | collective-permute-start | bytes 12296 | tf_op jit(solution)/shard_map/ppermute | solution.py:439
  23.9 3.6 %collective-permute-start.5 = (f32[8,128]{1,0:T(8,128)S(1)}, f32[8,128]{1,0:T(8,128)S(1)}, u32[]{:S(2)}, u32[]{:S(2)}) collective-permute-start(f32[8,128]{1,0:T(8,128)S(1)} %add.10), channel_id=1, source_target_pairs={{0,4},{2,6},{4,0},{6,2},{8,12},{10,14},{12,8},{14,10},{1,5},{3,7},... | collective-permute-start | bytes 12296 | tf_op jit(solution)/shard_map/ppermute | solution.py:439
  27.5 4.5 %collective-permute-start.6 = (f32[8,128]{1,0:T(8,128)S(1)}, f32[8,128]{1,0:T(8,128)S(1)}, u32[]{:S(2)}, u32[]{:S(2)}) collective-permute-start(f32[8,128]{1,0:T(8,128)S(1)} %add.11.near_ref), channel_id=1, source_target_pairs={{0,8},{2,10},{4,12},{6,14},{8,0},{10,2},{12,4},{14,6},{1,9},{3,11}... | collective-permute-start | bytes 12296 | tf_op jit(solution)/shard_map/ppermute | solution.py:440

commit v5 on v4

--- a/solution.py
+++ b/solution.py
@@ -87,14 +87,57 @@
     return slice(LANES * t, LANES * (t + 1))
 
 
-def stage_kernel(perturb_hbm, mine_hbm, perturb_ref, mine_ref, border_ref, sems):
+def border_levels(rows_of, count, plain, lead, taps_y, left, matrix, result):
+    sublane = lax.broadcasted_iota(jnp.int32, (8, LANES), 0)
+    blocks = []
+    for side in range(2):
+        for row in range(0, 32, 8):
+            place = lax.rem(sublane + row, EDGE)
+            if side == 0:
+                factors = [jnp.where(place < EDGE - d, plain[d], 0.0) for d in range(EDGE)]
+            else:
+                factors = [jnp.where(place >= d, lead[d], 0.0) for d in range(EDGE)]
+            block = []
+            for t in range(count):
+                total = None
+                for d in range(EDGE):
+                    at = row + d if side == 0 else 8 + row - d
+                    term = factors[d] * rows_of[side, t, at : at + 8, :]
+                    total = term if total is None else total + term
+                block.append(total)
+            blocks.append(columns(block, taps_y))
+            if len(blocks) == 2:
+                store_split(left, 64, 32 * side + row - 8, *blocks)
+                blocks = []
+    group = 4
+    for first in range(0, count, group):
+        result[64 * first : 64 * (first + group), :] = mixed(left, 64 * first, 64 * group, matrix)
+
+
+def clear_packed(rows_of, count):
+    zero = jnp.zeros((8, LANES), F32)
+    for t in range(count):
+        rows_of[0, t, 24:32, :] = zero
+        rows_of[0, t, 32:40, :] = zero
+        rows_of[1, t, 0:8, :] = zero
+        rows_of[1, t, 32:40, :] = zero
+
+
+def stage_kernel(
+    perturb_hbm, mine_hbm, mix_hbm, perturb_ref, mine_ref, border_ref, matrix_ref, matrix_t_ref, mix, sems
+):
     members, _, rows, cells = perturb_ref.shape
+    mix_copy = pltpu.make_async_copy(mix_hbm, mix, sems.at[members + 1])
+    mix_copy.start()
     copies = []
     for member in range(members):
         copies.append(pltpu.make_async_copy(perturb_hbm.at[member], perturb_ref.at[member], sems.at[member]))
     copies.append(pltpu.make_async_copy(mine_hbm, mine_ref, sems.at[members]))
     for copy in copies:
         copy.start()
+    mix_copy.wait()
+    build_mix(mix[...], matrix_ref)
+    build_mix(mix[...].T, matrix_t_ref)
     for member in range(members):
         copies[member].wait()
         for slot in range(SLOTS):
@@ -153,13 +196,14 @@
 
 
 def bulk_kernel(
-    owner_ref, taps_x_ref, taps_y_ref, mix_ref, perturb_ref, mine_ref, other_ref, control_hbm, velocity_hbm,
+    owner_ref, taps_x_ref, taps_y_ref, matrix, matrix_t, perturb_ref, mine_ref, other_ref, pair_ref, next_ref,
+    control_hbm, velocity_hbm,
     local_ref, cross_pair_ref, cross_next_ref, square_ref, control_ref, velocity_ref,
-    field, rows_of, left, turned, matrix, matrix_t, sems,
+    field, rows_of, packed, left, result, sems,
 ):
     members, _, rows, cells = perturb_ref.shape
     count = cells // LANES
-    tall = rows + 16
+    here = EDGE * members
     control_copy = pltpu.make_async_copy(control_hbm, control_ref, sems.at[0])
     velocity_copy = pltpu.make_async_copy(velocity_hbm, velocity_ref, sems.at[1])
     control_copy.start()
@@ -169,15 +213,30 @@
     tiles = lax.axis_size("tile")
     taps_x = [taps_x_ref[k] for k in range(7)]
     taps_y = [taps_y_ref[k] for k in range(7)]
-    build_mix(mix_ref[...], matrix)
-    build_mix(mix_ref[...].T, matrix_t)
+    first_taps, last_taps = taps_x[0:EDGE], taps_x[6 : 6 - EDGE : -1]
     for slot in range(SLOTS):
         field[slot] = jnp.where(owner_ref[slot] == me, mine_ref[0, slot], other_ref[0, slot])
     for half in range(2):
         rows_of[half, :, 0:8, :] = jnp.zeros((count, 8, LANES), F32)
-        rows_of[half, :, tall - 8 : tall, :] = jnp.zeros((count, 8, LANES), F32)
-    weight_top = jnp.where(tile > 0, 1.0, 0.0).astype(F32)
-    weight_bottom = jnp.where(tile < tiles - 1, 1.0, 0.0).astype(F32)
+        rows_of[half, :, rows + 8 : rows + 16, :] = jnp.zeros((count, 8, LANES), F32)
+    clear_packed(packed, count)
+
+    def unpack(up_ref, down_ref):
+        for t in range(count):
+            packed[0, t, 0:here, :] = up_ref[here * t : here * (t + 1), :]
+            packed[1, t, 8 : 8 + here, :] = down_ref[here * t : here * (t + 1), :]
+
+    by_parity(unpack, pair_ref, next_ref)
+    border_levels(packed, count, first_taps, last_taps, taps_y, left, matrix[...], result)
+    weights = [jnp.where(tile < tiles - 1, 1.0, 0.0).astype(F32), jnp.where(tile > 0, 1.0, 0.0).astype(F32)]
+    squares = jnp.zeros((8, LANES), F32)
+    for side in range(2):
+        total = [jnp.zeros((8, LANES), F32) for _ in range(4)]
+        for t in range(count):
+            for step in range(4):
+                value = result[64 * t + 32 * side + 8 * step : 64 * t + 32 * side + 8 * step + 8, :]
+                total[step] += value * value
+        squares += weights[side] * ((total[0] + total[1]) + (total[2] + total[3]))
 
     def pair_step(pair, carry):
         for half in range(2):
@@ -188,78 +247,45 @@
                     product += perturb_ref[member, slot, :, lanes_of(t)].astype(F32) * field[slot, :, lanes_of(t)]
                 rows_of[half, t, 8 : 8 + rows, :] = product
         blocks = []
+        size = 2 * rows
         for half in range(2):
-            for row in range(0, tall, 8):
-                used = range(7)
-                if row == 0:
-                    used = range(4, 7)
-                if row == tall - 8:
-                    used = range(0, 3)
+            for row in range(0, rows, 8):
                 block = []
                 for t in range(count):
                     total = None
-                    for k in used:
-                        term = taps_x[k] * rows_of[half, t, row + k - 3 : row + k + 5, :]
+                    for k in range(7):
+                        term = taps_x[k] * rows_of[half, t, row + k + 5 : row + k + 13, :]
                         total = term if total is None else total + term
                     block.append(total)
                 blocks.append(columns(block, taps_y))
                 if len(blocks) == 2:
-                    at = half * tall + row - 8
-                    store_split(left, 2 * tall, at, *blocks)
+                    store_split(left, size, half * rows + row - 8, *blocks)
                     blocks = []
         pl.when(pair == 0)(control_copy.wait)
         group = 4
         for first in range(0, count, group):
-            size = 2 * tall
             out = mixed(left, size * first, size * group, matrix[...])
             for t in range(first, first + group):
                 for half in range(2):
                     member = 2 * pair + half
-                    base = size * (t - first) + tall * half
-                    here = control_ref[member, :, lanes_of(t)] + out[base + 8 : base + 8 + rows]
-                    local_ref[member, :, lanes_of(t)] = here
-                    squared = here * here
+                    base = size * (t - first) + rows * half
+                    value = control_ref[member, :, lanes_of(t)] + out[base : base + rows]
+                    local_ref[member, :, lanes_of(t)] = value
+                    squared = value * value
                     for row in range(0, rows, 8):
                         carry += squared[row : row + 8]
-                    above, below = out[base : base + 8], out[base + tall - 8 : base + tall]
-                    carry += weight_top * (above * above) + weight_bottom * (below * below)
+                    packed[0, t, pl.ds(EDGE * member, EDGE), :] = value[rows - EDGE : rows]
+                    packed[1, t, pl.ds(8 + EDGE * member, EDGE), :] = value[0:EDGE]
         return carry
 
-    square_ref[...] = lax.fori_loop(0, members // 2, pair_step, jnp.zeros((8, LANES), F32))
+    square_ref[...] = lax.fori_loop(0, members // 2, pair_step, squares)
     velocity_copy.wait()
-    back = taps_y[::-1]
-
-    def turn_step(pair, carry):
-        for half in range(2):
-            member = 2 * pair + half
-            for t in range(count):
-                rows_of[half, t, 8:16, :] = local_ref[member, 0:8, lanes_of(t)]
-                rows_of[half, t, rows : rows + 8, :] = local_ref[member, rows - 8 : rows, lanes_of(t)]
-        for half in range(2):
-            first, last = [], []
-            for t in range(count):
-                total = taps_x[0] * rows_of[half, t, 8:16, :]
-                other = taps_x[6] * rows_of[half, t, rows : rows + 8, :]
-                for d in range(1, EDGE):
-                    total += taps_x[d] * rows_of[half, t, 8 - d : 16 - d, :]
-                    other += taps_x[6 - d] * rows_of[half, t, rows + d : rows + 8 + d, :]
-                first.append(total)
-                last.append(other)
-            store_split(left, 32, 16 * half, columns(first, back), columns(last, back))
-        out = mixed(left, 0, 32 * count, matrix_t[...])
+    border_levels(packed, count, last_taps, first_taps, taps_y[::-1], left, matrix_t[...], result)
+
+    def pack(cross_down_ref, cross_up_ref):
         for t in range(count):
-            for half in range(2):
-                turned[2 * pair + half, t] = out[32 * t + 16 * half : 32 * t + 16 * half + 16]
-        return carry
-
-    lax.fori_loop(0, members // 2, turn_step, 0)
-
-    def pack(cross_down_ref, cross_up_ref):
-        for member in range(members):
-            for t in range(count):
-                at = EDGE * (members * t + member)
-                cross_up_ref[at : at + EDGE, :] = turned[member, t, 0:EDGE, :]
-                cross_down_ref[at : at + EDGE, :] = turned[member, t, 16 - EDGE : 16, :]
+            cross_down_ref[here * t : here * (t + 1), :] = result[64 * t : 64 * t + here, :]
+            cross_up_ref[here * t : here * (t + 1), :] = result[64 * t + 32 : 64 * t + 32 + here, :]
 
     by_parity(pack, cross_pair_ref, cross_next_ref)
 
@@ -275,52 +301,24 @@
 
 
 def correct_kernel(
-    taps_x_ref, taps_y_ref, mix_ref, from_pair_ref, from_next_ref, local_ref, gradient_ref,
-    rows_of, left, result, matrix,
+    taps_x_ref, taps_y_ref, matrix, from_pair_ref, from_next_ref, local_ref, gradient_ref, packed, left, result
 ):
     members, rows, cells = local_ref.shape
     count = cells // LANES
     here = EDGE * members
     taps_x = [taps_x_ref[k] for k in range(7)]
     taps_y = [taps_y_ref[k] for k in range(7)]
-    build_mix(mix_ref[...], matrix)
-    zero = jnp.zeros((8, LANES), F32)
-    for t in range(count):
-        rows_of[0, t, 24:32, :] = zero
-        rows_of[0, t, 32:40, :] = zero
-        rows_of[1, t, 0:8, :] = zero
-        rows_of[1, t, 32:40, :] = zero
+    clear_packed(packed, count)
 
     def unpack(from_right_ref, from_left_ref):
         for t in range(count):
-            rows_of[0, t, 0:here, :] = from_left_ref[here * t : here * (t + 1), :]
-            rows_of[1, t, 8 : 8 + here, :] = from_right_ref[here * t : here * (t + 1), :]
+            packed[0, t, 0:here, :] = from_left_ref[here * t : here * (t + 1), :]
+            packed[1, t, 8 : 8 + here, :] = from_right_ref[here * t : here * (t + 1), :]
 
     by_parity(unpack, from_pair_ref, from_next_ref)
-    sublane = lax.broadcasted_iota(jnp.int32, (8, LANES), 0)
-    blocks = []
-    for side in range(2):
-        for row in range(0, 32, 8):
-            place = lax.rem(sublane + row, EDGE)
-            if side == 0:
-                factors = [jnp.where(place < EDGE - d, taps_x[d], 0.0) for d in range(EDGE)]
-            else:
-                factors = [jnp.where(place >= d, taps_x[6 - d], 0.0) for d in range(EDGE)]
-            block = []
-            for t in range(count):
-                total = None
-                for d in range(EDGE):
-                    at = row + d if side == 0 else 8 + row - d
-                    term = factors[d] * rows_of[side, t, at : at + 8, :]
-                    total = term if total is None else total + term
-                block.append(total)
-            blocks.append(columns(block, taps_y))
-            if len(blocks) == 2:
-                store_split(left, 64, 32 * side + row - 8, *blocks)
-                blocks = []
-    group = 4
-    for first in range(0, count, group):
-        result[64 * first : 64 * (first + group), :] = mixed(left, 64 * first, 64 * group, matrix[...])
+    border_levels(
+        packed, count, taps_x[0:EDGE], taps_x[6 : 6 - EDGE : -1], taps_y, left, matrix[...], result
+    )
     for member in range(members):
         for t in range(count):
             at = 64 * t + EDGE * member
@@ -359,20 +357,23 @@
     swap = [(0, 1), (1, 0)]
     other = lax.ppermute(adjoint_forcing, "member", swap)
     edges = EDGE * members * count
-    perturb, mine, border = pl.pallas_call(
+    square_matrix = (2 * LANES, 2 * LANES)
+    perturb, mine, border, matrix, matrix_t = pl.pallas_call(
         stage_kernel,
         name="stage",
         out_shape=(
             jax.ShapeDtypeStruct(perturb.shape, perturb.dtype),
             jax.ShapeDtypeStruct(adjoint_forcing.shape, F32),
             jax.ShapeDtypeStruct((SLOTS, 2, edges, LANES), F32),
+            jax.ShapeDtypeStruct(square_matrix, BF16),
+            jax.ShapeDtypeStruct(square_matrix, BF16),
         ),
-        in_specs=[HBM, HBM],
-        out_specs=(VMEM, VMEM, VMEM),
-        scratch_shapes=[pltpu.SemaphoreType.DMA((members + 1,))],
+        in_specs=[HBM, HBM, HBM],
+        out_specs=(VMEM,) * 5,
+        scratch_shapes=[pltpu.VMEM(vertical_mix.shape, F32), pltpu.SemaphoreType.DMA((members + 2,))],
         compiler_params=params(8),
         cost_estimate=cost(0, 8_000_000),
-    )(in_hbm(perturb), in_hbm(adjoint_forcing))
+    )(in_hbm(perturb), in_hbm(adjoint_forcing), in_hbm(vertical_mix))
     packed = jax.ShapeDtypeStruct((edges, LANES), F32)
     pair, after = pl.pallas_call(
         border_kernel,
@@ -386,25 +387,30 @@
     swaps = [(i, i + 1) for i in range(tiles - 1)] + [(i + 1, i) for i in range(tiles - 1)]
     from_next = lax.ppermute(after, "tile", [(i, j) for i, j in swaps if min(i, j) % 2 == 1])
     from_pair = lax.ppermute(pair, "tile", [(i, j) for i, j in swaps if min(i, j) % 2 == 0])
-    matrix = pltpu.VMEM((2 * LANES, 2 * LANES), BF16)
+    border_scratch = [
+        pltpu.VMEM((2, count, 40, LANES), F32),
+        pltpu.VMEM((count * 64, 2 * LANES), BF16),
+        pltpu.VMEM((count * 64, LANES), F32),
+    ]
     whole = jax.ShapeDtypeStruct(control.shape, F32)
     local, cross_pair, cross_next, square, control, velocity = pl.pallas_call(
         bulk_kernel,
         name="bulk",
         out_shape=(whole, packed, packed, jax.ShapeDtypeStruct((8, LANES), F32), whole, whole),
-        in_specs=[SMEM, SMEM, SMEM, VMEM, VMEM, VMEM, VMEM, HBM, HBM],
+        in_specs=[SMEM, SMEM, SMEM] + [VMEM] * 7 + [HBM, HBM],
         out_specs=(VMEM,) * 6,
         scratch_shapes=[
             pltpu.VMEM((SLOTS, rows, cells), F32),
             pltpu.VMEM((2, count, rows + 16, LANES), F32),
-            pltpu.VMEM((count * 2 * (rows + 16), 2 * LANES), BF16),
-            pltpu.VMEM((members, count, 16, LANES), F32),
-            matrix, matrix,
+            *border_scratch,
             pltpu.SemaphoreType.DMA((2,)),
         ],
         compiler_params=params(24),
         cost_estimate=cost(9_000_000_000, 12_000_000),
-    )(owner, taps_x, taps_y, vertical_mix, perturb, mine, other, in_hbm(control), in_hbm(velocity))
+    )(
+        owner, taps_x, taps_y, matrix, matrix_t, perturb, mine, other, pair, after,
+        in_hbm(control), in_hbm(velocity),
+    )
     near = pl.pallas_call(
         cross_kernel,
         name="cross_term",
@@ -420,16 +426,11 @@
         out_shape=whole,
         in_specs=[SMEM, SMEM, VMEM, VMEM, VMEM, VMEM],
         out_specs=VMEM,
-        scratch_shapes=[
-            pltpu.VMEM((2, count, 40, LANES), F32),
-            pltpu.VMEM((count * 64, 2 * LANES), BF16),
-            pltpu.VMEM((count * 64, LANES), F32),
-            matrix,
-        ],
+        scratch_shapes=border_scratch,
         input_output_aliases={5: 0},
         compiler_params=params(16),
         cost_estimate=cost(2_000_000_000, 2_000_000),
-    )(taps_x, taps_y, vertical_mix, from_pair, from_next, local)
+    )(taps_x, taps_y, matrix, from_pair, from_next, local)
     steps = [("member", swap)]
     width = 1
     while width < tiles:

time: 34.4 us -> 33.9 us (0.985)
  Pallas kernels: 15.7 us -> 13 us
  waiting for transfers between devices: 6.5 us -> 8.41 us
    ppermute x1, waiting for transfers between devices: 1.15 us -> 3.8 us  [body(): lax.ppermute(pair, 'tile', [(i, j) for i, j in swaps if min(i, j) % 2 == 0])]
    pallas_call x1, Pallas kernels: 9.22 us -> 6.58 us  [body(): pl.pallas_call(bulk_kernel, name='bulk', out_shape=(whole, packed, packed...]
    ppermute x3, waiting for transfers between devices: 4.77 us -> 4.32 us  [body(): near = near + lax.ppermute(near, axis, pairs)]
    ppermute x1, starting transfers between devices: 2.59 us -> 3.04 us  [body(): far = lax.ppermute(near, *steps[-1])]
  transfers between devices with their start and end apart: 7 -> 7, of which waited for: 5 -> 5; matrix products, arithmetic and copies ran while one was open for 0% -> 0% of each run, Pallas kernels for 37% -> 30%
where the time goes in v5:
time: 33.9 us; the launch traced here: 33.7 us
  Pallas kernels  13 us (38%)
  starting transfers between devices  11.5 us (34%)
  waiting for transfers between devices  8.41 us (25%)
  between operations  0.74 us (2%)
    pallas_call x1, Pallas kernels, body(): pl.pallas_call(bulk_kernel, name='bulk', out_shape=(whole, packed, packed...  6.58 us
    ppermute x3, starting transfers between devices, body(): near = near + lax.ppermute(near, axis, pairs)  4.63 us
    ppermute x3, waiting for transfers between devices, body(): near = near + lax.ppermute(near, axis, pairs)  4.32 us
    ppermute x1, waiting for transfers between devices, body(): lax.ppermute(pair, 'tile', [(i, j) for i, j in swaps if min(i, j) % 2 == 0])  3.8 us
    ppermute x1, starting transfers between devices, body(): far = lax.ppermute(near, *steps[-1])  3.04 us
    ppermute x1, starting transfers between devices, body(): lax.ppermute(pair, 'tile', [(i, j) for i, j in swaps if min(i, j) % 2 == 0])  2.67 us
    pallas_call x1, Pallas kernels, body(): pl.pallas_call(functools.partial(update_kernel, float(entries)), name='up...  2.24 us
    pallas_call x1, Pallas kernels, body(): pl.pallas_call(stage_kernel, name='stage', out_shape=(jax.ShapeDtypeStruc...  2.07 us
  transfers between devices with their start and end apart: 7, of which 5 were waited for; matrix products, arithmetic and copies ran while one was open for 0% of the time, Pallas kernels for 30%

profile of v5, /device:TPU:0, one launch (start us, length us, event | category | flops | bytes accessed | tf_op | source)
XLA Modules:
  0.0 33.7 jit_solution(10894789944827090439)
XLA Ops:
  0.6 0.0 copy-start
  0.6 0.5 %collective-permute-start = (f32[1,3,24,2048]{3,2,1,0:T(8,128)}, f32[1,3,24,2048]{3,2,1,0:T(8,128)S(1)}, u32[]{:S(2)}, u32[]{:S(2)}) collective-permute-start(f32[1,3,24,2048]{3,2,1,0:T(8,128)} %mine_hbm.1), channel_id=1, source_target_pairs={{0,1},{1,0},{2,3},{3,2},{4,5},{5,4},{6,7},{7,6},{8,9},{9,8},{10,11... | collective-permute-start | bytes 1769480 | tf_op jit(solution)/shard_map/ppermute | solution.py:358
  1.2 2.1 %stage.1 = (bf16[10,3,24,2048]{3,2,1,0:T(8,128)(2,1)S(1)}, f32[1,3,24,2048]{3,2,1,0:T(8,128)S(1)}, f32[3,2,480,128]{3,2,1,0:T(8,128)S(1)}, bf16[256,256]{1,0:T(8,128)(2,1)S(1)}, bf16[256,256]{1,0:T(8,128)(2,1)S(1)}) custom-call(bf16[10,3,24,2048]{3,2,1,0:T(8,128)(2,1)} %perturb_hbm.1, f32[1,3,24,2048]{3,2,1,0:T(8,128)} %mine_hbm.1, f32[64,64]{1,0:T(8,128)} %mix_hbm.1), custom_call_target="tpu_custom_call" | custom-call | bytes 8000000 | tf_op jit(solution)/shard_map/stage/pallas_call | solution.py:361
  3.2 0.0 copy-start.1
  3.3 0.0 copy-start.2
  3.3 0.0 collective-permute-done.other_ref
  3.3 0.0 copy-done
  3.3 0.8 %border_product.1 = (f32[480,128]{1,0:T(8,128)S(1)}, f32[480,128]{1,0:T(8,128)S(1)}) custom-call(s32[3]{0:T(128)S(1)} %bitcast.1, f32[3,2,480,128]{3,2,1,0:T(8,128)S(1)} %get-tuple-element.19.border_ref, f32[1,3,24,2048]{3,2,1,0:T(8,128)S(1)} %get-tuple-element.18.mine_ref, f32[1,3,24,2048]{3,2,1,0:T(8,128)S(1)} %collective-permute-done.other_ref), custom_call_target="tpu_custom_call" | custom-call | flops 4000000 | bytes 4000000 | tf_op jit(solution)/shard_map/border_product/pallas_call | solution.py:378
  4.1 2.7 %collective-permute-start.1 = (f32[480,128]{1,0:T(8,128)S(1)}, f32[480,128]{1,0:T(8,128)S(1)}, u32[]{:S(2)}, u32[]{:S(2)}) collective-permute-start(f32[480,128]{1,0:T(8,128)S(1)} %get-tuple-element.20.pair_ref), channel_id=1, source_target_pairs={{0,2},{4,6},{8,10},{12,14},{2,0},{6,4},{10,8},{14,12},{1,3},{5,7},... | collective-permute-start | bytes 737288 | tf_op jit(solution)/shard_map/ppermute | solution.py:389
  6.7 0.7 %collective-permute-start.2 = (f32[480,128]{1,0:T(8,128)S(1)}, f32[480,128]{1,0:T(8,128)S(1)}, u32[]{:S(2)}, u32[]{:S(2)}) collective-permute-start(f32[480,128]{1,0:T(8,128)S(1)} %get-tuple-element.21.next_ref), channel_id=1, source_target_pairs={{2,4},{6,8},{10,12},{4,2},{8,6},{12,10},{3,5},{7,9},{11,13},{5,3},... | collective-permute-start | bytes 737288 | tf_op jit(solution)/shard_map/ppermute | solution.py:388
  7.4 0.0 copy-done.1
  7.4 0.0 copy-done.2
  7.4 6.6 %bulk.1 = (f32[10,24,2048]{2,1,0:T(8,128)S(1)}, f32[480,128]{1,0:T(8,128)S(1)}, f32[480,128]{1,0:T(8,128)S(1)}, f32[8,128]{1,0:T(8,128)S(1)}, f32[10,24,2048]{2,1,0:T(8,128)S(1)}, /*index=5*/f32[10,24,2048]{2,1,0:T(8,128)S(1)}) custom-call(s32[3]{0:T(128)S(1)} %bitcast.2, f32[7]{0:T(128)S(1)} %copy-done.1, f32[7]{0:T(128)S(1)} %copy-done.2, ...), custom_call_target="tpu_custom_call" | custom-call | flops 8999999488 | bytes 12000000 | tf_op jit(solution)/shard_map/bulk/pallas_call | solution.py:396
  14.0 3.8 %collective-permute-done.1.from_pair_ref = f32[480,128]{1,0:T(8,128)S(1)} collective-permute-done((f32[480,128]{1,0:T(8,128)S(1)}, f32[480,128]{1,0:T(8,128)S(1)}, u32[]{:S(2)}, u32[]{:S(2)}) %collective-permute-start.1) | collective-permute-done | bytes 245792 | tf_op jit(solution)/shard_map/ppermute | solution.py:389
  17.8 0.0 collective-permute-done.2.from_next_ref
  17.8 0.1 cross_term.1
  17.9 0.1 collective-permute-start.3
  18.0 1.2 %collective-permute-done.3 = f32[8,128]{1,0:T(8,128)S(1)} collective-permute-done((f32[8,128]{1,0:T(8,128)S(1)}, f32[8,128]{1,0:T(8,128)S(1)}, u32[]{:S(2)}, u32[]{:S(2)}) %collective-permute-start.3) | collective-permute-done | bytes 4128 | tf_op jit(solution)/shard_map/ppermute | solution.py:440
  19.1 2.5 %collective-permute-start.4 = (f32[8,128]{1,0:T(8,128)S(1)}, f32[8,128]{1,0:T(8,128)S(1)}, u32[]{:S(2)}, u32[]{:S(2)}) collective-permute-start(f32[8,128]{1,0:T(8,128)S(1)} %add.9), channel_id=1, source_target_pairs={{0,2},{2,0},{4,6},{6,4},{8,10},{10,8},{12,14},{14,12},{1,3},{3,1},... | collective-permute-start | bytes 12296 | tf_op jit(solution)/shard_map/ppermute | solution.py:440
  21.6 1.6 %collective-permute-done.4 = f32[8,128]{1,0:T(8,128)S(1)} collective-permute-done((f32[8,128]{1,0:T(8,128)S(1)}, f32[8,128]{1,0:T(8,128)S(1)}, u32[]{:S(2)}, u32[]{:S(2)}) %collective-permute-start.4) | collective-permute-done | bytes 4128 | tf_op jit(solution)/shard_map/ppermute | solution.py:440
  23.2 2.1 %collective-permute-start.5 = (f32[8,128]{1,0:T(8,128)S(1)}, f32[8,128]{1,0:T(8,128)S(1)}, u32[]{:S(2)}, u32[]{:S(2)}) collective-permute-start(f32[8,128]{1,0:T(8,128)S(1)} %add.10), channel_id=1, source_target_pairs={{0,4},{2,6},{4,0},{6,2},{8,12},{10,14},{12,8},{14,10},{1,5},{3,7},... | collective-permute-start | bytes 12296 | tf_op jit(solution)/shard_map/ppermute | solution.py:440
  25.3 1.6 %collective-permute-done.5 = f32[8,128]{1,0:T(8,128)S(1)} collective-permute-done((f32[8,128]{1,0:T(8,128)S(1)}, f32[8,128]{1,0:T(8,128)S(1)}, u32[]{:S(2)}, u32[]{:S(2)}) %collective-permute-start.5) | collective-permute-done | bytes 4128 | tf_op jit(solution)/shard_map/ppermute | solution.py:440
  26.9 3.0 %collective-permute-start.6 = (f32[8,128]{1,0:T(8,128)S(1)}, f32[8,128]{1,0:T(8,128)S(1)}, u32[]{:S(2)}, u32[]{:S(2)}) collective-permute-start(f32[8,128]{1,0:T(8,128)S(1)} %add.11.near_ref), channel_id=1, source_target_pairs={{0,8},{2,10},{4,12},{6,14},{8,0},{10,2},{12,4},{14,6},{1,9},{3,11}... | collective-permute-start | bytes 12296 | tf_op jit(solution)/shard_map/ppermute | solution.py:441
  29.9 1.3 %border_correction.1.gradient_ref = f32[10,24,2048]{2,1,0:T(8,128)S(1)} custom-call(f32[7]{0:T(128)S(1)} %copy-done.1, f32[7]{0:T(128)S(1)} %copy-done.2, bf16[256,256]{1,0:T(8,128)(2,1)S(1)} %get-tuple-element.15.matrix, f32[480,128]{1,0:T(8,128)S(1)} %collective-permute-done.1.from_pair_ref, ...), custom_call_target="tpu_custom_call", output_to_operand_aliasing={{}: (5, {})} | custom-call | flops 2000000000 | bytes 2000000 | tf_op jit(solution)/shard_map/border_correction/pallas_call | solution.py:423
  31.2 0.3 collective-permute-done.6.far_ref
  31.5 2.2 %update.1 = (f32[10,24,2048]{2,1,0:T(8,128)}, f32[10,24,2048]{2,1,0:T(8,128)}) custom-call(f32[8,128]{1,0:T(8,128)S(1)} %add.11.near_ref, f32[8,128]{1,0:T(8,128)S(1)} %collective-permute-done.6.far_ref, f32[10,24,2048]{2,1,0:T(8,128)S(1)} %get-tuple-element.25.control_ref, f32[10,24,2048]{2,1,0:T(8,128)S(1)} %get-tuple-element.26.velocity_ref, ...), custom_call_target="tpu_custom_call" | custom-call | flops 3000000 | bytes 12000000 | tf_op jit(solution)/shard_map/update/pallas_call | solution.py:444
  (3 shorter events, 0.0 us)
Async XLA Ops:
  0.6 2.6 %copy-start = (s32[3,1]{0,1:T(1,128)S(1)}, s32[3,1]{0,1:T(1,128)}, u32[]{:S(2)}) copy-start(s32[3,1]{0,1:T(1,128)} %param.12) | copy-start | bytes 40
  0.6 2.6 %collective-permute-start = (f32[1,3,24,2048]{3,2,1,0:T(8,128)}, f32[1,3,24,2048]{3,2,1,0:T(8,128)S(1)}, u32[]{:S(2)}, u32[]{:S(2)}) collective-permute-start(f32[1,3,24,2048]{3,2,1,0:T(8,128)} %mine_hbm.1), channel_id=1, source_target_pairs={{0,1},{1,0},{2,3},{3,2},{4,5},{5,4},{6,7},{7,6},{8,9},{9,8},{10,11... | collective-permute-start | bytes 1769480 | tf_op jit(solution)/shard_map/ppermute | solution.py:358
  3.2 4.2 %copy-start.1 = (f32[7]{0:T(128)S(1)}, f32[7]{0:T(128)}, u32[]{:S(2)}) copy-start(f32[7]{0:T(128)} %taps_x_ref.3) | copy-start | bytes 88
  3.3 4.2 %copy-start.2 = (f32[7]{0:T(128)S(1)}, f32[7]{0:T(128)}, u32[]{:S(2)}) copy-start(f32[7]{0:T(128)} %taps_y_ref.3) | copy-start | bytes 88
  4.1 13.7 %collective-permute-start.1 = (f32[480,128]{1,0:T(8,128)S(1)}, f32[480,128]{1,0:T(8,128)S(1)}, u32[]{:S(2)}, u32[]{:S(2)}) collective-permute-start(f32[480,128]{1,0:T(8,128)S(1)} %get-tuple-element.20.pair_ref), channel_id=1, source_target_pairs={{0,2},{4,6},{8,10},{12,14},{2,0},{6,4},{10,8},{14,12},{1,3},{5,7},... | collective-permute-start | bytes 737288 | tf_op jit(solution)/shard_map/ppermute | solution.py:389
  6.7 11.1 %collective-permute-start.2 = (f32[480,128]{1,0:T(8,128)S(1)}, f32[480,128]{1,0:T(8,128)S(1)}, u32[]{:S(2)}, u32[]{:S(2)}) collective-permute-start(f32[480,128]{1,0:T(8,128)S(1)} %get-tuple-element.21.next_ref), channel_id=1, source_target_pairs={{2,4},{6,8},{10,12},{4,2},{8,6},{12,10},{3,5},{7,9},{11,13},{5,3},... | collective-permute-start | bytes 737288 | tf_op jit(solution)/shard_map/ppermute | solution.py:388
  17.9 1.2 %collective-permute-start.3 = (f32[8,128]{1,0:T(8,128)S(1)}, f32[8,128]{1,0:T(8,128)S(1)}, u32[]{:S(2)}, u32[]{:S(2)}) collective-permute-start(f32[8,128]{1,0:T(8,128)S(1)} %cross_term.1), channel_id=1, source_target_pairs={{0,1},{1,0},{2,3},{3,2},{4,5},{5,4},{6,7},{7,6},{8,9},{9,8},{10,11... | collective-permute-start | bytes 12296 | tf_op jit(solution)/shard_map/ppermute | solution.py:440
  19.1 4.1 %collective-permute-start.4 = (f32[8,128]{1,0:T(8,128)S(1)}, f32[8,128]{1,0:T(8,128)S(1)}, u32[]{:S(2)}, u32[]{:S(2)}) collective-permute-start(f32[8,128]{1,0:T(8,128)S(1)} %add.9), channel_id=1, source_target_pairs={{0,2},{2,0},{4,6},{6,4},{8,10},{10,8},{12,14},{14,12},{1,3},{3,1},... | collective-permute-start | bytes 12296 | tf_op jit(solution)/shard_map/ppermute | solution.py:440
  23.2 3.7 %collective-permute-start.5 = (f32[8,128]{1,0:T(8,128)S(1)}, f32[8,128]{1,0:T(8,128)S(1)}, u32[]{:S(2)}, u32[]{:S(2)}) collective-permute-start(f32[8,128]{1,0:T(8,128)S(1)} %add.10), channel_id=1, source_target_pairs={{0,4},{2,6},{4,0},{6,2},{8,12},{10,14},{12,8},{14,10},{1,5},{3,7},... | collective-permute-start | bytes 12296 | tf_op jit(solution)/shard_map/ppermute | solution.py:440
  26.9 4.6 %collective-permute-start.6 = (f32[8,128]{1,0:T(8,128)S(1)}, f32[8,128]{1,0:T(8,128)S(1)}, u32[]{:S(2)}, u32[]{:S(2)}) collective-permute-start(f32[8,128]{1,0:T(8,128)S(1)} %add.11.near_ref), channel_id=1, source_target_pairs={{0,8},{2,10},{4,12},{6,14},{8,0},{10,2},{12,4},{14,6},{1,9},{3,11}... | collective-permute-start | bytes 12296 | tf_op jit(solution)/shard_map/ppermute | solution.py:441

commit v6 on v5

--- a/solution.py
+++ b/solution.py
@@ -431,14 +431,15 @@
         compiler_params=params(16),
         cost_estimate=cost(2_000_000_000, 2_000_000),
     )(taps_x, taps_y, matrix, from_pair, from_next, local)
-    steps = [("member", swap)]
+    near = near + lax.ppermute(near, "member", swap)
+    steps = []
     width = 1
     while width < tiles:
-        steps.append(("tile", [(i, i ^ width) for i in range(tiles)]))
+        steps.append([(groups * i + g, groups * (i ^ width) + groups - 1 - g) for i in range(tiles) for g in range(groups)])
         width *= 2
-    for axis, pairs in steps[:-1]:
-        near = near + lax.ppermute(near, axis, pairs)
-    far = lax.ppermute(near, *steps[-1])
+    for pairs in steps[:-1]:
+        near = near + lax.ppermute(near, ("tile", "member"), pairs)
+    far = lax.ppermute(near, ("tile", "member"), steps[-1])
     entries = members * groups * rows * tiles * cells
     return tuple(
         pl.pallas_call(

time: 33.9 us -> 32.2 us (0.950)
  starting transfers between devices: 11.5 us -> 10.7 us
  waiting for transfers between devices: 8.41 us -> 7.65 us
    ppermute x4, starting transfers between devices: 7.67 us -> 6.8 us  [the longest x2 4.01 us: body(): near = near + lax.ppermute(near, ('tile', 'member'), pairs)]
    ppermute x4, waiting for transfers between devices: 4.61 us -> 3.84 us  [the longest x2 2.66 us: body(): near = near + lax.ppermute(near, ('tile', 'member'), pairs)]
  transfers between devices with their start and end apart: 7 -> 7, of which waited for: 5 -> 4; matrix products, arithmetic and copies ran while one was open for 0% -> 0% of each run, Pallas kernels for 30% -> 31%
where the time goes in v6:
time: 32.2 us; the launch traced here: 32.1 us
  Pallas kernels  13 us (40%)
  starting transfers between devices  10.7 us (33%)
  waiting for transfers between devices  7.65 us (24%)
  between operations  0.74 us (2%)
    pallas_call x1, Pallas kernels, body(): pl.pallas_call(bulk_kernel, name='bulk', out_shape=(whole, packed, packed...  6.58 us
    ppermute x2, starting transfers between devices, body(): near = near + lax.ppermute(near, ('tile', 'member'), pairs)  4.01 us
    ppermute x1, waiting for transfers between devices, body(): lax.ppermute(pair, 'tile', [(i, j) for i, j in swaps if min(i, j) % 2 == 0])  3.8 us
    ppermute x1, starting transfers between devices, body(): far = lax.ppermute(near, ('tile', 'member'), steps[-1])  2.72 us
    ppermute x1, starting transfers between devices, body(): lax.ppermute(pair, 'tile', [(i, j) for i, j in swaps if min(i, j) % 2 == 0])  2.67 us
    ppermute x2, waiting for transfers between devices, body(): near = near + lax.ppermute(near, ('tile', 'member'), pairs)  2.66 us
    pallas_call x1, Pallas kernels, body(): pl.pallas_call(functools.partial(update_kernel, float(entries)), name='up...  2.24 us
    pallas_call x1, Pallas kernels, body(): pl.pallas_call(stage_kernel, name='stage', out_shape=(jax.ShapeDtypeStruc...  2.07 us
  transfers between devices with their start and end apart: 7, of which 4 were waited for; matrix products, arithmetic and copies ran while one was open for 0% of the time, Pallas kernels for 31%

profile of v6, /device:TPU:0, one launch (start us, length us, event | category | flops | bytes accessed | tf_op | source)
XLA Modules:
  0.0 32.1 jit_solution(16372219726700591853)
XLA Ops:
  0.6 0.0 copy-start
  0.6 0.5 %collective-permute-start = (f32[1,3,24,2048]{3,2,1,0:T(8,128)}, f32[1,3,24,2048]{3,2,1,0:T(8,128)S(1)}, u32[]{:S(2)}, u32[]{:S(2)}) collective-permute-start(f32[1,3,24,2048]{3,2,1,0:T(8,128)} %mine_hbm.1), channel_id=1, source_target_pairs={{0,1},{1,0},{2,3},{3,2},{4,5},{5,4},{6,7},{7,6},{8,9},{9,8},{10,11... | collective-permute-start | bytes 1769480 | tf_op jit(solution)/shard_map/ppermute | solution.py:358
  1.2 2.1 %stage.1 = (bf16[10,3,24,2048]{3,2,1,0:T(8,128)(2,1)S(1)}, f32[1,3,24,2048]{3,2,1,0:T(8,128)S(1)}, f32[3,2,480,128]{3,2,1,0:T(8,128)S(1)}, bf16[256,256]{1,0:T(8,128)(2,1)S(1)}, bf16[256,256]{1,0:T(8,128)(2,1)S(1)}) custom-call(bf16[10,3,24,2048]{3,2,1,0:T(8,128)(2,1)} %perturb_hbm.1, f32[1,3,24,2048]{3,2,1,0:T(8,128)} %mine_hbm.1, f32[64,64]{1,0:T(8,128)} %mix_hbm.1), custom_call_target="tpu_custom_call" | custom-call | bytes 8000000 | tf_op jit(solution)/shard_map/stage/pallas_call | solution.py:361
  3.2 0.0 copy-start.1
  3.3 0.0 copy-start.2
  3.3 0.0 collective-permute-done.other_ref
  3.3 0.0 copy-done
  3.3 0.8 %border_product.1 = (f32[480,128]{1,0:T(8,128)S(1)}, f32[480,128]{1,0:T(8,128)S(1)}) custom-call(s32[3]{0:T(128)S(1)} %bitcast.1, f32[3,2,480,128]{3,2,1,0:T(8,128)S(1)} %get-tuple-element.19.border_ref, f32[1,3,24,2048]{3,2,1,0:T(8,128)S(1)} %get-tuple-element.18.mine_ref, f32[1,3,24,2048]{3,2,1,0:T(8,128)S(1)} %collective-permute-done.other_ref), custom_call_target="tpu_custom_call" | custom-call | flops 4000000 | bytes 4000000 | tf_op jit(solution)/shard_map/border_product/pallas_call | solution.py:378
  4.1 2.7 %collective-permute-start.1 = (f32[480,128]{1,0:T(8,128)S(1)}, f32[480,128]{1,0:T(8,128)S(1)}, u32[]{:S(2)}, u32[]{:S(2)}) collective-permute-start(f32[480,128]{1,0:T(8,128)S(1)} %get-tuple-element.20.pair_ref), channel_id=1, source_target_pairs={{0,2},{4,6},{8,10},{12,14},{2,0},{6,4},{10,8},{14,12},{1,3},{5,7},... | collective-permute-start | bytes 737288 | tf_op jit(solution)/shard_map/ppermute | solution.py:389
  6.7 0.7 %collective-permute-start.2 = (f32[480,128]{1,0:T(8,128)S(1)}, f32[480,128]{1,0:T(8,128)S(1)}, u32[]{:S(2)}, u32[]{:S(2)}) collective-permute-start(f32[480,128]{1,0:T(8,128)S(1)} %get-tuple-element.21.next_ref), channel_id=1, source_target_pairs={{2,4},{6,8},{10,12},{4,2},{8,6},{12,10},{3,5},{7,9},{11,13},{5,3},... | collective-permute-start | bytes 737288 | tf_op jit(solution)/shard_map/ppermute | solution.py:388
  7.4 0.0 copy-done.1
  7.4 0.0 copy-done.2
  7.4 6.6 %bulk.1 = (f32[10,24,2048]{2,1,0:T(8,128)S(1)}, f32[480,128]{1,0:T(8,128)S(1)}, f32[480,128]{1,0:T(8,128)S(1)}, f32[8,128]{1,0:T(8,128)S(1)}, f32[10,24,2048]{2,1,0:T(8,128)S(1)}, /*index=5*/f32[10,24,2048]{2,1,0:T(8,128)S(1)}) custom-call(s32[3]{0:T(128)S(1)} %bitcast.2, f32[7]{0:T(128)S(1)} %copy-done.1, f32[7]{0:T(128)S(1)} %copy-done.2, ...), custom_call_target="tpu_custom_call" | custom-call | flops 8999999488 | bytes 12000000 | tf_op jit(solution)/shard_map/bulk/pallas_call | solution.py:396
  14.0 3.8 %collective-permute-done.1.from_pair_ref = f32[480,128]{1,0:T(8,128)S(1)} collective-permute-done((f32[480,128]{1,0:T(8,128)S(1)}, f32[480,128]{1,0:T(8,128)S(1)}, u32[]{:S(2)}, u32[]{:S(2)}) %collective-permute-start.1) | collective-permute-done | bytes 245792 | tf_op jit(solution)/shard_map/ppermute | solution.py:389
  17.8 0.0 collective-permute-done.2.from_next_ref
  17.8 0.1 cross_term.1
  17.9 0.1 collective-permute-start.3
  18.0 1.2 %collective-permute-done.3 = f32[8,128]{1,0:T(8,128)S(1)} collective-permute-done((f32[8,128]{1,0:T(8,128)S(1)}, f32[8,128]{1,0:T(8,128)S(1)}, u32[]{:S(2)}, u32[]{:S(2)}) %collective-permute-start.3) | collective-permute-done | bytes 4128 | tf_op jit(solution)/shard_map/ppermute | solution.py:434
  19.1 2.3 %collective-permute-start.4 = (f32[8,128]{1,0:T(8,128)S(1)}, f32[8,128]{1,0:T(8,128)S(1)}, u32[]{:S(2)}, u32[]{:S(2)}) collective-permute-start(f32[8,128]{1,0:T(8,128)S(1)} %add.9), channel_id=1, source_target_pairs={{0,3},{1,2},{2,1},{3,0},{4,7},{5,6},{6,5},{7,4},{8,11},{9,10},{10,... | collective-permute-start | bytes 12296 | tf_op jit(solution)/shard_map/ppermute | solution.py:441
  21.4 1.3 %collective-permute-done.4 = f32[8,128]{1,0:T(8,128)S(1)} collective-permute-done((f32[8,128]{1,0:T(8,128)S(1)}, f32[8,128]{1,0:T(8,128)S(1)}, u32[]{:S(2)}, u32[]{:S(2)}) %collective-permute-start.4) | collective-permute-done | bytes 4128 | tf_op jit(solution)/shard_map/ppermute | solution.py:441
  22.7 1.8 %collective-permute-start.5 = (f32[8,128]{1,0:T(8,128)S(1)}, f32[8,128]{1,0:T(8,128)S(1)}, u32[]{:S(2)}, u32[]{:S(2)}) collective-permute-start(f32[8,128]{1,0:T(8,128)S(1)} %add.10), channel_id=1, source_target_pairs={{0,5},{1,4},{2,7},{3,6},{4,1},{5,0},{6,3},{7,2},{8,13},{9,12},{10,... | collective-permute-start | bytes 12296 | tf_op jit(solution)/shard_map/ppermute | solution.py:441
  24.5 1.3 %collective-permute-done.5 = f32[8,128]{1,0:T(8,128)S(1)} collective-permute-done((f32[8,128]{1,0:T(8,128)S(1)}, f32[8,128]{1,0:T(8,128)S(1)}, u32[]{:S(2)}, u32[]{:S(2)}) %collective-permute-start.5) | collective-permute-done | bytes 4128 | tf_op jit(solution)/shard_map/ppermute | solution.py:441
  25.8 2.7 %collective-permute-start.6 = (f32[8,128]{1,0:T(8,128)S(1)}, f32[8,128]{1,0:T(8,128)S(1)}, u32[]{:S(2)}, u32[]{:S(2)}) collective-permute-start(f32[8,128]{1,0:T(8,128)S(1)} %add.11.near_ref), channel_id=1, source_target_pairs={{0,9},{1,8},{2,11},{3,10},{4,13},{5,12},{6,15},{7,14},{8,1},{9,0},... | collective-permute-start | bytes 12296 | tf_op jit(solution)/shard_map/ppermute | solution.py:442
  28.5 1.3 %border_correction.1.gradient_ref = f32[10,24,2048]{2,1,0:T(8,128)S(1)} custom-call(f32[7]{0:T(128)S(1)} %copy-done.1, f32[7]{0:T(128)S(1)} %copy-done.2, bf16[256,256]{1,0:T(8,128)(2,1)S(1)} %get-tuple-element.15.matrix, f32[480,128]{1,0:T(8,128)S(1)} %collective-permute-done.1.from_pair_ref, ...), custom_call_target="tpu_custom_call", output_to_operand_aliasing={{}: (5, {})} | custom-call | flops 2000000000 | bytes 2000000 | tf_op jit(solution)/shard_map/border_correction/pallas_call | solution.py:423
  29.8 0.0 collective-permute-done.6.far_ref
  29.8 2.2 %update.1 = (f32[10,24,2048]{2,1,0:T(8,128)}, f32[10,24,2048]{2,1,0:T(8,128)}) custom-call(f32[8,128]{1,0:T(8,128)S(1)} %add.11.near_ref, f32[8,128]{1,0:T(8,128)S(1)} %collective-permute-done.6.far_ref, f32[10,24,2048]{2,1,0:T(8,128)S(1)} %get-tuple-element.25.control_ref, f32[10,24,2048]{2,1,0:T(8,128)S(1)} %get-tuple-element.26.velocity_ref, ...), custom_call_target="tpu_custom_call" | custom-call | flops 3000000 | bytes 12000000 | tf_op jit(solution)/shard_map/update/pallas_call | solution.py:445
  (3 shorter events, 0.0 us)
Async XLA Ops:
  0.6 2.6 %copy-start = (s32[3,1]{0,1:T(1,128)S(1)}, s32[3,1]{0,1:T(1,128)}, u32[]{:S(2)}) copy-start(s32[3,1]{0,1:T(1,128)} %param.12) | copy-start | bytes 40
  0.6 2.6 %collective-permute-start = (f32[1,3,24,2048]{3,2,1,0:T(8,128)}, f32[1,3,24,2048]{3,2,1,0:T(8,128)S(1)}, u32[]{:S(2)}, u32[]{:S(2)}) collective-permute-start(f32[1,3,24,2048]{3,2,1,0:T(8,128)} %mine_hbm.1), channel_id=1, source_target_pairs={{0,1},{1,0},{2,3},{3,2},{4,5},{5,4},{6,7},{7,6},{8,9},{9,8},{10,11... | collective-permute-start | bytes 1769480 | tf_op jit(solution)/shard_map/ppermute | solution.py:358
  3.2 4.2 %copy-start.1 = (f32[7]{0:T(128)S(1)}, f32[7]{0:T(128)}, u32[]{:S(2)}) copy-start(f32[7]{0:T(128)} %taps_x_ref.3) | copy-start | bytes 88
  3.3 4.2 %copy-start.2 = (f32[7]{0:T(128)S(1)}, f32[7]{0:T(128)}, u32[]{:S(2)}) copy-start(f32[7]{0:T(128)} %taps_y_ref.3) | copy-start | bytes 88
  4.1 13.7 %collective-permute-start.1 = (f32[480,128]{1,0:T(8,128)S(1)}, f32[480,128]{1,0:T(8,128)S(1)}, u32[]{:S(2)}, u32[]{:S(2)}) collective-permute-start(f32[480,128]{1,0:T(8,128)S(1)} %get-tuple-element.20.pair_ref), channel_id=1, source_target_pairs={{0,2},{4,6},{8,10},{12,14},{2,0},{6,4},{10,8},{14,12},{1,3},{5,7},... | collective-permute-start | bytes 737288 | tf_op jit(solution)/shard_map/ppermute | solution.py:389
  6.7 11.1 %collective-permute-start.2 = (f32[480,128]{1,0:T(8,128)S(1)}, f32[480,128]{1,0:T(8,128)S(1)}, u32[]{:S(2)}, u32[]{:S(2)}) collective-permute-start(f32[480,128]{1,0:T(8,128)S(1)} %get-tuple-element.21.next_ref), channel_id=1, source_target_pairs={{2,4},{6,8},{10,12},{4,2},{8,6},{12,10},{3,5},{7,9},{11,13},{5,3},... | collective-permute-start | bytes 737288 | tf_op jit(solution)/shard_map/ppermute | solution.py:388
  17.9 1.2 %collective-permute-start.3 = (f32[8,128]{1,0:T(8,128)S(1)}, f32[8,128]{1,0:T(8,128)S(1)}, u32[]{:S(2)}, u32[]{:S(2)}) collective-permute-start(f32[8,128]{1,0:T(8,128)S(1)} %cross_term.1), channel_id=1, source_target_pairs={{0,1},{1,0},{2,3},{3,2},{4,5},{5,4},{6,7},{7,6},{8,9},{9,8},{10,11... | collective-permute-start | bytes 12296 | tf_op jit(solution)/shard_map/ppermute | solution.py:434
  19.1 3.6 %collective-permute-start.4 = (f32[8,128]{1,0:T(8,128)S(1)}, f32[8,128]{1,0:T(8,128)S(1)}, u32[]{:S(2)}, u32[]{:S(2)}) collective-permute-start(f32[8,128]{1,0:T(8,128)S(1)} %add.9), channel_id=1, source_target_pairs={{0,3},{1,2},{2,1},{3,0},{4,7},{5,6},{6,5},{7,4},{8,11},{9,10},{10,... | collective-permute-start | bytes 12296 | tf_op jit(solution)/shard_map/ppermute | solution.py:441
  22.7 3.1 %collective-permute-start.5 = (f32[8,128]{1,0:T(8,128)S(1)}, f32[8,128]{1,0:T(8,128)S(1)}, u32[]{:S(2)}, u32[]{:S(2)}) collective-permute-start(f32[8,128]{1,0:T(8,128)S(1)} %add.10), channel_id=1, source_target_pairs={{0,5},{1,4},{2,7},{3,6},{4,1},{5,0},{6,3},{7,2},{8,13},{9,12},{10,... | collective-permute-start | bytes 12296 | tf_op jit(solution)/shard_map/ppermute | solution.py:441
  25.8 4.0 %collective-permute-start.6 = (f32[8,128]{1,0:T(8,128)S(1)}, f32[8,128]{1,0:T(8,128)S(1)}, u32[]{:S(2)}, u32[]{:S(2)}) collective-permute-start(f32[8,128]{1,0:T(8,128)S(1)} %add.11.near_ref), channel_id=1, source_target_pairs={{0,9},{1,8},{2,11},{3,10},{4,13},{5,12},{6,15},{7,14},{8,1},{9,0},... | collective-permute-start | bytes 12296 | tf_op jit(solution)/shard_map/ppermute | solution.py:442

commit v7 on v6

--- a/solution.py
+++ b/solution.py
@@ -124,18 +124,29 @@
 
 
 def stage_kernel(
-    perturb_hbm, mine_hbm, mix_hbm, perturb_ref, mine_ref, border_ref, matrix_ref, matrix_t_ref, mix, sems
+    perturb_hbm, mine_hbm, mix_hbm, owner_hbm, taps_x_hbm, taps_y_hbm,
+    perturb_ref, mine_ref, border_ref, matrix_ref, matrix_t_ref, vector_ref,
+    mix, owner, taps_x, taps_y, sems,
 ):
     members, _, rows, cells = perturb_ref.shape
-    mix_copy = pltpu.make_async_copy(mix_hbm, mix, sems.at[members + 1])
-    mix_copy.start()
+    small = ((mix_hbm, mix), (owner_hbm, owner), (taps_x_hbm, taps_x), (taps_y_hbm, taps_y))
+    small = [pltpu.make_async_copy(src, dst, sems.at[members + 1 + i]) for i, (src, dst) in enumerate(small)]
+    for copy in small:
+        copy.start()
     copies = []
     for member in range(members):
         copies.append(pltpu.make_async_copy(perturb_hbm.at[member], perturb_ref.at[member], sems.at[member]))
     copies.append(pltpu.make_async_copy(mine_hbm, mine_ref, sems.at[members]))
     for copy in copies:
         copy.start()
-    mix_copy.wait()
+    for copy in small:
+        copy.wait()
+    me = lax.axis_index("member")
+    for slot in range(SLOTS):
+        vector_ref[slot] = jnp.full((8, LANES), jnp.where(owner[slot] == me, 1.0, 0.0), F32)
+    for k in range(7):
+        vector_ref[SLOTS + k] = jnp.full((8, LANES), taps_x[k], F32)
+        vector_ref[SLOTS + 7 + k] = jnp.full((8, LANES), taps_y[k], F32)
     build_mix(mix[...], matrix_ref)
     build_mix(mix[...].T, matrix_t_ref)
     for member in range(members):
@@ -155,44 +166,46 @@
     pl.when(odd)(lambda: run(second, first))
 
 
-def border_kernel(owner_ref, border_ref, mine_ref, other_ref, pair_ref, next_ref):
-    by_parity(functools.partial(border_rows, owner_ref, border_ref, mine_ref, other_ref), pair_ref, next_ref)
-
-
-def border_rows(owner_ref, border_ref, mine_ref, other_ref, up_ref, down_ref):
+def border_kernel(which, vector_ref, border_ref, mine_ref, other_ref, *refs):
+    run = functools.partial(border_rows, vector_ref, border_ref, mine_ref, other_ref, refs[-1])
+    odd = lax.rem(lax.axis_index("tile"), 2) == 1
+    pl.when(jnp.logical_not(odd))(lambda: run(1 - which))
+    pl.when(odd)(lambda: run(which))
+
+
+def border_rows(vector_ref, border_ref, mine_ref, other_ref, out_ref, side):
     _, _, rows, cells = mine_ref.shape
-    total_rows = up_ref.shape[0]
+    start = side * (rows - EDGE)
+    total_rows = out_ref.shape[0]
     per_tile = total_rows // (cells // LANES)
-    me = lax.axis_index("member")
-    valid = [owner_ref[slot] == me for slot in range(SLOTS)]
+    valid = [vector_ref[slot, 0:1, :] > 0.5 for slot in range(SLOTS)]
     sublane = lax.broadcasted_iota(jnp.int32, (8, LANES), 0)
     phase = [lax.rem(sublane + shift, EDGE) for shift in range(EDGE)]
     is_zero = [value == 0 for value in phase]
     is_one = [value == 1 for value in phase]
-    for start, ref, side in ((0, down_ref, 0), (rows - EDGE, up_ref, 1)):
-        whole = {}
-        for t in range(cells // LANES):
+    whole = {}
+    for t in range(cells // LANES):
+        for slot in range(SLOTS):
+            lines = []
+            for i in range(EDGE):
+                here = mine_ref[0, slot, start + i : start + i + 1, lanes_of(t)]
+                there = other_ref[0, slot, start + i : start + i + 1, lanes_of(t)]
+                lines.append(jnp.broadcast_to(jnp.where(valid[slot], here, there), (8, LANES)))
+            for shift in range(EDGE):
+                whole[t, slot, shift] = jnp.where(
+                    is_zero[shift], lines[0], jnp.where(is_one[shift], lines[1], lines[2])
+                )
+        for row in range(0, total_rows, 8):
+            if (row + 7) // per_tile != t:
+                continue
+            total = None
             for slot in range(SLOTS):
-                lines = []
-                for i in range(EDGE):
-                    here = mine_ref[0, slot, start + i : start + i + 1, lanes_of(t)]
-                    there = other_ref[0, slot, start + i : start + i + 1, lanes_of(t)]
-                    lines.append(jnp.broadcast_to(jnp.where(valid[slot], here, there), (8, LANES)))
-                for shift in range(EDGE):
-                    whole[t, slot, shift] = jnp.where(
-                        is_zero[shift], lines[0], jnp.where(is_one[shift], lines[1], lines[2])
-                    )
-            for row in range(0, total_rows, 8):
-                if (row + 7) // per_tile != t:
-                    continue
-                total = None
-                for slot in range(SLOTS):
-                    field = whole[t, slot, row % EDGE]
-                    if row // per_tile != t:
-                        field = jnp.where(sublane < per_tile * t - row, whole[t - 1, slot, row % EDGE], field)
-                    term = border_ref[slot, side, row : row + 8, :] * field
-                    total = term if total is None else total + term
-                ref[row : row + 8, :] = total
+                field = whole[t, slot, row % EDGE]
+                if row // per_tile != t:
+                    field = jnp.where(sublane < per_tile * t - row, whole[t - 1, slot, row % EDGE], field)
+                term = border_ref[slot, side, row : row + 8, :] * field
+                total = term if total is None else total + term
+            out_ref[row : row + 8, :] = total
 
 
 def bulk_kernel(
@@ -301,13 +314,13 @@
 
 
 def correct_kernel(
-    taps_x_ref, taps_y_ref, matrix, from_pair_ref, from_next_ref, local_ref, gradient_ref, packed, left, result
+    vector_ref, matrix, from_pair_ref, from_next_ref, local_ref, gradient_ref, packed, left, result
 ):
     members, rows, cells = local_ref.shape
     count = cells // LANES
     here = EDGE * members
-    taps_x = [taps_x_ref[k] for k in range(7)]
-    taps_y = [taps_y_ref[k] for k in range(7)]
+    taps_x = [vector_ref[SLOTS + k] for k in range(7)]
+    taps_y = [vector_ref[SLOTS + 7 + k] for k in range(7)]
     clear_packed(packed, count)
 
     def unpack(from_right_ref, from_left_ref):
@@ -358,7 +371,7 @@
     other = lax.ppermute(adjoint_forcing, "member", swap)
     edges = EDGE * members * count
     square_matrix = (2 * LANES, 2 * LANES)
-    perturb, mine, border, matrix, matrix_t = pl.pallas_call(
+    perturb, mine, border, matrix, matrix_t, vectors = pl.pallas_call(
         stage_kernel,
         name="stage",
         out_shape=(
@@ -367,23 +380,35 @@
             jax.ShapeDtypeStruct((SLOTS, 2, edges, LANES), F32),
             jax.ShapeDtypeStruct(square_matrix, BF16),
             jax.ShapeDtypeStruct(square_matrix, BF16),
+            jax.ShapeDtypeStruct((SLOTS + 14, 8, LANES), F32),
         ),
-        in_specs=[HBM, HBM, HBM],
-        out_specs=(VMEM,) * 5,
-        scratch_shapes=[pltpu.VMEM(vertical_mix.shape, F32), pltpu.SemaphoreType.DMA((members + 2,))],
+        in_specs=[HBM] * 6,
+        out_specs=(VMEM,) * 6,
+        scratch_shapes=[
+            pltpu.VMEM(vertical_mix.shape, F32),
+            pltpu.SMEM((SLOTS,), jnp.int32),
+            pltpu.SMEM((7,), F32),
+            pltpu.SMEM((7,), F32),
+            pltpu.SemaphoreType.DMA((members + 5,)),
+        ],
         compiler_params=params(8),
         cost_estimate=cost(0, 8_000_000),
-    )(in_hbm(perturb), in_hbm(adjoint_forcing), in_hbm(vertical_mix))
+    )(*map(in_hbm, (perturb, adjoint_forcing, vertical_mix, owner, taps_x, taps_y)))
     packed = jax.ShapeDtypeStruct((edges, LANES), F32)
-    pair, after = pl.pallas_call(
-        border_kernel,
-        name="border_product",
-        out_shape=(packed, packed),
-        in_specs=[SMEM, VMEM, VMEM, VMEM],
-        out_specs=(VMEM, VMEM),
-        compiler_params=params(8),
-        cost_estimate=cost(4_000_000, 4_000_000),
-    )(owner, border, mine, other)
+    sent = []
+    for which in range(2):
+        sent.append(
+            pl.pallas_call(
+                functools.partial(border_kernel, which),
+                name=f"border_product_{which}",
+                out_shape=packed,
+                in_specs=[VMEM, VMEM, VMEM, VMEM] + [pl.BlockSpec(memory_space=pl.ANY)] * which,
+                out_specs=VMEM,
+                compiler_params=params(8),
+                cost_estimate=cost(2_000_000, 2_000_000),
+            )(vectors, border, mine, other, *sent)
+        )
+    pair, after = sent
     swaps = [(i, i + 1) for i in range(tiles - 1)] + [(i + 1, i) for i in range(tiles - 1)]
     from_next = lax.ppermute(after, "tile", [(i, j) for i, j in swaps if min(i, j) % 2 == 1])
     from_pair = lax.ppermute(pair, "tile", [(i, j) for i, j in swaps if min(i, j) % 2 == 0])
@@ -424,13 +449,13 @@
         correct_kernel,
         name="border_correction",
         out_shape=whole,
-        in_specs=[SMEM, SMEM, VMEM, VMEM, VMEM, VMEM],
+        in_specs=[VMEM] * 5,
         out_specs=VMEM,
         scratch_shapes=border_scratch,
-        input_output_aliases={5: 0},
+        input_output_aliases={4: 0},
         compiler_params=params(16),
         cost_estimate=cost(2_000_000_000, 2_000_000),
-    )(taps_x, taps_y, matrix, from_pair, from_next, local)
+    )(vectors, matrix, from_pair, from_next, local)
     near = near + lax.ppermute(near, "member", swap)
     steps = []
     width = 1

time: 32.2 us -> 31.6 us (0.981)
  Pallas kernels: 13 us -> 12.1 us
    ppermute x1, waiting for transfers between devices: 0.03 us -> 0.57 us  [body(): far = lax.ppermute(near, ('tile', 'member'), steps[-1])]
    pallas_call x1, Pallas kernels: 1.29 us -> 0.75 us  [body(): pl.pallas_call(correct_kernel, name='border_correction', out_shape=whole,...]
    pallas_call x1 -> x2, Pallas kernels: 0.78 us -> 0.29 us  [body(): pl.pallas_call(functools.partial(border_kernel, which), name=f'border_pro...]
  transfers between devices with their start and end apart: 7 -> 7, of which waited for: 4 -> 5; matrix products, arithmetic and copies ran while one was open for 0% -> 0% of each run, Pallas kernels for 31% -> 31%
where the time goes in v7:
time: 31.6 us; the launch traced here: 31.5 us
  Pallas kernels  12.1 us (38%)
  starting transfers between devices  10.7 us (34%)
  waiting for transfers between devices  7.93 us (25%)
  between operations  0.75 us (2%)
    pallas_call x1, Pallas kernels, body(): pl.pallas_call(bulk_kernel, name='bulk', out_shape=(whole, packed, packed...  6.68 us
    ppermute x2, starting transfers between devices, body(): near = near + lax.ppermute(near, ('tile', 'member'), pairs)  4.01 us
    ppermute x1, waiting for transfers between devices, body(): lax.ppermute(pair, 'tile', [(i, j) for i, j in swaps if min(i, j) % 2 == 0])  3.54 us
    ppermute x1, starting transfers between devices, body(): far = lax.ppermute(near, ('tile', 'member'), steps[-1])  2.72 us
    ppermute x2, waiting for transfers between devices, body(): near = near + lax.ppermute(near, ('tile', 'member'), pairs)  2.66 us
    ppermute x1, starting transfers between devices, body(): lax.ppermute(pair, 'tile', [(i, j) for i, j in swaps if min(i, j) % 2 == 0])  2.66 us
    pallas_call x1, Pallas kernels, body(): pl.pallas_call(functools.partial(update_kernel, float(entries)), name='up...  2.24 us
    pallas_call x1, Pallas kernels, body(): pl.pallas_call(stage_kernel, name='stage', out_shape=(jax.ShapeDtypeStruc...  2.1 us
  transfers between devices with their start and end apart: 7, of which 5 were waited for; matrix products, arithmetic and copies ran while one was open for 0% of the time, Pallas kernels for 31%

profile of v7, /device:TPU:0, one launch (start us, length us, event | category | flops | bytes accessed | tf_op | source)
XLA Modules:
  0.0 31.5 jit_solution(9368653949153349195)
XLA Ops:
  0.6 0.5 %collective-permute-start = (f32[1,3,24,2048]{3,2,1,0:T(8,128)}, f32[1,3,24,2048]{3,2,1,0:T(8,128)S(1)}, u32[]{:S(2)}, u32[]{:S(2)}) collective-permute-start(f32[1,3,24,2048]{3,2,1,0:T(8,128)} %mine_hbm.1), channel_id=1, source_target_pairs={{0,1},{1,0},{2,3},{3,2},{4,5},{5,4},{6,7},{7,6},{8,9},{9,8},{10,11... | collective-permute-start | bytes 1769480 | tf_op jit(solution)/shard_map/ppermute | solution.py:371
  1.1 2.1 %stage.1 = (bf16[10,3,24,2048]{3,2,1,0:T(8,128)(2,1)S(1)}, f32[1,3,24,2048]{3,2,1,0:T(8,128)S(1)}, f32[3,2,480,128]{3,2,1,0:T(8,128)S(1)}, bf16[256,256]{1,0:T(8...) custom-call(bf16[10,3,24,2048]{3,2,1,0:T(8,128)(2,1)} %perturb_hbm.1, ...), custom_call_target="tpu_custom_call" | custom-call | bytes 8000000 | tf_op jit(solution)/shard_map/stage/pallas_call | solution.py:374
  3.3 0.0 collective-permute-done.other_ref
  3.3 0.1 border_product_0.1.refs_0_.pair_ref
  3.4 0.0 copy-start
  3.4 0.0 copy-start.1
  3.5 0.0 copy-start.2
  3.5 2.7 %collective-permute-start.1 = (f32[480,128]{1,0:T(8,128)S(1)}, f32[480,128]{1,0:T(8,128)S(1)}, u32[]{:S(2)}, u32[]{:S(2)}) collective-permute-start(f32[480,128]{1,0:T(8,128)S(1)} %border_product_0.1.refs_0_.pair_ref), channel_id=1, source_target_pairs={{0,2},{4,6},{8,10},{12,14},{2,0},{6,4},{10,8},{14,12},{1,3},{5,7},... | collective-permute-start | bytes 737288 | tf_op jit(solution)/shard_map/ppermute | solution.py:414
  6.1 0.1 border_product_1.1.next_ref
  6.3 0.7 %collective-permute-start.2 = (f32[480,128]{1,0:T(8,128)S(1)}, f32[480,128]{1,0:T(8,128)S(1)}, u32[]{:S(2)}, u32[]{:S(2)}) collective-permute-start(f32[480,128]{1,0:T(8,128)S(1)} %border_product_1.1.next_ref), channel_id=1, source_target_pairs={{2,4},{6,8},{10,12},{4,2},{8,6},{12,10},{3,5},{7,9},{11,13},{5,3},... | collective-permute-start | bytes 737288 | tf_op jit(solution)/shard_map/ppermute | solution.py:413
  6.9 0.0 copy-done
  7.0 0.0 copy-done.1
  7.0 0.0 copy-done.2
  7.0 6.7 %bulk.1 = (f32[10,24,2048]{2,1,0:T(8,128)S(1)}, f32[480,128]{1,0:T(8,128)S(1)}, f32[480,128]{1,0:T(8,128)S(1)}, f32[8,128]{1,0:T(8,128)S(1)}, f32[10,24,2048]{2,1,0:T(8,128)S(1)}, /*index=5*/f32[10,24,2048]{2,1,0:T(8,128)S(1)}) custom-call(s32[3]{0:T(128)S(1)} %bitcast.2, f32[7]{0:T(128)S(1)} %copy-done.1, f32[7]{0:T(128)S(1)} %copy-done.2, ...), custom_call_target="tpu_custom_call" | custom-call | flops 8999999488 | bytes 12000000 | tf_op jit(solution)/shard_map/bulk/pallas_call | solution.py:421
  13.7 0.0 collective-permute-done.2.from_next_ref
  13.7 3.5 %collective-permute-done.1.from_pair_ref = f32[480,128]{1,0:T(8,128)S(1)} collective-permute-done((f32[480,128]{1,0:T(8,128)S(1)}, f32[480,128]{1,0:T(8,128)S(1)}, u32[]{:S(2)}, u32[]{:S(2)}) %collective-permute-start.1) | collective-permute-done | bytes 245792 | tf_op jit(solution)/shard_map/ppermute | solution.py:414
  17.2 0.1 cross_term.1
  17.3 0.1 collective-permute-start.3
  17.3 1.2 %collective-permute-done.3 = f32[8,128]{1,0:T(8,128)S(1)} collective-permute-done((f32[8,128]{1,0:T(8,128)S(1)}, f32[8,128]{1,0:T(8,128)S(1)}, u32[]{:S(2)}, u32[]{:S(2)}) %collective-permute-start.3) | collective-permute-done | bytes 4128 | tf_op jit(solution)/shard_map/ppermute | solution.py:459
  18.5 2.3 %collective-permute-start.4 = (f32[8,128]{1,0:T(8,128)S(1)}, f32[8,128]{1,0:T(8,128)S(1)}, u32[]{:S(2)}, u32[]{:S(2)}) collective-permute-start(f32[8,128]{1,0:T(8,128)S(1)} %add.9), channel_id=1, source_target_pairs={{0,3},{1,2},{2,1},{3,0},{4,7},{5,6},{6,5},{7,4},{8,11},{9,10},{10,... | collective-permute-start | bytes 12296 | tf_op jit(solution)/shard_map/ppermute | solution.py:466
  20.8 1.3 %collective-permute-done.4 = f32[8,128]{1,0:T(8,128)S(1)} collective-permute-done((f32[8,128]{1,0:T(8,128)S(1)}, f32[8,128]{1,0:T(8,128)S(1)}, u32[]{:S(2)}, u32[]{:S(2)}) %collective-permute-start.4) | collective-permute-done | bytes 4128 | tf_op jit(solution)/shard_map/ppermute | solution.py:466
  22.1 1.8 %collective-permute-start.5 = (f32[8,128]{1,0:T(8,128)S(1)}, f32[8,128]{1,0:T(8,128)S(1)}, u32[]{:S(2)}, u32[]{:S(2)}) collective-permute-start(f32[8,128]{1,0:T(8,128)S(1)} %add.10), channel_id=1, source_target_pairs={{0,5},{1,4},{2,7},{3,6},{4,1},{5,0},{6,3},{7,2},{8,13},{9,12},{10,... | collective-permute-start | bytes 12296 | tf_op jit(solution)/shard_map/ppermute | solution.py:466
  23.8 1.3 %collective-permute-done.5 = f32[8,128]{1,0:T(8,128)S(1)} collective-permute-done((f32[8,128]{1,0:T(8,128)S(1)}, f32[8,128]{1,0:T(8,128)S(1)}, u32[]{:S(2)}, u32[]{:S(2)}) %collective-permute-start.5) | collective-permute-done | bytes 4128 | tf_op jit(solution)/shard_map/ppermute | solution.py:466
  25.2 2.7 %collective-permute-start.6 = (f32[8,128]{1,0:T(8,128)S(1)}, f32[8,128]{1,0:T(8,128)S(1)}, u32[]{:S(2)}, u32[]{:S(2)}) collective-permute-start(f32[8,128]{1,0:T(8,128)S(1)} %add.11.near_ref), channel_id=1, source_target_pairs={{0,9},{1,8},{2,11},{3,10},{4,13},{5,12},{6,15},{7,14},{8,1},{9,0},... | collective-permute-start | bytes 12296 | tf_op jit(solution)/shard_map/ppermute | solution.py:467
  27.9 0.7 %border_correction.1.gradient_ref = f32[10,24,2048]{2,1,0:T(8,128)S(1)} custom-call(f32[17,8,128]{2,1,0:T(8,128)S(1)} %get-tuple-element.18.vector_ref, bf16[256,256]{1,0:T(8,128)(2,1)S(1)} %get-tuple-element.14.matrix, f32[480,128]{1,0:T(8,128)S(1)} %collective-permute-done.1.from_pair_ref, ...), custom_call_target="tpu_custom_call", output_to_operand_aliasing={{}: (4, {})} | custom-call | flops 2000000000 | bytes 2000000 | tf_op jit(solution)/shard_map/border_correction/pallas_call | solution.py:448
  28.7 0.6 %collective-permute-done.6.far_ref = f32[8,128]{1,0:T(8,128)S(1)} collective-permute-done((f32[8,128]{1,0:T(8,128)S(1)}, f32[8,128]{1,0:T(8,128)S(1)}, u32[]{:S(2)}, u32[]{:S(2)}) %collective-permute-start.6) | collective-permute-done | bytes 4128 | tf_op jit(solution)/shard_map/ppermute | solution.py:467
  29.2 2.2 %update.1 = (f32[10,24,2048]{2,1,0:T(8,128)}, f32[10,24,2048]{2,1,0:T(8,128)}) custom-call(f32[8,128]{1,0:T(8,128)S(1)} %add.11.near_ref, f32[8,128]{1,0:T(8,128)S(1)} %collective-permute-done.6.far_ref, f32[10,24,2048]{2,1,0:T(8,128)S(1)} %get-tuple-element.23.control_ref, f32[10,24,2048]{2,1,0:T(8,128)S(1)} %get-tuple-element.24.velocity_ref, ...), custom_call_target="tpu_custom_call" | custom-call | flops 3000000 | bytes 12000000 | tf_op jit(solution)/shard_map/update/pallas_call | solution.py:470
  (3 shorter events, 0.0 us)
Async XLA Ops:
  0.6 2.6 %collective-permute-start = (f32[1,3,24,2048]{3,2,1,0:T(8,128)}, f32[1,3,24,2048]{3,2,1,0:T(8,128)S(1)}, u32[]{:S(2)}, u32[]{:S(2)}) collective-permute-start(f32[1,3,24,2048]{3,2,1,0:T(8,128)} %mine_hbm.1), channel_id=1, source_target_pairs={{0,1},{1,0},{2,3},{3,2},{4,5},{5,4},{6,7},{7,6},{8,9},{9,8},{10,11... | collective-permute-start | bytes 1769480 | tf_op jit(solution)/shard_map/ppermute | solution.py:371
  3.4 3.5 %copy-start = (s32[3,1]{0,1:T(1,128)S(1)}, s32[3,1]{0,1:T(1,128)}, u32[]{:S(2)}) copy-start(s32[3,1]{0,1:T(1,128)} %param.12) | copy-start | bytes 40
  3.4 3.5 %copy-start.1 = (f32[7]{0:T(128)S(1)}, f32[7]{0:T(128)}, u32[]{:S(2)}) copy-start(f32[7]{0:T(128)} %taps_x_ref.1) | copy-start | bytes 88
  3.5 3.5 %copy-start.2 = (f32[7]{0:T(128)S(1)}, f32[7]{0:T(128)}, u32[]{:S(2)}) copy-start(f32[7]{0:T(128)} %taps_y_ref.1) | copy-start | bytes 88
  3.5 13.7 %collective-permute-start.1 = (f32[480,128]{1,0:T(8,128)S(1)}, f32[480,128]{1,0:T(8,128)S(1)}, u32[]{:S(2)}, u32[]{:S(2)}) collective-permute-start(f32[480,128]{1,0:T(8,128)S(1)} %border_product_0.1.refs_0_.pair_ref), channel_id=1, source_target_pairs={{0,2},{4,6},{8,10},{12,14},{2,0},{6,4},{10,8},{14,12},{1,3},{5,7},... | collective-permute-start | bytes 737288 | tf_op jit(solution)/shard_map/ppermute | solution.py:414
  6.3 7.4 %collective-permute-start.2 = (f32[480,128]{1,0:T(8,128)S(1)}, f32[480,128]{1,0:T(8,128)S(1)}, u32[]{:S(2)}, u32[]{:S(2)}) collective-permute-start(f32[480,128]{1,0:T(8,128)S(1)} %border_product_1.1.next_ref), channel_id=1, source_target_pairs={{2,4},{6,8},{10,12},{4,2},{8,6},{12,10},{3,5},{7,9},{11,13},{5,3},... | collective-permute-start | bytes 737288 | tf_op jit(solution)/shard_map/ppermute | solution.py:413
  17.3 1.2 %collective-permute-start.3 = (f32[8,128]{1,0:T(8,128)S(1)}, f32[8,128]{1,0:T(8,128)S(1)}, u32[]{:S(2)}, u32[]{:S(2)}) collective-permute-start(f32[8,128]{1,0:T(8,128)S(1)} %cross_term.1), channel_id=1, source_target_pairs={{0,1},{1,0},{2,3},{3,2},{4,5},{5,4},{6,7},{7,6},{8,9},{9,8},{10,11... | collective-permute-start | bytes 12296 | tf_op jit(solution)/shard_map/ppermute | solution.py:459
  18.5 3.6 %collective-permute-start.4 = (f32[8,128]{1,0:T(8,128)S(1)}, f32[8,128]{1,0:T(8,128)S(1)}, u32[]{:S(2)}, u32[]{:S(2)}) collective-permute-start(f32[8,128]{1,0:T(8,128)S(1)} %add.9), channel_id=1, source_target_pairs={{0,3},{1,2},{2,1},{3,0},{4,7},{5,6},{6,5},{7,4},{8,11},{9,10},{10,... | collective-permute-start | bytes 12296 | tf_op jit(solution)/shard_map/ppermute | solution.py:466
  22.1 3.1 %collective-permute-start.5 = (f32[8,128]{1,0:T(8,128)S(1)}, f32[8,128]{1,0:T(8,128)S(1)}, u32[]{:S(2)}, u32[]{:S(2)}) collective-permute-start(f32[8,128]{1,0:T(8,128)S(1)} %add.10), channel_id=1, source_target_pairs={{0,5},{1,4},{2,7},{3,6},{4,1},{5,0},{6,3},{7,2},{8,13},{9,12},{10,... | collective-permute-start | bytes 12296 | tf_op jit(solution)/shard_map/ppermute | solution.py:466
  25.2 4.0 %collective-permute-start.6 = (f32[8,128]{1,0:T(8,128)S(1)}, f32[8,128]{1,0:T(8,128)S(1)}, u32[]{:S(2)}, u32[]{:S(2)}) collective-permute-start(f32[8,128]{1,0:T(8,128)S(1)} %add.11.near_ref), channel_id=1, source_target_pairs={{0,9},{1,8},{2,11},{3,10},{4,13},{5,12},{6,15},{7,14},{8,1},{9,0},... | collective-permute-start | bytes 12296 | tf_op jit(solution)/shard_map/ppermute | solution.py:467

commit v8 on v7

--- a/solution.py
+++ b/solution.py
@@ -310,7 +310,8 @@
         which = 2 * (step % 2)
         total[which] += cross_pair_ref[at] * from_pair_ref[at]
         total[which + 1] += cross_next_ref[at] * from_next_ref[at]
-    total_ref[...] = square_ref[...] + 2.0 * ((total[0] + total[1]) + (total[2] + total[3]))
+    whole = square_ref[...] + 2.0 * ((total[0] + total[1]) + (total[2] + total[3]))
+    total_ref[...] = jnp.sum(whole, axis=0, keepdims=True)
 
 
 def correct_kernel(
@@ -439,7 +440,7 @@
     near = pl.pallas_call(
         cross_kernel,
         name="cross_term",
-        out_shape=jax.ShapeDtypeStruct((8, LANES), F32),
+        out_shape=jax.ShapeDtypeStruct((1, LANES), F32),
         in_specs=[VMEM] * 5,
         out_specs=VMEM,
         compiler_params=params(8),

time: 31.6 us -> 31.4 us (level)
  no operation moved by 1% of the time
where the time goes in v8:
time: 31.4 us; the launch traced here: 31.3 us
  Pallas kernels  12.1 us (39%)
  starting transfers between devices  10.6 us (34%)
  waiting for transfers between devices  7.78 us (25%)
  between operations  0.75 us (2%)
    pallas_call x1, Pallas kernels, body(): pl.pallas_call(bulk_kernel, name='bulk', out_shape=(whole, packed, packed...  6.69 us
    ppermute x2, starting transfers between devices, body(): near = near + lax.ppermute(near, ('tile', 'member'), pairs)  4.02 us
    ppermute x1, waiting for transfers between devices, body(): lax.ppermute(pair, 'tile', [(i, j) for i, j in swaps if min(i, j) % 2 == 0])  3.53 us
    ppermute x1, starting transfers between devices, body(): far = lax.ppermute(near, ('tile', 'member'), steps[-1])  2.68 us
    ppermute x1, starting transfers between devices, body(): lax.ppermute(pair, 'tile', [(i, j) for i, j in swaps if min(i, j) % 2 == 0])  2.66 us
    ppermute x2, waiting for transfers between devices, body(): near = near + lax.ppermute(near, ('tile', 'member'), pairs)  2.59 us
    pallas_call x1, Pallas kernels, body(): pl.pallas_call(functools.partial(update_kernel, float(entries)), name='up...  2.24 us
    pallas_call x1, Pallas kernels, body(): pl.pallas_call(stage_kernel, name='stage', out_shape=(jax.ShapeDtypeStruc...  2.1 us
  transfers between devices with their start and end apart: 7, of which 5 were waited for; matrix products, arithmetic and copies ran while one was open for 0% of the time, Pallas kernels for 31%

profile of v8, /device:TPU:0, one launch (start us, length us, event | category | flops | bytes accessed | tf_op | source)
XLA Modules:
  0.0 31.3 jit_solution(8446554039050814591)
XLA Ops:
  0.6 0.5 %collective-permute-start = (f32[1,3,24,2048]{3,2,1,0:T(8,128)}, f32[1,3,24,2048]{3,2,1,0:T(8,128)S(1)}, u32[]{:S(2)}, u32[]{:S(2)}) collective-permute-start(f32[1,3,24,2048]{3,2,1,0:T(8,128)} %mine_hbm.1), channel_id=1, source_target_pairs={{0,1},{1,0},{2,3},{3,2},{4,5},{5,4},{6,7},{7,6},{8,9},{9,8},{10,11... | collective-permute-start | bytes 1769480 | tf_op jit(solution)/shard_map/ppermute | solution.py:372
  1.1 2.1 %stage.1 = (bf16[10,3,24,2048]{3,2,1,0:T(8,128)(2,1)S(1)}, f32[1,3,24,2048]{3,2,1,0:T(8,128)S(1)}, f32[3,2,480,128]{3,2,1,0:T(8,128)S(1)}, bf16[256,256]{1,0:T(8...) custom-call(bf16[10,3,24,2048]{3,2,1,0:T(8,128)(2,1)} %perturb_hbm.1, ...), custom_call_target="tpu_custom_call" | custom-call | bytes 8000000 | tf_op jit(solution)/shard_map/stage/pallas_call | solution.py:375
  3.3 0.0 collective-permute-done.other_ref
  3.3 0.1 border_product_0.1.refs_0_.pair_ref
  3.4 0.0 copy-start
  3.4 0.0 copy-start.1
  3.5 0.0 copy-start.2
  3.5 2.7 %collective-permute-start.1 = (f32[480,128]{1,0:T(8,128)S(1)}, f32[480,128]{1,0:T(8,128)S(1)}, u32[]{:S(2)}, u32[]{:S(2)}) collective-permute-start(f32[480,128]{1,0:T(8,128)S(1)} %border_product_0.1.refs_0_.pair_ref), channel_id=1, source_target_pairs={{0,2},{4,6},{8,10},{12,14},{2,0},{6,4},{10,8},{14,12},{1,3},{5,7},... | collective-permute-start | bytes 737288 | tf_op jit(solution)/shard_map/ppermute | solution.py:415
  6.1 0.1 border_product_1.1.next_ref
  6.3 0.7 %collective-permute-start.2 = (f32[480,128]{1,0:T(8,128)S(1)}, f32[480,128]{1,0:T(8,128)S(1)}, u32[]{:S(2)}, u32[]{:S(2)}) collective-permute-start(f32[480,128]{1,0:T(8,128)S(1)} %border_product_1.1.next_ref), channel_id=1, source_target_pairs={{2,4},{6,8},{10,12},{4,2},{8,6},{12,10},{3,5},{7,9},{11,13},{5,3},... | collective-permute-start | bytes 737288 | tf_op jit(solution)/shard_map/ppermute | solution.py:414
  6.9 0.0 copy-done
  7.0 0.0 copy-done.1
  7.0 0.0 copy-done.2
  7.0 6.7 %bulk.1 = (f32[10,24,2048]{2,1,0:T(8,128)S(1)}, f32[480,128]{1,0:T(8,128)S(1)}, f32[480,128]{1,0:T(8,128)S(1)}, f32[8,128]{1,0:T(8,128)S(1)}, f32[10,24,2048]{2,1,0:T(8,128)S(1)}, /*index=5*/f32[10,24,2048]{2,1,0:T(8,128)S(1)}) custom-call(s32[3]{0:T(128)S(1)} %bitcast.2, f32[7]{0:T(128)S(1)} %copy-done.1, f32[7]{0:T(128)S(1)} %copy-done.2, ...), custom_call_target="tpu_custom_call" | custom-call | flops 8999999488 | bytes 12000000 | tf_op jit(solution)/shard_map/bulk/pallas_call | solution.py:422
  13.7 0.0 collective-permute-done.2.from_next_ref
  13.7 3.5 %collective-permute-done.1.from_pair_ref = f32[480,128]{1,0:T(8,128)S(1)} collective-permute-done((f32[480,128]{1,0:T(8,128)S(1)}, f32[480,128]{1,0:T(8,128)S(1)}, u32[]{:S(2)}, u32[]{:S(2)}) %collective-permute-start.1) | collective-permute-done | bytes 245792 | tf_op jit(solution)/shard_map/ppermute | solution.py:415
  17.2 0.1 cross_term.1
  17.3 0.1 collective-permute-start.3
  17.3 1.1 %collective-permute-done.3 = f32[1,128]{1,0:T(1,128)S(1)} collective-permute-done((f32[1,128]{1,0:T(1,128)S(1)}, f32[1,128]{1,0:T(1,128)S(1)}, u32[]{:S(2)}, u32[]{:S(2)}) %collective-permute-start.3) | collective-permute-done | bytes 544 | tf_op jit(solution)/shard_map/ppermute | solution.py:460
  18.5 2.3 %collective-permute-start.4 = (f32[1,128]{1,0:T(1,128)S(1)}, f32[1,128]{1,0:T(1,128)S(1)}, u32[]{:S(2)}, u32[]{:S(2)}) collective-permute-start(f32[1,128]{1,0:T(1,128)S(1)} %add.9), channel_id=1, source_target_pairs={{0,3},{1,2},{2,1},{3,0},{4,7},{5,6},{6,5},{7,4},{8,11},{9,10},{10,... | collective-permute-start | bytes 1544 | tf_op jit(solution)/shard_map/ppermute | solution.py:467
  20.8 1.3 %collective-permute-done.4 = f32[1,128]{1,0:T(1,128)S(1)} collective-permute-done((f32[1,128]{1,0:T(1,128)S(1)}, f32[1,128]{1,0:T(1,128)S(1)}, u32[]{:S(2)}, u32[]{:S(2)}) %collective-permute-start.4) | collective-permute-done | bytes 544 | tf_op jit(solution)/shard_map/ppermute | solution.py:467
  22.1 1.7 %collective-permute-start.5 = (f32[1,128]{1,0:T(1,128)S(1)}, f32[1,128]{1,0:T(1,128)S(1)}, u32[]{:S(2)}, u32[]{:S(2)}) collective-permute-start(f32[1,128]{1,0:T(1,128)S(1)} %add.10), channel_id=1, source_target_pairs={{0,5},{1,4},{2,7},{3,6},{4,1},{5,0},{6,3},{7,2},{8,13},{9,12},{10,... | collective-permute-start | bytes 1544 | tf_op jit(solution)/shard_map/ppermute | solution.py:467
  23.8 1.3 %collective-permute-done.5 = f32[1,128]{1,0:T(1,128)S(1)} collective-permute-done((f32[1,128]{1,0:T(1,128)S(1)}, f32[1,128]{1,0:T(1,128)S(1)}, u32[]{:S(2)}, u32[]{:S(2)}) %collective-permute-start.5) | collective-permute-done | bytes 544 | tf_op jit(solution)/shard_map/ppermute | solution.py:467
  25.1 2.7 %collective-permute-start.6 = (f32[1,128]{1,0:T(1,128)S(1)}, f32[1,128]{1,0:T(1,128)S(1)}, u32[]{:S(2)}, u32[]{:S(2)}) collective-permute-start(f32[1,128]{1,0:T(1,128)S(1)} %add.11.near_ref), channel_id=1, source_target_pairs={{0,9},{1,8},{2,11},{3,10},{4,13},{5,12},{6,15},{7,14},{8,1},{9,0},... | collective-permute-start | bytes 1544 | tf_op jit(solution)/shard_map/ppermute | solution.py:468
  27.8 0.7 %border_correction.1.gradient_ref = f32[10,24,2048]{2,1,0:T(8,128)S(1)} custom-call(f32[17,8,128]{2,1,0:T(8,128)S(1)} %get-tuple-element.18.vector_ref, bf16[256,256]{1,0:T(8,128)(2,1)S(1)} %get-tuple-element.14.matrix, f32[480,128]{1,0:T(8,128)S(1)} %collective-permute-done.1.from_pair_ref, ...), custom_call_target="tpu_custom_call", output_to_operand_aliasing={{}: (4, {})} | custom-call | flops 2000000000 | bytes 2000000 | tf_op jit(solution)/shard_map/border_correction/pallas_call | solution.py:449
  28.5 0.5 %collective-permute-done.6.far_ref = f32[1,128]{1,0:T(1,128)S(1)} collective-permute-done((f32[1,128]{1,0:T(1,128)S(1)}, f32[1,128]{1,0:T(1,128)S(1)}, u32[]{:S(2)}, u32[]{:S(2)}) %collective-permute-start.6) | collective-permute-done | bytes 544 | tf_op jit(solution)/shard_map/ppermute | solution.py:468
  29.1 2.2 %update.1 = (f32[10,24,2048]{2,1,0:T(8,128)}, f32[10,24,2048]{2,1,0:T(8,128)}) custom-call(f32[1,128]{1,0:T(1,128)S(1)} %add.11.near_ref, f32[1,128]{1,0:T(1,128)S(1)} %collective-permute-done.6.far_ref, f32[10,24,2048]{2,1,0:T(8,128)S(1)} %get-tuple-element.23.control_ref, f32[10,24,2048]{2,1,0:T(8,128)S(1)} %get-tuple-element.24.velocity_ref, ...), custom_call_target="tpu_custom_call" | custom-call | flops 3000000 | bytes 12000000 | tf_op jit(solution)/shard_map/update/pallas_call | solution.py:471
  (3 shorter events, 0.0 us)
Async XLA Ops:
  0.6 2.6 %collective-permute-start = (f32[1,3,24,2048]{3,2,1,0:T(8,128)}, f32[1,3,24,2048]{3,2,1,0:T(8,128)S(1)}, u32[]{:S(2)}, u32[]{:S(2)}) collective-permute-start(f32[1,3,24,2048]{3,2,1,0:T(8,128)} %mine_hbm.1), channel_id=1, source_target_pairs={{0,1},{1,0},{2,3},{3,2},{4,5},{5,4},{6,7},{7,6},{8,9},{9,8},{10,11... | collective-permute-start | bytes 1769480 | tf_op jit(solution)/shard_map/ppermute | solution.py:372
  3.4 3.5 %copy-start = (s32[3,1]{0,1:T(1,128)S(1)}, s32[3,1]{0,1:T(1,128)}, u32[]{:S(2)}) copy-start(s32[3,1]{0,1:T(1,128)} %param.12) | copy-start | bytes 40
  3.4 3.5 %copy-start.1 = (f32[7]{0:T(128)S(1)}, f32[7]{0:T(128)}, u32[]{:S(2)}) copy-start(f32[7]{0:T(128)} %taps_x_ref.1) | copy-start | bytes 88
  3.5 3.5 %copy-start.2 = (f32[7]{0:T(128)S(1)}, f32[7]{0:T(128)}, u32[]{:S(2)}) copy-start(f32[7]{0:T(128)} %taps_y_ref.1) | copy-start | bytes 88
  3.5 13.7 %collective-permute-start.1 = (f32[480,128]{1,0:T(8,128)S(1)}, f32[480,128]{1,0:T(8,128)S(1)}, u32[]{:S(2)}, u32[]{:S(2)}) collective-permute-start(f32[480,128]{1,0:T(8,128)S(1)} %border_product_0.1.refs_0_.pair_ref), channel_id=1, source_target_pairs={{0,2},{4,6},{8,10},{12,14},{2,0},{6,4},{10,8},{14,12},{1,3},{5,7},... | collective-permute-start | bytes 737288 | tf_op jit(solution)/shard_map/ppermute | solution.py:415
  6.3 7.4 %collective-permute-start.2 = (f32[480,128]{1,0:T(8,128)S(1)}, f32[480,128]{1,0:T(8,128)S(1)}, u32[]{:S(2)}, u32[]{:S(2)}) collective-permute-start(f32[480,128]{1,0:T(8,128)S(1)} %border_product_1.1.next_ref), channel_id=1, source_target_pairs={{2,4},{6,8},{10,12},{4,2},{8,6},{12,10},{3,5},{7,9},{11,13},{5,3},... | collective-permute-start | bytes 737288 | tf_op jit(solution)/shard_map/ppermute | solution.py:414
  17.3 1.2 %collective-permute-start.3 = (f32[1,128]{1,0:T(1,128)S(1)}, f32[1,128]{1,0:T(1,128)S(1)}, u32[]{:S(2)}, u32[]{:S(2)}) collective-permute-start(f32[1,128]{1,0:T(1,128)S(1)} %cross_term.1), channel_id=1, source_target_pairs={{0,1},{1,0},{2,3},{3,2},{4,5},{5,4},{6,7},{7,6},{8,9},{9,8},{10,11... | collective-permute-start | bytes 1544 | tf_op jit(solution)/shard_map/ppermute | solution.py:460
  18.5 3.6 %collective-permute-start.4 = (f32[1,128]{1,0:T(1,128)S(1)}, f32[1,128]{1,0:T(1,128)S(1)}, u32[]{:S(2)}, u32[]{:S(2)}) collective-permute-start(f32[1,128]{1,0:T(1,128)S(1)} %add.9), channel_id=1, source_target_pairs={{0,3},{1,2},{2,1},{3,0},{4,7},{5,6},{6,5},{7,4},{8,11},{9,10},{10,... | collective-permute-start | bytes 1544 | tf_op jit(solution)/shard_map/ppermute | solution.py:467
  22.1 3.0 %collective-permute-start.5 = (f32[1,128]{1,0:T(1,128)S(1)}, f32[1,128]{1,0:T(1,128)S(1)}, u32[]{:S(2)}, u32[]{:S(2)}) collective-permute-start(f32[1,128]{1,0:T(1,128)S(1)} %add.10), channel_id=1, source_target_pairs={{0,5},{1,4},{2,7},{3,6},{4,1},{5,0},{6,3},{7,2},{8,13},{9,12},{10,... | collective-permute-start | bytes 1544 | tf_op jit(solution)/shard_map/ppermute | solution.py:467
  25.1 4.0 %collective-permute-start.6 = (f32[1,128]{1,0:T(1,128)S(1)}, f32[1,128]{1,0:T(1,128)S(1)}, u32[]{:S(2)}, u32[]{:S(2)}) collective-permute-start(f32[1,128]{1,0:T(1,128)S(1)} %add.11.near_ref), channel_id=1, source_target_pairs={{0,9},{1,8},{2,11},{3,10},{4,13},{5,12},{6,15},{7,14},{8,1},{9,0},... | collective-permute-start | bytes 1544 | tf_op jit(solution)/shard_map/ppermute | solution.py:468

commit v9 on v8

--- a/solution.py
+++ b/solution.py
@@ -130,13 +130,15 @@
 ):
     members, _, rows, cells = perturb_ref.shape
     small = ((mix_hbm, mix), (owner_hbm, owner), (taps_x_hbm, taps_x), (taps_y_hbm, taps_y))
-    small = [pltpu.make_async_copy(src, dst, sems.at[members + 1 + i]) for i, (src, dst) in enumerate(small)]
+    small = [pltpu.make_async_copy(src, dst, sems.at[members + 2 + i]) for i, (src, dst) in enumerate(small)]
     for copy in small:
         copy.start()
     copies = []
     for member in range(members):
         copies.append(pltpu.make_async_copy(perturb_hbm.at[member], perturb_ref.at[member], sems.at[member]))
-    copies.append(pltpu.make_async_copy(mine_hbm, mine_ref, sems.at[members]))
+    for side, start in enumerate((0, rows - 8)):
+        source = mine_hbm.at[0, :, pl.ds(start, 8)]
+        copies.append(pltpu.make_async_copy(source, mine_ref.at[side], sems.at[members + side]))
     for copy in copies:
         copy.start()
     for copy in small:
@@ -158,6 +160,7 @@
                     value = perturb_ref[member, slot, start : start + 8, lanes_of(t)].astype(F32)
                     border_ref[slot, side, at : at + EDGE, :] = value[first : first + EDGE]
     copies[members].wait()
+    copies[members + 1].wait()
 
 
 def by_parity(run, first, second):
@@ -174,8 +177,8 @@
 
 
 def border_rows(vector_ref, border_ref, mine_ref, other_ref, out_ref, side):
-    _, _, rows, cells = mine_ref.shape
-    start = side * (rows - EDGE)
+    _, _, rows, cells = other_ref.shape
+    start, near = side * (rows - EDGE), side * (8 - EDGE)
     total_rows = out_ref.shape[0]
     per_tile = total_rows // (cells // LANES)
     valid = [vector_ref[slot, 0:1, :] > 0.5 for slot in range(SLOTS)]
@@ -188,7 +191,7 @@
         for slot in range(SLOTS):
             lines = []
             for i in range(EDGE):
-                here = mine_ref[0, slot, start + i : start + i + 1, lanes_of(t)]
+                here = mine_ref[side, slot, near + i : near + i + 1, lanes_of(t)]
                 there = other_ref[0, slot, start + i : start + i + 1, lanes_of(t)]
                 lines.append(jnp.broadcast_to(jnp.where(valid[slot], here, there), (8, LANES)))
             for shift in range(EDGE):
@@ -209,14 +212,16 @@
 
 
 def bulk_kernel(
-    owner_ref, taps_x_ref, taps_y_ref, matrix, matrix_t, perturb_ref, mine_ref, other_ref, pair_ref, next_ref,
-    control_hbm, velocity_hbm,
+    owner_ref, taps_x_ref, taps_y_ref, matrix, matrix_t, perturb_ref, other_ref, pair_ref, next_ref,
+    mine_hbm, control_hbm, velocity_hbm,
     local_ref, cross_pair_ref, cross_next_ref, square_ref, control_ref, velocity_ref,
-    field, rows_of, packed, left, result, sems,
+    mine, field, rows_of, packed, left, result, sems,
 ):
     members, _, rows, cells = perturb_ref.shape
     count = cells // LANES
     here = EDGE * members
+    mine_copy = pltpu.make_async_copy(mine_hbm, mine, sems.at[2])
+    mine_copy.start()
     control_copy = pltpu.make_async_copy(control_hbm, control_ref, sems.at[0])
     velocity_copy = pltpu.make_async_copy(velocity_hbm, velocity_ref, sems.at[1])
     control_copy.start()
@@ -227,8 +232,6 @@
     taps_x = [taps_x_ref[k] for k in range(7)]
     taps_y = [taps_y_ref[k] for k in range(7)]
     first_taps, last_taps = taps_x[0:EDGE], taps_x[6 : 6 - EDGE : -1]
-    for slot in range(SLOTS):
-        field[slot] = jnp.where(owner_ref[slot] == me, mine_ref[0, slot], other_ref[0, slot])
     for half in range(2):
         rows_of[half, :, 0:8, :] = jnp.zeros((count, 8, LANES), F32)
         rows_of[half, :, rows + 8 : rows + 16, :] = jnp.zeros((count, 8, LANES), F32)
@@ -250,6 +253,10 @@
                 value = result[64 * t + 32 * side + 8 * step : 64 * t + 32 * side + 8 * step + 8, :]
                 total[step] += value * value
         squares += weights[side] * ((total[0] + total[1]) + (total[2] + total[3]))
+
+    mine_copy.wait()
+    for slot in range(SLOTS):
+        field[slot] = jnp.where(owner_ref[slot] == me, mine[0, slot], other_ref[0, slot])
 
     def pair_step(pair, carry):
         for half in range(2):
@@ -377,7 +384,7 @@
         name="stage",
         out_shape=(
             jax.ShapeDtypeStruct(perturb.shape, perturb.dtype),
-            jax.ShapeDtypeStruct(adjoint_forcing.shape, F32),
+            jax.ShapeDtypeStruct((2, SLOTS, 8, cells), F32),
             jax.ShapeDtypeStruct((SLOTS, 2, edges, LANES), F32),
             jax.ShapeDtypeStruct(square_matrix, BF16),
             jax.ShapeDtypeStruct(square_matrix, BF16),
@@ -390,7 +397,7 @@
             pltpu.SMEM((SLOTS,), jnp.int32),
             pltpu.SMEM((7,), F32),
             pltpu.SMEM((7,), F32),
-            pltpu.SemaphoreType.DMA((members + 5,)),
+            pltpu.SemaphoreType.DMA((members + 6,)),
         ],
         compiler_params=params(8),
         cost_estimate=cost(0, 8_000_000),
@@ -423,19 +430,20 @@
         bulk_kernel,
         name="bulk",
         out_shape=(whole, packed, packed, jax.ShapeDtypeStruct((8, LANES), F32), whole, whole),
-        in_specs=[SMEM, SMEM, SMEM] + [VMEM] * 7 + [HBM, HBM],
+        in_specs=[SMEM, SMEM, SMEM] + [VMEM] * 6 + [HBM, HBM, HBM],
         out_specs=(VMEM,) * 6,
         scratch_shapes=[
+            pltpu.VMEM(adjoint_forcing.shape, F32),
             pltpu.VMEM((SLOTS, rows, cells), F32),
             pltpu.VMEM((2, count, rows + 16, LANES), F32),
             *border_scratch,
-            pltpu.SemaphoreType.DMA((2,)),
+            pltpu.SemaphoreType.DMA((3,)),
         ],
         compiler_params=params(24),
         cost_estimate=cost(9_000_000_000, 12_000_000),
     )(
-        owner, taps_x, taps_y, matrix, matrix_t, perturb, mine, other, pair, after,
-        in_hbm(control), in_hbm(velocity),
+        owner, taps_x, taps_y, matrix, matrix_t, perturb, other, pair, after,
+        in_hbm(adjoint_forcing), in_hbm(control), in_hbm(velocity),
     )
     near = pl.pallas_call(
         cross_kernel,

time: 31.4 us -> 31.4 us (level)
  no operation moved by 1% of the time
where the time goes in v9:
time: 31.4 us; the launch traced here: 31.2 us
  Pallas kernels  12.2 us (39%)
  starting transfers between devices  10.7 us (34%)
  waiting for transfers between devices  7.48 us (24%)
  between operations  0.75 us (2%)
    pallas_call x1, Pallas kernels, body(): pl.pallas_call(bulk_kernel, name='bulk', out_shape=(whole, packed, packed...  6.89 us
    ppermute x2, starting transfers between devices, body(): near = near + lax.ppermute(near, ('tile', 'member'), pairs)  4.02 us
    ppermute x1, waiting for transfers between devices, body(): lax.ppermute(pair, 'tile', [(i, j) for i, j in swaps if min(i, j) % 2 == 0])  3.23 us
    ppermute x1, starting transfers between devices, body(): lax.ppermute(pair, 'tile', [(i, j) for i, j in swaps if min(i, j) % 2 == 0])  2.74 us
    ppermute x1, starting transfers between devices, body(): far = lax.ppermute(near, ('tile', 'member'), steps[-1])  2.68 us
    ppermute x2, waiting for transfers between devices, body(): near = near + lax.ppermute(near, ('tile', 'member'), pairs)  2.59 us
    pallas_call x1, Pallas kernels, body(): pl.pallas_call(functools.partial(update_kernel, float(entries)), name='up...  2.24 us
    pallas_call x1, Pallas kernels, body(): pl.pallas_call(stage_kernel, name='stage', out_shape=(jax.ShapeDtypeStruc...  2.03 us
  transfers between devices with their start and end apart: 7, of which 5 were waited for; matrix products, arithmetic and copies ran while one was open for 0% of the time, Pallas kernels for 31%

profile of v9, /device:TPU:0, one launch (start us, length us, event | category | flops | bytes accessed | tf_op | source)
XLA Modules:
  0.0 31.2 jit_solution(11531011475639747843)
XLA Ops:
  0.6 0.5 %collective-permute-start = (f32[1,3,24,2048]{3,2,1,0:T(8,128)}, f32[1,3,24,2048]{3,2,1,0:T(8,128)S(1)}, u32[]{:S(2)}, u32[]{:S(2)}) collective-permute-start(f32[1,3,24,2048]{3,2,1,0:T(8,128)} %mine_hbm.3), channel_id=1, source_target_pairs={{0,1},{1,0},{2,3},{3,2},{4,5},{5,4},{6,7},{7,6},{8,9},{9,8},{10,11... | collective-permute-start | bytes 1769480 | tf_op jit(solution)/shard_map/ppermute | solution.py:379
  1.1 2.0 %stage.1 = (bf16[10,3,24,2048]{3,2,1,0:T(8,128)(2,1)S(1)}, f32[2,3,8,2048]{3,2,1,0:T(8,128)S(1)}, f32[3,2,480,128]{3,2,1,0:T(8,128)S(1)}, bf16[256,256]{1,0:T(8,...) custom-call(bf16[10,3,24,2048]{3,2,1,0:T(8,128)(2,1)} %perturb_hbm.1, ...), custom_call_target="tpu_custom_call" | custom-call | bytes 8000000 | tf_op jit(solution)/shard_map/stage/pallas_call | solution.py:382
  3.2 0.0 collective-permute-done.other_ref
  3.2 0.1 border_product_0.1.refs_0_.pair_ref
  3.4 0.0 copy-start
  3.4 0.0 copy-start.1
  3.4 0.0 copy-start.2
  3.4 2.7 %collective-permute-start.1 = (f32[480,128]{1,0:T(8,128)S(1)}, f32[480,128]{1,0:T(8,128)S(1)}, u32[]{:S(2)}, u32[]{:S(2)}) collective-permute-start(f32[480,128]{1,0:T(8,128)S(1)} %border_product_0.1.refs_0_.pair_ref), channel_id=1, source_target_pairs={{0,2},{4,6},{8,10},{12,14},{2,0},{6,4},{10,8},{14,12},{1,3},{5,7},... | collective-permute-start | bytes 737288 | tf_op jit(solution)/shard_map/ppermute | solution.py:422
  6.1 0.1 border_product_1.1.next_ref
  6.3 0.7 %collective-permute-start.2 = (f32[480,128]{1,0:T(8,128)S(1)}, f32[480,128]{1,0:T(8,128)S(1)}, u32[]{:S(2)}, u32[]{:S(2)}) collective-permute-start(f32[480,128]{1,0:T(8,128)S(1)} %border_product_1.1.next_ref), channel_id=1, source_target_pairs={{2,4},{6,8},{10,12},{4,2},{8,6},{12,10},{3,5},{7,9},{11,13},{5,3},... | collective-permute-start | bytes 737288 | tf_op jit(solution)/shard_map/ppermute | solution.py:421
  7.0 0.0 copy-done
  7.0 0.0 copy-done.1
  7.0 0.0 copy-done.2
  7.0 6.9 %bulk.1 = (f32[10,24,2048]{2,1,0:T(8,128)S(1)}, f32[480,128]{1,0:T(8,128)S(1)}, f32[480,128]{1,0:T(8,128)S(1)}, f32[8,128]{1,0:T(8,128)S(1)}, f32[10,24,2048]{2,1,0:T(8,128)S(1)}, /*index=5*/f32[10,24,2048]{2,1,0:T(8,128)S(1)}) custom-call(s32[3]{0:T(128)S(1)} %bitcast.2, f32[7]{0:T(128)S(1)} %copy-done.1, f32[7]{0:T(128)S(1)} %copy-done.2, ...), custom_call_target="tpu_custom_call" | custom-call | flops 8999999488 | bytes 12000000 | tf_op jit(solution)/shard_map/bulk/pallas_call | solution.py:429
  13.9 0.0 collective-permute-done.2.from_next_ref
  13.9 3.2 %collective-permute-done.1.from_pair_ref = f32[480,128]{1,0:T(8,128)S(1)} collective-permute-done((f32[480,128]{1,0:T(8,128)S(1)}, f32[480,128]{1,0:T(8,128)S(1)}, u32[]{:S(2)}, u32[]{:S(2)}) %collective-permute-start.1) | collective-permute-done | bytes 245792 | tf_op jit(solution)/shard_map/ppermute | solution.py:422
  17.1 0.1 cross_term.1
  17.2 0.1 collective-permute-start.3
  17.3 1.1 %collective-permute-done.3 = f32[1,128]{1,0:T(1,128)S(1)} collective-permute-done((f32[1,128]{1,0:T(1,128)S(1)}, f32[1,128]{1,0:T(1,128)S(1)}, u32[]{:S(2)}, u32[]{:S(2)}) %collective-permute-start.3) | collective-permute-done | bytes 544 | tf_op jit(solution)/shard_map/ppermute | solution.py:468
  18.4 2.3 %collective-permute-start.4 = (f32[1,128]{1,0:T(1,128)S(1)}, f32[1,128]{1,0:T(1,128)S(1)}, u32[]{:S(2)}, u32[]{:S(2)}) collective-permute-start(f32[1,128]{1,0:T(1,128)S(1)} %add.9), channel_id=1, source_target_pairs={{0,3},{1,2},{2,1},{3,0},{4,7},{5,6},{6,5},{7,4},{8,11},{9,10},{10,... | collective-permute-start | bytes 1544 | tf_op jit(solution)/shard_map/ppermute | solution.py:475
  20.7 1.3 %collective-permute-done.4 = f32[1,128]{1,0:T(1,128)S(1)} collective-permute-done((f32[1,128]{1,0:T(1,128)S(1)}, f32[1,128]{1,0:T(1,128)S(1)}, u32[]{:S(2)}, u32[]{:S(2)}) %collective-permute-start.4) | collective-permute-done | bytes 544 | tf_op jit(solution)/shard_map/ppermute | solution.py:475
  22.0 1.7 %collective-permute-start.5 = (f32[1,128]{1,0:T(1,128)S(1)}, f32[1,128]{1,0:T(1,128)S(1)}, u32[]{:S(2)}, u32[]{:S(2)}) collective-permute-start(f32[1,128]{1,0:T(1,128)S(1)} %add.10), channel_id=1, source_target_pairs={{0,5},{1,4},{2,7},{3,6},{4,1},{5,0},{6,3},{7,2},{8,13},{9,12},{10,... | collective-permute-start | bytes 1544 | tf_op jit(solution)/shard_map/ppermute | solution.py:475
  23.7 1.3 %collective-permute-done.5 = f32[1,128]{1,0:T(1,128)S(1)} collective-permute-done((f32[1,128]{1,0:T(1,128)S(1)}, f32[1,128]{1,0:T(1,128)S(1)}, u32[]{:S(2)}, u32[]{:S(2)}) %collective-permute-start.5) | collective-permute-done | bytes 544 | tf_op jit(solution)/shard_map/ppermute | solution.py:475
  25.0 2.7 %collective-permute-start.6 = (f32[1,128]{1,0:T(1,128)S(1)}, f32[1,128]{1,0:T(1,128)S(1)}, u32[]{:S(2)}, u32[]{:S(2)}) collective-permute-start(f32[1,128]{1,0:T(1,128)S(1)} %add.11.near_ref), channel_id=1, source_target_pairs={{0,9},{1,8},{2,11},{3,10},{4,13},{5,12},{6,15},{7,14},{8,1},{9,0},... | collective-permute-start | bytes 1544 | tf_op jit(solution)/shard_map/ppermute | solution.py:476
  27.7 0.7 %border_correction.1.gradient_ref = f32[10,24,2048]{2,1,0:T(8,128)S(1)} custom-call(f32[17,8,128]{2,1,0:T(8,128)S(1)} %get-tuple-element.17.vector_ref, bf16[256,256]{1,0:T(8,128)(2,1)S(1)} %get-tuple-element.14.matrix, f32[480,128]{1,0:T(8,128)S(1)} %collective-permute-done.1.from_pair_ref, ...), custom_call_target="tpu_custom_call", output_to_operand_aliasing={{}: (4, {})} | custom-call | flops 2000000000 | bytes 2000000 | tf_op jit(solution)/shard_map/border_correction/pallas_call | solution.py:457
  28.4 0.5 %collective-permute-done.6.far_ref = f32[1,128]{1,0:T(1,128)S(1)} collective-permute-done((f32[1,128]{1,0:T(1,128)S(1)}, f32[1,128]{1,0:T(1,128)S(1)}, u32[]{:S(2)}, u32[]{:S(2)}) %collective-permute-start.6) | collective-permute-done | bytes 544 | tf_op jit(solution)/shard_map/ppermute | solution.py:476
  29.0 2.2 %update.1 = (f32[10,24,2048]{2,1,0:T(8,128)}, f32[10,24,2048]{2,1,0:T(8,128)}) custom-call(f32[1,128]{1,0:T(1,128)S(1)} %add.11.near_ref, f32[1,128]{1,0:T(1,128)S(1)} %collective-permute-done.6.far_ref, f32[10,24,2048]{2,1,0:T(8,128)S(1)} %get-tuple-element.23.control_ref, f32[10,24,2048]{2,1,0:T(8,128)S(1)} %get-tuple-element.24.velocity_ref, ...), custom_call_target="tpu_custom_call" | custom-call | flops 3000000 | bytes 12000000 | tf_op jit(solution)/shard_map/update/pallas_call | solution.py:479
  (3 shorter events, 0.0 us)
Async XLA Ops:
  0.6 2.6 %collective-permute-start = (f32[1,3,24,2048]{3,2,1,0:T(8,128)}, f32[1,3,24,2048]{3,2,1,0:T(8,128)S(1)}, u32[]{:S(2)}, u32[]{:S(2)}) collective-permute-start(f32[1,3,24,2048]{3,2,1,0:T(8,128)} %mine_hbm.3), channel_id=1, source_target_pairs={{0,1},{1,0},{2,3},{3,2},{4,5},{5,4},{6,7},{7,6},{8,9},{9,8},{10,11... | collective-permute-start | bytes 1769480 | tf_op jit(solution)/shard_map/ppermute | solution.py:379
  3.4 3.6 %copy-start = (s32[3,1]{0,1:T(1,128)S(1)}, s32[3,1]{0,1:T(1,128)}, u32[]{:S(2)}) copy-start(s32[3,1]{0,1:T(1,128)} %param.12) | copy-start | bytes 40
  3.4 3.6 %copy-start.1 = (f32[7]{0:T(128)S(1)}, f32[7]{0:T(128)}, u32[]{:S(2)}) copy-start(f32[7]{0:T(128)} %taps_x_ref.1) | copy-start | bytes 88
  3.4 3.6 %copy-start.2 = (f32[7]{0:T(128)S(1)}, f32[7]{0:T(128)}, u32[]{:S(2)}) copy-start(f32[7]{0:T(128)} %taps_y_ref.1) | copy-start | bytes 88
  3.4 13.7 %collective-permute-start.1 = (f32[480,128]{1,0:T(8,128)S(1)}, f32[480,128]{1,0:T(8,128)S(1)}, u32[]{:S(2)}, u32[]{:S(2)}) collective-permute-start(f32[480,128]{1,0:T(8,128)S(1)} %border_product_0.1.refs_0_.pair_ref), channel_id=1, source_target_pairs={{0,2},{4,6},{8,10},{12,14},{2,0},{6,4},{10,8},{14,12},{1,3},{5,7},... | collective-permute-start | bytes 737288 | tf_op jit(solution)/shard_map/ppermute | solution.py:422
  6.3 7.6 %collective-permute-start.2 = (f32[480,128]{1,0:T(8,128)S(1)}, f32[480,128]{1,0:T(8,128)S(1)}, u32[]{:S(2)}, u32[]{:S(2)}) collective-permute-start(f32[480,128]{1,0:T(8,128)S(1)} %border_product_1.1.next_ref), channel_id=1, source_target_pairs={{2,4},{6,8},{10,12},{4,2},{8,6},{12,10},{3,5},{7,9},{11,13},{5,3},... | collective-permute-start | bytes 737288 | tf_op jit(solution)/shard_map/ppermute | solution.py:421
  17.2 1.2 %collective-permute-start.3 = (f32[1,128]{1,0:T(1,128)S(1)}, f32[1,128]{1,0:T(1,128)S(1)}, u32[]{:S(2)}, u32[]{:S(2)}) collective-permute-start(f32[1,128]{1,0:T(1,128)S(1)} %cross_term.1), channel_id=1, source_target_pairs={{0,1},{1,0},{2,3},{3,2},{4,5},{5,4},{6,7},{7,6},{8,9},{9,8},{10,11... | collective-permute-start | bytes 1544 | tf_op jit(solution)/shard_map/ppermute | solution.py:468
  18.4 3.6 %collective-permute-start.4 = (f32[1,128]{1,0:T(1,128)S(1)}, f32[1,128]{1,0:T(1,128)S(1)}, u32[]{:S(2)}, u32[]{:S(2)}) collective-permute-start(f32[1,128]{1,0:T(1,128)S(1)} %add.9), channel_id=1, source_target_pairs={{0,3},{1,2},{2,1},{3,0},{4,7},{5,6},{6,5},{7,4},{8,11},{9,10},{10,... | collective-permute-start | bytes 1544 | tf_op jit(solution)/shard_map/ppermute | solution.py:475
  22.0 3.0 %collective-permute-start.5 = (f32[1,128]{1,0:T(1,128)S(1)}, f32[1,128]{1,0:T(1,128)S(1)}, u32[]{:S(2)}, u32[]{:S(2)}) collective-permute-start(f32[1,128]{1,0:T(1,128)S(1)} %add.10), channel_id=1, source_target_pairs={{0,5},{1,4},{2,7},{3,6},{4,1},{5,0},{6,3},{7,2},{8,13},{9,12},{10,... | collective-permute-start | bytes 1544 | tf_op jit(solution)/shard_map/ppermute | solution.py:475
  25.0 4.0 %collective-permute-start.6 = (f32[1,128]{1,0:T(1,128)S(1)}, f32[1,128]{1,0:T(1,128)S(1)}, u32[]{:S(2)}, u32[]{:S(2)}) collective-permute-start(f32[1,128]{1,0:T(1,128)S(1)} %add.11.near_ref), channel_id=1, source_target_pairs={{0,9},{1,8},{2,11},{3,10},{4,13},{5,12},{6,15},{7,14},{8,1},{9,0},... | collective-permute-start | bytes 1544 | tf_op jit(solution)/shard_map/ppermute | solution.py:476
